TPU v7x, 32 devices: a whole 2x2x4 slice. The times are simulated.
32 devices in a mesh: sp: 4 (over x, core), ep: 8 (over z, y).
Axes of the slice: x: 2, y: 2, z: 4, core: 2. Of those that a mesh axis runs over, the one named last changes fastest.
Arguments:
- latent: bfloat16 [8, 512, 4096], P('ep', 'sp'), may hold values from -36 to 36
- attention_in: bfloat16 [8, 512, 3, 4096], P('ep', 'sp'), may hold values from -6 to 6
- out_weight: bfloat16 [4096, 4096], P('sp'), may hold values from -0.09375 to 0.09375
- modulation: float32 [4, 4096], replicated, may hold values from -4 to 4
- route_experts: int32 [8, 512, 2], P('ep', 'sp'), may hold values from 0 to 15, as said below
- route_slots: int32 [8, 512, 2], P('ep', 'sp'), may hold values from 0 to 23, as said below
- route_gates: float32 [8, 512, 2], P('ep', 'sp'), may hold values from 0.1 to 1
- gate_weight: bfloat16 [8, 4096, 4096], P('ep', None, 'sp'), may hold values from -0.09375 to 0.09375
- up_weight: bfloat16 [8, 4096, 4096], P('ep', None, 'sp'), may hold values from -0.09375 to 0.09375
- down_weight: bfloat16 [8, 4096, 4096], P('ep', 'sp'), may hold values from -0.125 to 0.125
Outputs:
- block_out: bfloat16 [8, 512, 4096], P('ep', 'sp')
Inputs may be any that keep to these rules, and one draw needn't show every extreme that they name: `route_experts`: each token names two different experts. Among the 128 tokens of one device block no expert is named more than 24 times; in every device block some expert is named exactly 24 times, and one expert is named exactly 24 times in every device block. `route_slots`: the routes of one device block to one expert hold distinct slots.
All inputs are finite; a program needn't handle non-finite values.
Results may differ from a plain program's by a relative error of at most 0.013.
Values may be sent and summed in bfloat16 or wider, within the bound.
No kernel may reach another device: no remote copies, remote signals or barrier semaphores. Data moves between devices by JAX's collectives and lax.ppermute only.
A program may use at most 192 MiB of HBM per device.

v0:
```python
import math

import jax
import jax.numpy as jnp
from jax import lax
from jax.sharding import PartitionSpec as P

HD = 128


def attend(block):
    queries = block[:, 0, 0]
    key_rows = block[:, 1, 0]
    value_rows = block[:, 2, 0]
    score_scale = 1.0 / math.sqrt(HD)
    scores = (
        jnp.einsum("qhd,khd->hqk", queries, key_rows, preferred_element_type=jnp.float32)
        * score_scale
    )
    top_rows = jnp.max(scores, axis=-1, keepdims=True)
    lifted = jnp.exp(scores - top_rows)
    weights = (lifted / jnp.sum(lifted, axis=-1, keepdims=True)).astype(jnp.bfloat16)
    mixed = jnp.einsum("hqk,khd->qhd", weights, value_rows, preferred_element_type=jnp.float32)
    return mixed.astype(jnp.bfloat16)


def feed_forward(rows, gate_shard, up_shard, down_shard):
    gate_part = jnp.dot(rows, gate_shard, preferred_element_type=jnp.float32)
    up_part = jnp.dot(rows, up_shard, preferred_element_type=jnp.float32)
    activation = (jax.nn.silu(gate_part) * up_part).astype(jnp.bfloat16)
    return jnp.dot(activation, down_shard, preferred_element_type=jnp.float32).astype(jnp.bfloat16)


def local(
    latent,
    attention_in,
    out_weight,
    modulation,
    route_experts,
    route_slots,
    route_gates,
    gate_weight,
    up_weight,
    down_weight,
):
    n_sp = lax.axis_size("sp")
    n_ep = lax.axis_size("ep")
    tokens = latent.shape[1]
    width = latent.shape[2]
    group_heads = out_weight.shape[0] // HD
    window_len = tokens * n_sp
    packed = attention_in[0].reshape(tokens, 3, n_sp, group_heads, HD)
    attended = attend(lax.all_to_all(packed, "sp", split_axis=2, concat_axis=0, tiled=True))
    flat_heads = attended.reshape(window_len, group_heads * HD)
    projected = lax.psum_scatter(
        jnp.dot(flat_heads, out_weight, preferred_element_type=jnp.float32).astype(jnp.bfloat16),
        "sp",
        scatter_dimension=0,
        tiled=True,
    ).astype(jnp.float32)
    residual = latent[0].astype(jnp.float32) + modulation[0] * projected
    row_mean = jnp.mean(residual, axis=-1, keepdims=True)
    centered = residual - row_mean
    variance = jnp.mean(centered * centered, axis=-1, keepdims=True)
    normed = centered * lax.rsqrt(variance + 1e-06)
    moe_in = (normed * (1.0 + modulation[2]) + modulation[1]).astype(jnp.bfloat16)
    experts_count = 2 * n_ep
    capacity = max(2, 3 * tokens // experts_count)
    shard_count = n_sp // 2
    cell_index = route_experts[0] * capacity + route_slots[0]
    slot_grid = jnp.arange(experts_count * capacity, dtype=jnp.int32)
    one_hot = (
        (cell_index[:, 0:1] == slot_grid[None, :]) | (cell_index[:, 1:2] == slot_grid[None, :])
    ).astype(jnp.bfloat16)
    dispatched = jnp.einsum(
        "tc,td->cd", one_hot, moe_in, preferred_element_type=jnp.float32
    ).astype(jnp.bfloat16)
    by_expert = dispatched.reshape(n_ep, 2, capacity, width)
    spread = jnp.broadcast_to(
        jnp.transpose(by_expert, (1, 0, 2, 3))[:, None], (2, shard_count, n_ep, capacity, width)
    )
    spread = spread.reshape(n_sp * n_ep, capacity, width)
    rows = lax.all_to_all(spread, ("sp", "ep"), split_axis=0, concat_axis=0, tiled=True)
    partial_value = feed_forward(
        rows.reshape(-1, width), gate_weight[0], up_weight[0], down_weight[0]
    ).reshape(rows.shape)
    returned = lax.all_to_all(partial_value, ("sp", "ep"), split_axis=0, concat_axis=0, tiled=True)
    summed = jnp.sum(
        returned.reshape(2, shard_count, n_ep, capacity, width).astype(jnp.float32), axis=1
    )
    per_expert = jnp.transpose(summed, (1, 0, 2, 3)).reshape(experts_count * capacity, width)
    picked = jnp.take(per_expert, cell_index.reshape(-1), axis=0).reshape(tokens, 2, width)
    gate_values = route_gates[0]
    combined = gate_values[:, 0:1] * picked[:, 0] + gate_values[:, 1:2] * picked[:, 1]
    return (residual + modulation[3] * combined).astype(jnp.bfloat16)[None]


def solution(mesh):
    return jax.shard_map(
        local,
        mesh=mesh,
        in_specs=(
            P("ep", "sp", None),
            P("ep", "sp", None, None),
            P("sp", None),
            P(),
            P("ep", "sp", None),
            P("ep", "sp", None),
            P("ep", "sp", None),
            P("ep", None, "sp"),
            P("ep", None, "sp"),
            P("ep", "sp", None),
        ),
        out_specs=P("ep", "sp", None),
        check_vma=False,
    )
```

profile of v0, /device:TPU:0, one launch (start us, length us, event | category | flops | bytes accessed | tf_op | source)
XLA Modules:
  0.0 496.4 jit_solution(8078189894525809518)
XLA Ops:
  6.5 4.7 copy.28
  11.2 4.7 copy.29
  15.9 41.2 %all_to_all.28 = bf16[128,3,4,8,128]{4,0,3,1,2:T(8,128)(2,1)S(1)} all-to-all(bf16[128,3,4,8,128]{4,0,3,1,2:T(8,128)(2,1)} %copy.29), channel_id=1, replica_groups=mesh['sp'=4,'ep'=8] {'sp'}, dimensions={2} | all-to-all | bytes 6291456 | tf_op jit(solution)/shard_map/all_to_all | solution.py:53
  57.1 0.4 copy.30
  57.5 1.8 copy-done.2
  59.3 1.3 fusion.27
  60.5 3.2 copy-done.3
  63.7 2.2 fusion.49
  65.9 8.9 %fusion.25 = bf16[8,512,128]{1,2,0:T(8,128)(2,1)S(1)} fusion(f32[8,512]{1,0:T(8,128)S(1)} %fusion.49, bf16[512,3,1,8,128]{4,0,3,2,1:T(8,128)(2,1)} %bitcast.104, f32[8,512,512]{1,2,0:T(8,128)} %copy-done.3), kind=kOutput, calls=%fused_computation.31 | convolution fusion | flops 547885568 | bytes 18890752 | tf_op jit(solution)/shard_map/hqk,khd->qhd/dot_general | solution.py:23
  74.9 9.5 %convolution_convert_fusion = bf16[512,4096]{1,0:T(8,128)(2,1)} fusion(bf16[512,1024]{0,1:T(8,128)(2,1)S(1)} %bitcast.120, bf16[1024,4096]{1,0:T(8,128)(2,1)} %param.12), kind=kOutput, calls=%fused_computation.14 | convolution fusion | flops 4297064448 | bytes 13631488 | tf_op jit(solution)/shard_map/dot_general | solution.py:56
  84.4 0.6 copy-done.6
  85.1 0.2 copy-done.5
  85.3 44.9 %reduce-scatter.2.cloned.1.call-done = bf16[128,4096]{1,0:T(8,128)(2,1)} async-done(((bf16[512,4096]{1,0:T(8,128)(2,1)}), bf16[128,4096]{1,0:T(8,128)(2,1)}) %reduce-scatter.2.cloned.1.call-update) | async-done | bytes 1048592 | tf_op jit(solution)/shard_map/reduce_scatter | solution.py:55
  130.2 1.7 fusion.26
  132.0 1.8 multiply_reduce_fusion.1
  133.8 1.2 convolution_convert_fusion.1
  135.0 0.2 copy.33
  135.2 0.8 broadcast_in_dim.12
  136.0 144.4 %all_to_all.29 = bf16[32,24,4096]{2,1,0:T(8,128)(2,1)S(1)} all-to-all(bf16[32,24,4096]{2,1,0:T(8,128)(2,1)S(1)} %bitcast.98), channel_id=1, replica_groups=mesh['sp'=4,'ep'=8] {'sp','ep'}, dimensions={0} | all-to-all | bytes 12582912 | tf_op jit(solution)/shard_map/all_to_all | solution.py:83
  280.3 2.7 copy-done.4
  283.0 8.4 %fusion.3 = f32[768,1024]{1,0:T(8,128)} fusion(bf16[768,4096]{1,0:T(8,128)(2,1)S(1)} %bitcast.106, bf16[1,4096,1024]{2,1,0:T(8,128)(2,1)S(1)} %bitcast.119), kind=kOutput, calls=%fused_computation.5 | convolution fusion | flops 6442450944 | bytes 17825792 | tf_op jit(solution)/shard_map/dot_general | solution.py:29
  291.4 22.4 %fusion.8 = bf16[768,4096]{1,0:T(8,128)(2,1)} fusion(bf16[1,1024,4096]{2,1,0:T(8,128)(2,1)} %param.19, f32[768,1024]{1,0:T(8,128)} %fusion.3, bf16[768,4096]{1,0:T(8,128)(2,1)} %bitcast.107, bf16[1,4096,1024]{2,1,0:T(8,128)(2,1)} %param.17), kind=kOutput, calls=%fused_computation.13 | convolution fusion | flops 12892766208 | bytes 32505856 | tf_op jit(solution)/shard_map/dot_general | solution.py:31
  313.9 4.0 all-to-all-start.2
  317.9 0.1 copy.35
  318.0 0.1 add.98
  318.2 142.3 %all-to-all-done.2 = bf16[32,24,4096]{2,1,0:T(8,128)(2,1)} async-done(((bf16[32,24,4096]{2,1,0:T(8,128)(2,1)}), bf16[32,24,4096]{2,1,0:T(8,128)(2,1)}, u32[]{:S(2)}, u32[]{:S(2)}) %all-to-all-start.2) | async-done | bytes 6291488 | tf_op jit(solution)/shard_map/all_to_all | solution.py:87
  460.4 5.1 %convert_reduce_fusion = f32[2,8,24,4096]{3,2,1,0:T(8,128)S(1)} fusion(bf16[2,2,8,24,4096]{4,3,2,1,0:T(8,128)(2,1)} %bitcast.39), kind=kLoop, calls=%fused_computation.2 | loop fusion | flops 4718592 | bytes 12582912 | tf_op jit(solution)/shard_map/reduce_sum | solution.py:88
  465.6 3.1 copy.34
  468.7 8.5 %gather_fusion = f32[256,4096]{1,0:T(8,128)} fusion(f32[384,4096]{1,0:T(8,128)} %bitcast.97, s32[1024]{0:T(1024)S(1)} %pad_clamp_fusion), kind=kCustom, calls=%fused_computation | custom fusion | bytes 8389632 | tf_op jit(solution)/shard_map/jit(_take)/gather | solution.py:92
  477.1 5.8 %gather.7 = f32[128,2,4096]{2,1,0:T(2,128)} reshape(f32[256,4096]{1,0:T(8,128)} %gather_fusion) | data formatting | bytes 8388608 | tf_op jit(solution)/shard_map/jit(_take)/gather | solution.py:92
  483.0 4.9 copy_select_fusion
  487.9 1.7 fusion.34
  (28 shorter events, 0.2 us)
Async XLA Ops:
  6.5 123.7 %reduce-scatter.2.cloned.1.call-start = ((), (), s32[]{:S(2)}) async-start(), calls=%async_computation.4 | async-start | bytes 5242880 | tf_op jit(solution)/shard_map/reduce_scatter | solution.py:55
  57.5 1.8 copy-start.2
  60.5 3.2 copy-start.3
  84.4 0.7 copy-start.6
  84.4 0.7 copy-start.7
  84.4 0.9 copy-start.5
  84.4 45.8 %copy-start = (bf16[1,128,4096]{2,1,0:T(8,128)(2,1)S(1)}, bf16[1,128,4096]{2,1,0:T(8,128)(2,1)}, u32[]{:S(2)}) copy-start(bf16[1,128,4096]{2,1,0:T(8,128)(2,1)} %param.10) | copy-start | bytes 3145732
  130.2 3.5 copy-start.1
  135.2 147.8 %slice-start = ((s8[8388608]{0:T(1024)(128)(4,1)}), s8[4194304]{0:T(1024)(128)(4,1)S(1)}, s32[]{:S(2)}) async-start(s8[8388608]{0:T(1024)(128)(4,1)} %bitcast.118), calls=%async_computation.5 | async-start | bytes 8388608
  136.0 147.0 %slice-start.1 = ((s8[8388608]{0:T(1024)(128)(4,1)}), s8[4194304]{0:T(1024)(128)(4,1)S(1)}, s32[]{:S(2)}) async-start(s8[8388608]{0:T(1024)(128)(4,1)} %bitcast.118), calls=%async_computation.6 | async-start | bytes 8388608
  280.3 2.7 copy-start.4
  313.9 4.3 copy-start.8
  313.9 146.6 %all-to-all-start.2 = ((bf16[32,24,4096]{2,1,0:T(8,128)(2,1)}), bf16[32,24,4096]{2,1,0:T(8,128)(2,1)}, u32[]{:S(2)}, u32[]{:S(2)}) async-start(bf16[32,24,4096]{2,1,0:T(8,128)(2,1)} %bitcast.105), calls=%async_computation.3 | async-start | bytes 12582912 | tf_op jit(solution)/shard_map/all_to_all | solution.py:87
Sparse Core Ops, SparseCore 0:
  84.5 45.6 reduce-scatter.1
where the time goes:
time: 497 us; the launch traced here: 496 us
  waiting for transfers between devices  187 us (38%)
  blocking collectives  186 us (37%)
  matrix products  51.7 us (10%)
  local copies, waits for them, and re-layouts  36.8 us (7%)
  other arithmetic  17.5 us (4%)
  between operations  13.5 us (3%)
    all_to_all x1, blocking collectives, local(): lax.all_to_all(spread, ('sp', 'ep'), split_axis=0, concat_axis=0, tiled=T...  144 us
    all_to_all x1, waiting for transfers between devices, local(): lax.all_to_all(partial_value, ('sp', 'ep'), split_axis=0, concat_axis=0,...  142 us
    reduce_scatter x1, waiting for transfers between devices, local(): lax.psum_scatter(jnp.dot(flat_heads, out_weight, preferred_element_type=j...  44.9 us
    all_to_all x1, blocking collectives, local(): lax.all_to_all(packed, 'sp', split_axis=2, concat_axis=0, tiled=True)  41.2 us
    dot_general x1, matrix products, feed_forward(): jnp.dot(activation, down_shard, preferred_element_type=jnp.float32)  22.4 us
    gather x2, local copies, waits for them, and re-layouts, local(): jnp.take(per_expert, cell_index.reshape(-1), axis=0)  14.3 us
    unnamed x23, local copies, waits for them, and re-layouts  13.2 us
  transfers between devices with their start and end apart: 2, of which 2 were waited for; matrix products, arithmetic and copies ran while one was open for 0% of the time, Pallas kernels for 0%

commit v1 on v0

v1 whole, which is shorter than its diff:
```python
import functools
import math

import jax
import jax.numpy as jnp
from jax import lax
from jax.experimental import pallas as pl
from jax.experimental.pallas import tpu as pltpu
from jax.sharding import Mesh, PartitionSpec as P

HD = 128
VMEM = pl.BlockSpec(memory_space=pltpu.VMEM)
PARAMS = pltpu.CompilerParams(vmem_limit_bytes=48 * 1024 * 1024)


def dot32(a, b):
    return jnp.dot(a, b, preferred_element_type=jnp.float32)


def cost(flops, moved):
    return pl.CostEstimate(flops=int(flops), bytes_accessed=int(moved), transcendentals=0)


def attention_kernel(n_blocks, *refs):
    blocks = refs[:n_blocks]
    keep_ref, give_ref = refs[n_blocks:]
    factor = math.log2(math.e) / math.sqrt(HD)
    for head in range(keep_ref.shape[-1] // HD):
        cols = slice(head * HD, (head + 1) * HD)
        key_rows = jnp.concatenate([block[1, :, cols] for block in blocks], axis=0)
        value_rows = jnp.concatenate([block[2, :, cols] for block in blocks], axis=0)
        for i, block in enumerate(blocks):
            scores = lax.dot_general(
                block[0, :, cols],
                key_rows,
                (((1,), (1,)), ((), ())),
                preferred_element_type=jnp.float32,
            )
            lifted = jnp.exp2((scores - jnp.max(scores, axis=-1, keepdims=True)) * factor)
            total = jnp.sum(lifted, axis=-1, keepdims=True)
            mixed = dot32(lifted.astype(jnp.bfloat16), value_rows) / total
            out_ref = give_ref if i % 2 else keep_ref
            out_ref[i // 2, :, cols] = mixed.astype(jnp.bfloat16)


def attend(blocks):
    _, tokens, width = blocks[0].shape
    count = len(blocks)
    out = jax.ShapeDtypeStruct((count // 2, tokens, width), jnp.bfloat16)
    length = count * tokens
    return pl.pallas_call(
        functools.partial(attention_kernel, count),
        out_shape=(out, out),
        in_specs=[VMEM] * count,
        out_specs=(VMEM, VMEM),
        compiler_params=PARAMS,
        cost_estimate=cost(16 * length * length * width, 8 * length * width),
    )(*blocks)


def project_first_kernel(mine_ref, theirs_ref, mine_w, theirs_w, out_ref):
    n_x, tokens, width = mine_ref.shape
    mine = mine_ref[...].reshape(n_x * tokens, width)
    theirs = theirs_ref[...].reshape(n_x * tokens, width)
    out_ref[...] = dot32(mine, mine_w[...]) + dot32(theirs, theirs_w[...])


def project_first(mine, theirs, mine_w, theirs_w):
    n_x, tokens, part = mine.shape
    width = mine_w.shape[1]
    tile = min(512, width)
    rows = n_x * tokens
    whole = pl.BlockSpec((n_x, tokens, part), lambda n: (0, 0, 0))
    weight = pl.BlockSpec((part, tile), lambda n: (0, n))
    return pl.pallas_call(
        project_first_kernel,
        grid=(width // tile,),
        out_shape=jax.ShapeDtypeStruct((rows, width), jnp.float32),
        in_specs=[whole, whole, weight, weight],
        out_specs=pl.BlockSpec((rows, tile), lambda n: (0, n)),
        compiler_params=PARAMS,
        cost_estimate=cost(4 * rows * part * width, 4 * part * width + 4 * rows * width),
    )(mine, theirs, mine_w, theirs_w)


def project_last_kernel(mine_ref, theirs_ref, mine_w, theirs_w, acc_ref, own_ref, *send_refs):
    n_x, tokens, width = mine_ref.shape
    mine = mine_ref[...].reshape(n_x * tokens, width)
    theirs = theirs_ref[...].reshape(n_x * tokens, width)
    total = acc_ref[...] + dot32(mine, mine_w[...]) + dot32(theirs, theirs_w[...])
    own_ref[...] = total[:tokens]
    for i, send_ref in enumerate(send_refs):
        send_ref[...] = total[(i + 1) * tokens : (i + 2) * tokens].astype(jnp.bfloat16)


def project_last(mine, theirs, mine_w, theirs_w, acc, start, size):
    n_x, tokens, part = mine.shape
    tile = min(512, size)
    first = start // tile
    depth = mine_w.shape[0] // part - 1
    rows = n_x * tokens
    whole = pl.BlockSpec((n_x, tokens, part), lambda n: (0, 0, 0))
    weight = pl.BlockSpec((part, tile), lambda n: (depth, first + n))
    out = pl.BlockSpec((tokens, tile), lambda n: (0, n))
    return pl.pallas_call(
        project_last_kernel,
        grid=(size // tile,),
        out_shape=[jax.ShapeDtypeStruct((tokens, size), jnp.float32)]
        + [jax.ShapeDtypeStruct((tokens, size), jnp.bfloat16)] * (n_x - 1),
        in_specs=[
            whole,
            whole,
            weight,
            weight,
            pl.BlockSpec((rows, tile), lambda n: (0, first + n)),
        ],
        out_specs=[out] * n_x,
        compiler_params=PARAMS,
        cost_estimate=cost(4 * rows * part * size, 4 * part * size + 8 * rows * size),
    )(mine, theirs, mine_w, theirs_w, acc)


def norm_kernel(n_parts, n_recv, cuts, latent_ref, mod_ref, cells_ref, *refs):
    own_refs = refs[:n_parts]
    recv_refs = refs[n_parts : n_parts * (1 + n_recv)]
    residual_ref, *sent_refs = refs[n_parts * (1 + n_recv) :]
    tokens, width = latent_ref.shape
    size = width // n_parts
    sums = 0.0
    for i in range(n_parts):
        cut = slice(i * size, (i + 1) * size)
        projected = own_refs[i][...]
        for j in range(n_recv):
            projected = projected + recv_refs[i * n_recv + j][...].astype(jnp.float32)
        part = latent_ref[:, cut].astype(jnp.float32) + mod_ref[0:1, cut] * projected
        residual_ref[:, cut] = part
        sums = sums + jnp.sum(part, axis=-1, keepdims=True)
    row_mean = sums / width
    squares = 0.0
    for i in range(n_parts):
        cut = slice(i * size, (i + 1) * size)
        centered = residual_ref[:, cut] - row_mean
        squares = squares + jnp.sum(centered * centered, axis=-1, keepdims=True)
    inverse = lax.rsqrt(squares / width + 1e-06)
    cells = lax.broadcasted_iota(jnp.int32, (sent_refs[0].shape[0], tokens), 0)
    one_hot = ((cells == cells_ref[0:1, :]) | (cells == cells_ref[1:2, :])).astype(jnp.bfloat16)
    for (start, size), sent_ref in zip(cuts, sent_refs):
        cut = slice(start, start + size)
        normed = (residual_ref[:, cut] - row_mean) * inverse
        moe_in = (normed * (1.0 + mod_ref[2:3, cut]) + mod_ref[1:2, cut]).astype(jnp.bfloat16)
        sent_ref[...] = dot32(one_hot, moe_in).astype(jnp.bfloat16)


def norm_and_pack(latent, modulation, cells, n_cells, own, received, cuts):
    tokens, width = latent.shape
    flat = [piece for pieces in received for piece in pieces]
    count = 3 + len(own) + len(flat)
    return pl.pallas_call(
        functools.partial(norm_kernel, len(own), len(received[0]), cuts),
        out_shape=[jax.ShapeDtypeStruct((tokens, width), jnp.float32)]
        + [jax.ShapeDtypeStruct((n_cells, size), jnp.bfloat16) for _, size in cuts],
        in_specs=[VMEM] * count,
        out_specs=[VMEM] * (1 + len(cuts)),
        compiler_params=PARAMS,
        cost_estimate=cost(2 * n_cells * tokens * width, 20 * tokens * width),
    )(latent, modulation, cells, *own, *flat)


def ffn_in_kernel(first, last, rows_ref, *refs):
    weights, refs = refs[:4], refs[4:]
    sums = [dot32(rows_ref[...], weight[...]) for weight in weights]
    if not first:
        olds, refs = refs[:4], refs[4:]
        sums = [total + old[...] for total, old in zip(sums, olds)]
    if last:
        for gate, up, out_ref in zip(sums[:2], sums[2:], refs):
            out_ref[...] = (gate / (1.0 + jnp.exp(-gate)) * up).astype(jnp.bfloat16)
    else:
        for total, out_ref in zip(sums, refs):
            out_ref[...] = total


def ffn_in(rows, weights, olds, start, last):
    count, size = rows.shape
    units = weights[0].shape[1]
    tile = min(256, units)
    block = start // size
    weight = pl.BlockSpec((size, tile), lambda n: (block, n))
    part = pl.BlockSpec((count, tile), lambda n: (0, n))
    outs = 2 if last else 4
    kind = jnp.bfloat16 if last else jnp.float32
    return pl.pallas_call(
        functools.partial(ffn_in_kernel, not olds, last),
        grid=(units // tile,),
        out_shape=[jax.ShapeDtypeStruct((count, units), kind)] * outs,
        in_specs=[pl.BlockSpec((count, size), lambda n: (0, 0))] + [weight] * 4 + [part] * len(olds),
        out_specs=[part] * outs,
        compiler_params=PARAMS,
        cost_estimate=cost(8 * count * size * units, 8 * size * units + 16 * count * units),
    )(rows, *weights, *olds)


def ffn_out_kernel(mine_ref, theirs_ref, mine_w, theirs_w, out_ref):
    total = dot32(mine_ref[...], mine_w[...]) + dot32(theirs_ref[...], theirs_w[...])
    out_ref[...] = total.astype(jnp.bfloat16)


def ffn_out(acts, weights, start, size):
    count, units = acts[0].shape
    tile = min(512, size)
    first = start // tile
    act = pl.BlockSpec((count, units), lambda n: (0, 0))
    weight = pl.BlockSpec((units, tile), lambda n: (0, first + n))
    return pl.pallas_call(
        ffn_out_kernel,
        grid=(size // tile,),
        out_shape=jax.ShapeDtypeStruct((count, size), jnp.bfloat16),
        in_specs=[act, act, weight, weight],
        out_specs=pl.BlockSpec((count, tile), lambda n: (0, n)),
        compiler_params=PARAMS,
        cost_estimate=cost(4 * count * size * units, 4 * size * units + 2 * count * size),
    )(*acts, *weights)


def combine_kernel(residual_ref, mod_ref, cells_ref, gates_ref, back_ref, *refs):
    out_ref = refs[-1]
    tokens = residual_ref.shape[0]
    copies = back_ref.shape[1]
    n_cells = 2 * back_ref.shape[2]
    cells = lax.broadcasted_iota(jnp.int32, (tokens, n_cells), 1)
    combined = 0.0
    for route in range(2):
        one_hot = (cells == cells_ref[:, route : route + 1]).astype(jnp.bfloat16)
        picked = 0.0
        for i in range(copies):
            part = back_ref[:, i].reshape(n_cells, back_ref.shape[3])
            picked = picked + dot32(one_hot, part)
        combined = combined + gates_ref[:, route : route + 1] * picked
    out_ref[...] = (residual_ref[...] + mod_ref[3:4, :] * combined).astype(jnp.bfloat16)


def combine(residual, modulation, cells, gates, back, start, previous):
    tokens, width = residual.shape
    _, copies, half, size = back.shape
    tile = min(512, size)
    first = start // tile
    wide = pl.BlockSpec((tokens, tile), lambda n: (0, first + n))
    small = pl.BlockSpec((tokens, 2), lambda n: (0, 0))
    more = [] if previous is None else [previous]
    return pl.pallas_call(
        combine_kernel,
        grid=(size // tile,),
        out_shape=jax.ShapeDtypeStruct((tokens, width), jnp.bfloat16),
        in_specs=[
            wide,
            pl.BlockSpec((4, tile), lambda n: (0, first + n)),
            small,
            small,
            pl.BlockSpec((2, copies, half, tile), lambda n: (0, 0, 0, n)),
        ]
        + [pl.BlockSpec(memory_space=pl.ANY)] * len(more),
        out_specs=wide,
        input_output_aliases={5: 0} if more else {},
        compiler_params=PARAMS,
        cost_estimate=cost(8 * tokens * half * copies * size, 4 * half * copies * size + 6 * tokens * size),
    )(residual, modulation, cells, gates, back, *more)


def local(
    latent,
    attention_in,
    out_weight,
    modulation,
    route_experts,
    route_slots,
    route_gates,
    gate_weight,
    up_weight,
    down_weight,
):
    n_x = lax.axis_size("x")
    n_ep = lax.axis_size("ep")
    tokens = latent.shape[1]
    width = latent.shape[2]
    group_width = out_weight.shape[0]
    my_x = lax.axis_index("x")
    my_core = lax.axis_index("core")
    swap = [(0, 1), (1, 0)]
    sp_axes = ("x", "core")
    chip_axes = ("x", "ep")

    def other_core(value):
        return lax.ppermute(value, "core", swap)

    def shift(dx, dc):
        return [
            (2 * x + c, 2 * ((x + dx) % n_x) + (c ^ dc)) for x in range(n_x) for c in range(2)
        ]

    packed = jnp.transpose(attention_in[0], (1, 0, 2))
    last_part = group_width // 4
    parts = ((0, group_width - last_part), (group_width - last_part, last_part))
    pieces = []
    for start, size in parts:
        for dx in range(n_x):
            for dc in range(2):
                group = 2 * ((my_x + dx) % n_x) + (my_core ^ dc)
                pieces.append(
                    lax.dynamic_slice_in_dim(packed, group * group_width + start, size, axis=2)
                )
    blocks = []
    for i, piece in enumerate(pieces):
        dx, dc = (i // 2) % n_x, i % 2
        blocks.append(lax.ppermute(piece, sp_axes, shift(dx, dc)) if dx or dc else piece)

    out_other = other_core(out_weight)
    gates_up = (
        gate_weight[0],
        other_core(gate_weight[0]),
        up_weight[0],
        other_core(up_weight[0]),
    )
    downs = (down_weight[0], other_core(down_weight[0]))

    mine, given = attend(blocks[: 2 * n_x])
    acc = project_first(mine, other_core(given), out_weight, out_other)
    mine, given = attend(blocks[2 * n_x :])
    theirs = other_core(given)
    size = width // 2
    own, received = [], []
    for i in range(2):
        term, *sends = project_last(mine, theirs, out_weight, out_other, acc, i * size, size)
        own.append(term)
        received.append(
            [
                lax.ppermute(send, "x", [(x, (x - dx) % n_x) for x in range(n_x)])
                for dx, send in enumerate(sends, 1)
            ]
        )

    experts_count = 2 * n_ep
    capacity = max(2, 3 * tokens // experts_count)
    copies = n_x // 2
    n_cells = experts_count * capacity
    experts = route_experts[0]
    cell_index = ((experts % 2) * n_ep + experts // 2) * capacity + route_slots[0]

    cuts = ((0, 3 * width // 4), (3 * width // 4, width // 4))
    residual, *sent = norm_and_pack(
        latent[0], modulation, cell_index.T, n_cells, own, received, cuts
    )
    sums = ()
    for (start, size), part in zip(cuts, sent):
        part = jnp.broadcast_to(
            part.reshape(2, 1, n_ep, capacity, size), (2, copies, n_ep, capacity, size)
        ).reshape(n_x * n_ep, capacity, size)
        rows = lax.all_to_all(part, chip_axes, split_axis=0, concat_axis=0, tiled=True)
        sums = ffn_in(rows.reshape(-1, size), gates_up, sums, start, start + size == width)

    cuts = ((0, width // 4), (width // 4, 3 * width // 4))
    out = None
    for start, size in cuts:
        value = ffn_out(sums, downs, start, size).reshape(n_x * n_ep, capacity, size)
        back = lax.all_to_all(value, chip_axes, split_axis=0, concat_axis=0, tiled=True)
        back = back.reshape(2, copies, n_ep * capacity, size)
        out = combine(residual, modulation, cell_index, route_gates[0], back, start, out)
    return out[None]


def solution(mesh):
    n_sp, n_ep = mesh.devices.shape
    chips = Mesh(mesh.devices.reshape(n_sp // 2, 2, n_ep), ("x", "core", "ep"))
    sp = ("x", "core")
    return jax.shard_map(
        local,
        mesh=chips,
        in_specs=(
            P("ep", sp, None),
            P("ep", sp, None, None),
            P(sp, None),
            P(),
            P("ep", sp, None),
            P("ep", sp, None),
            P("ep", sp, None),
            P("ep", None, sp),
            P("ep", None, sp),
            P("ep", sp, None),
        ),
        out_specs=P("ep", sp, None),
        check_vma=False,
    )
```

time: 497 us -> 283 us (0.57)
  blocking collectives: 186 us -> 60.8 us
  waiting for transfers between devices: 187 us -> 107 us
  Pallas kernels: 0 us -> 72.2 us
  matrix products: 51.7 us -> 0 us
  starting transfers between devices: 3.97 us -> 28.5 us
  local copies, waits for them, and re-layouts: 36.8 us -> 13 us
  other arithmetic: 17.5 us -> 0.07 us
  between operations: 13.5 us -> 0.16 us
    all_to_all x2 -> x1, blocking collectives: 186 us -> 60.8 us  [local(): lax.all_to_all(part, chip_axes, split_axis=0, concat_axis=0, tiled=True)]
    all_to_all x1 -> x3, waiting for transfers between devices: 142 us -> 57.1 us  [the longest x2 57.1 us: local(): lax.all_to_all(value, chip_axes, split_axis=0, concat_axis=0, tiled=True)]
    pallas_call x0 -> x12, Pallas kernels: none -> 72.2 us  [the longest x2 23 us: ffn_in(): pl.pallas_call(functools.partial(ffn_in_kernel, not olds, last), grid=(un...]
    dot_general x6 -> x0, matrix products: 51.7 us -> none  [the longest x1 22.4 us: feed_forward(): jnp.dot(activation, down_shard, preferred_element_type=jnp.float32)]
    ppermute x0 -> x14, waiting for transfers between devices: none -> 49.8 us  [the longest x6 30.5 us: local(): lax.ppermute(piece, sp_axes, shift(dx, dc))]
    reduce_scatter x1 -> x0, waiting for transfers between devices: 44.9 us -> none  [local(): lax.psum_scatter(jnp.dot(flat_heads, out_weight, preferred_element_type=j...]
    gather x2 -> x0, local copies, waits for them, and re-layouts: 14.3 us -> none  [local(): jnp.take(per_expert, cell_index.reshape(-1), axis=0)]
    ppermute x0 -> x14, starting transfers between devices: none -> 14.3 us  [the longest x6 10.6 us: local(): lax.ppermute(piece, sp_axes, shift(dx, dc))]
  transfers between devices with their start and end apart: 2 -> 17, of which waited for: 2 -> 8; matrix products, arithmetic and copies ran while one was open for 0% -> 1% of each run, Pallas kernels for 0% -> 23%
where the time goes in v1:
time: 283 us; the launch traced here: 282 us
  waiting for transfers between devices  107 us (38%)
  Pallas kernels  72.2 us (26%)
  blocking collectives  60.8 us (21%)
  starting transfers between devices  28.5 us (10%)
  local copies, waits for them, and re-layouts  13 us (5%)
    all_to_all x1, blocking collectives, local(): lax.all_to_all(part, chip_axes, split_axis=0, concat_axis=0, tiled=True)  60.8 us
    all_to_all x2, waiting for transfers between devices, local(): lax.all_to_all(value, chip_axes, split_axis=0, concat_axis=0, tiled=True)  57.1 us
    ppermute x6, waiting for transfers between devices, local(): lax.ppermute(piece, sp_axes, shift(dx, dc))  30.5 us
    pallas_call x2, Pallas kernels, ffn_in(): pl.pallas_call(functools.partial(ffn_in_kernel, not olds, last), grid=(un...  23 us
    ppermute x2, waiting for transfers between devices, local(): lax.ppermute(send, 'x', [(x, (x - dx) % n_x) for x in range(n_x)])  19.3 us
    pallas_call x2, Pallas kernels, ffn_out(): pl.pallas_call(ffn_out_kernel, grid=(size // tile,), out_shape=jax.ShapeD...  14.3 us
    ppermute x6, starting transfers between devices, local(): lax.ppermute(piece, sp_axes, shift(dx, dc))  10.6 us
    all_to_all x2, starting transfers between devices, local(): lax.all_to_all(value, chip_axes, split_axis=0, concat_axis=0, tiled=True)  10.4 us
  transfers between devices with their start and end apart: 17, of which 8 were waited for; matrix products, arithmetic and copies ran while one was open for 1% of the time, Pallas kernels for 23%

profile of v1, /device:TPU:0, one launch (start us, length us, event | category | flops | bytes accessed | tf_op | source)
XLA Modules:
  0.0 281.6 jit_solution(17469901836285061672)
XLA Ops:
  2.4 2.9 %collective-permute-start.1 = (bf16[3,128,256]{2,1,0:T(8,128)(2,1)S(1)}, bf16[3,128,256]{2,1,0:T(8,128)(2,1)S(1)}, u32[]{:S(2)}, u32[]{:S(2)}) collective-permute-start(bf16[3,128,256]{2,1,0:T(8,128)(2,1)S(1)} %get-tuple-element.44), channel_id=1, source_target_pairs={{0,16},{8,24},{16,0},{24,8},{1,17},{9,25},{17,1},{25,9},{2,18},{10... | collective-permute-start | bytes 589832 | tf_op jit(solution)/shard_map/ppermute | solution.py:314
  5.3 1.8 dynamic-slice_bitcast_fusion
  7.1 6.7 %collective-permute-done.refs_1_ = bf16[3,128,256]{2,1,0:T(8,128)(2,1)S(1)} collective-permute-done((bf16[3,128,256]{2,1,0:T(8,128)(2,1)S(1)}, bf16[3,128,256]{2,1,0:T(8,128)(2,1)S(1)}, u32[]{:S(2)}, u32[]{:S(2)}) %collective-permute-start) | collective-permute-done | bytes 196640 | tf_op jit(solution)/shard_map/ppermute | solution.py:314
  14.2 2.6 collective-permute-start.6
  16.8 10.4 %collective-permute-done.5.refs_1_ = bf16[3,128,768]{2,1,0:T(8,128)(2,1)S(1)} collective-permute-done((bf16[3,128,768]{2,1,0:T(8,128)(2,1)S(1)}, bf16[3,128,768]{2,1,0:T(8,128)(2,1)S(1)}, u32[]{:S(2)}, u32[]{:S(2)}) %collective-permute-start.5) | collective-permute-done | bytes 589856 | tf_op jit(solution)/shard_map/ppermute | solution.py:314
  27.2 2.6 collective-permute-start.7
  30.7 12.5 %collective-permute-done.7.refs_3_ = bf16[3,128,768]{2,1,0:T(8,128)(2,1)S(1)} collective-permute-done((bf16[3,128,768]{2,1,0:T(8,128)(2,1)S(1)}, bf16[3,128,768]{2,1,0:T(8,128)(2,1)S(1)}, u32[]{:S(2)}, u32[]{:S(2)}) %collective-permute-start.7) | collective-permute-done | bytes 589856 | tf_op jit(solution)/shard_map/ppermute | solution.py:314
  43.2 1.9 collective-permute-start.2
  45.1 6.4 %shard_map.101 = (bf16[2,128,768]{2,1,0:T(8,128)(2,1)S(1)}, bf16[2,128,768]{2,1,0:T(8,128)(2,1)S(1)}) custom-call(bf16[3,128,768]{2,1,0:T(8,128)(2,1)S(1)} %get-tuple-element.41.refs_0_, bf16[3,128,768]{2,1,0:T(8,128)(2,1)S(1)} %collective-permute-done.5.refs_1_, bf16[3,128,768]{2,1,0:T(8,128)(2,1)S(1)} %collective-permute-done.6.refs_2_, ...), custom_call_target="tpu_custom_call" | custom-call | flops 3221225472 | bytes 3145728 | tf_op jit(solution)/shard_map/pallas_call | solution.py:51
  52.0 2.2 shard_map.100
  54.4 8.9 %shard_map.102.acc_ref = f32[256,4096]{1,0:T(8,128)S(1)} custom-call(bf16[2,128,768]{2,1,0:T(8,128)(2,1)S(1)} %get-tuple-element.24.mine_ref, bf16[2,128,768]{2,1,0:T(8,128)(2,1)S(1)} %collective-permute-done.8.theirs_ref, bf16[1024,4096]{1,0:T(8,128)(2,1)} %mine_w.5, bf16[1024,4096]{1,0:T(8,128)(2,1)} %collective-permute-done.4.theirs_w), custom_call_target="tpu_custom_call" | custom-call | flops 3221225472 | bytes 16777216 | tf_op jit(solution)/shard_map/pallas_call | solution.py:75
  63.4 4.1 %shard_map.104 = (f32[128,2048]{1,0:T(8,128)S(1)}, bf16[128,2048]{1,0:T(8,128)(2,1)}) custom-call(bf16[2,128,256]{2,1,0:T(8,128)(2,1)S(1)} %get-tuple-element.22.mine_ref, bf16[2,128,256]{2,1,0:T(8,128)(2,1)S(1)} %collective-permute-done.3.theirs_ref, bf16[1024,4096]{1,0:T(8,128)(2,1)} %mine_w.5, bf16[1024,4096]{1,0:T(8,128)(2,1)} %collective-permute-done.4.theirs_w, ...), custom_call_target="tpu_custom_call" | custom-call | flops 536870912 | bytes 6291456 | tf_op jit(solution)/shard_map/pallas_call | solution.py:105
  68.2 4.0 %shard_map.103 = (f32[128,2048]{1,0:T(8,128)S(1)}, bf16[128,2048]{1,0:T(8,128)(2,1)}) custom-call(bf16[2,128,256]{2,1,0:T(8,128)(2,1)S(1)} %get-tuple-element.22.mine_ref, bf16[2,128,256]{2,1,0:T(8,128)(2,1)S(1)} %collective-permute-done.3.theirs_ref, bf16[1024,4096]{1,0:T(8,128)(2,1)} %mine_w.5, bf16[1024,4096]{1,0:T(8,128)(2,1)} %collective-permute-done.4.theirs_w, ...), custom_call_target="tpu_custom_call" | custom-call | flops 536870912 | bytes 6291456 | tf_op jit(solution)/shard_map/pallas_call | solution.py:105
  74.0 8.6 %collective-permute-done.10.refs_3_ = bf16[128,2048]{1,0:T(8,128)(2,1)} collective-permute-done((bf16[128,2048]{1,0:T(8,128)(2,1)}, bf16[128,2048]{1,0:T(8,128)(2,1)}, u32[]{:S(2)}, u32[]{:S(2)}) %collective-permute-start.10) | collective-permute-done | bytes 524320 | tf_op jit(solution)/shard_map/ppermute | solution.py:336
  82.6 10.7 %collective-permute-done.9.refs_2_ = bf16[128,2048]{1,0:T(8,128)(2,1)} collective-permute-done((bf16[128,2048]{1,0:T(8,128)(2,1)}, bf16[128,2048]{1,0:T(8,128)(2,1)}, u32[]{:S(2)}, u32[]{:S(2)}) %collective-permute-start.9) | collective-permute-done | bytes 524320 | tf_op jit(solution)/shard_map/ppermute | solution.py:336
  93.3 4.2 %shard_map.105 = (f32[128,4096]{1,0:T(8,128)}, bf16[384,3072]{1,0:T(8,128)(2,1)}, bf16[384,1024]{1,0:T(8,128)(2,1)S(1)}) custom-call(bf16[128,4096]{1,0:T(8,128)(2,1)S(1)} %bitcast.73, f32[4,4096]{1,0:T(4,128)S(1)} %copy-done.9, s32[2,128]{1,0:T(2,128)S(1)} %copy.14.cells_ref, f32[128,2048]{1,0:T(8,128)S(1)} %get-tuple-element.26.refs_0_, ...), custom_call_target="tpu_custom_call" | custom-call | flops 402653184 | bytes 10485760 | tf_op jit(solution)/shard_map/pallas_call | solution.py:158
  97.5 60.8 %all_to_all.20 = bf16[16,24,3072]{2,1,0:T(8,128)(2,1)} all-to-all(bf16[16,24,3072]{2,1,0:T(8,128)(2,1)} %bitcast.87), channel_id=1, replica_groups=mesh['x'=2,'core'=2,'ep'=8] {'x','ep'}, dimensions={0} | all-to-all | bytes 4718592 | tf_op jit(solution)/shard_map/all_to_all | solution.py:357
  158.3 3.8 %all-to-all-start = ((bf16[16,24,1024]{2,1,0:T(8,128)(2,1)}), bf16[16,24,1024]{2,1,0:T(8,128)(2,1)S(1)}, u32[]{:S(2)}, u32[]{:S(2)}) async-start(bf16[16,24,1024]{2,1,0:T(8,128)(2,1)} %bitcast.74), calls=%async_computation | async-start | bytes 1572864 | tf_op jit(solution)/shard_map/all_to_all | solution.py:357
  162.1 16.0 %shard_map.106 = (f32[384,1024]{1,0:T(8,128)S(1)}, f32[384,1024]{1,0:T(8,128)S(1)}, f32[384,1024]{1,0:T(8,128)S(1)}, f32[384,1024]{1,0:T(8,128)}) custom-call(bf16[384,3072]{1,0:T(8,128)(2,1)} %bitcast.86, bf16[4096,1024]{1,0:T(8,128)(2,1)} %bitcast.78, bf16[4096,1024]{1,0:T(8,128)(2,1)} %collective-permute-done.11.refs_1_, bf16[4096,1024]{1,0:T(8,128)(2,1)} %bitcast.81, ...), custom_call_target="tpu_custom_call" | custom-call | flops 9663676416 | bytes 31457280 | tf_op jit(solution)/shard_map/pallas_call | solution.py:192
  181.7 1.4 copy-done.3
  183.1 1.4 copy-done.5
  184.5 6.9 %shard_map.107 = (bf16[384,1024]{1,0:T(8,128)(2,1)S(1)}, bf16[384,1024]{1,0:T(8,128)(2,1)S(1)}) custom-call(bf16[384,1024]{1,0:T(8,128)(2,1)S(1)} %bitcast.71, bf16[4096,1024]{1,0:T(8,128)(2,1)} %bitcast.79, bf16[4096,1024]{1,0:T(8,128)(2,1)} %collective-permute-done.11.refs_1_, bf16[4096,1024]{1,0:T(8,128)(2,1)} %bitcast.82, ...), custom_call_target="tpu_custom_call" | custom-call | flops 3221225472 | bytes 14680064 | tf_op jit(solution)/shard_map/pallas_call | solution.py:192
  191.5 4.3 %shard_map.109 = bf16[384,1024]{1,0:T(8,128)(2,1)} custom-call(bf16[384,1024]{1,0:T(8,128)(2,1)S(1)} %get-tuple-element.37.mine_ref, bf16[384,1024]{1,0:T(8,128)(2,1)S(1)} %get-tuple-element.38.theirs_ref, bf16[1024,4096]{1,0:T(8,128)(2,1)} %bitcast.84, bf16[1024,4096]{1,0:T(8,128)(2,1)} %collective-permute-done.13.theirs_w), custom_call_target="tpu_custom_call" | custom-call | flops 1610612736 | bytes 4980736 | tf_op jit(solution)/shard_map/pallas_call | solution.py:214
  195.7 6.7 %all-to-all-start.3 = ((bf16[16,24,1024]{2,1,0:T(8,128)(2,1)}), bf16[16,24,1024]{2,1,0:T(8,128)(2,1)S(1)}, u32[]{:S(2)}, u32[]{:S(2)}) async-start(bf16[16,24,1024]{2,1,0:T(8,128)(2,1)} %bitcast.30), calls=%async_computation.3 | async-start | bytes 1572864 | tf_op jit(solution)/shard_map/all_to_all | solution.py:364
  202.4 10.0 %shard_map.108 = bf16[384,3072]{1,0:T(8,128)(2,1)} custom-call(bf16[384,1024]{1,0:T(8,128)(2,1)S(1)} %get-tuple-element.37.mine_ref, bf16[384,1024]{1,0:T(8,128)(2,1)S(1)} %get-tuple-element.38.theirs_ref, bf16[1024,4096]{1,0:T(8,128)(2,1)} %bitcast.85, bf16[1024,4096]{1,0:T(8,128)(2,1)} %collective-permute-done.13.theirs_w), custom_call_target="tpu_custom_call" | custom-call | flops 4831838208 | bytes 14942208 | tf_op jit(solution)/shard_map/pallas_call | solution.py:214
  212.4 9.0 %all-to-all-done.3 = bf16[16,24,1024]{2,1,0:T(8,128)(2,1)S(1)} async-done(((bf16[16,24,1024]{2,1,0:T(8,128)(2,1)}), bf16[16,24,1024]{2,1,0:T(8,128)(2,1)S(1)}, u32[]{:S(2)}, u32[]{:S(2)}) %all-to-all-start.3) | async-done | bytes 786464 | tf_op jit(solution)/shard_map/all_to_all | solution.py:364
  221.4 3.7 %all-to-all-start.2 = ((bf16[16,24,3072]{2,1,0:T(8,128)(2,1)}), bf16[16,24,3072]{2,1,0:T(8,128)(2,1)S(1)}, u32[]{:S(2)}, u32[]{:S(2)}) async-start(bf16[16,24,3072]{2,1,0:T(8,128)(2,1)} %bitcast.28), calls=%async_computation.2 | async-start | bytes 4718592 | tf_op jit(solution)/shard_map/all_to_all | solution.py:364
  225.3 1.6 copy-done
  226.9 1.5 shard_map.110.refs_0_
  228.4 48.1 %all-to-all-done.2 = bf16[16,24,3072]{2,1,0:T(8,128)(2,1)S(1)} async-done(((bf16[16,24,3072]{2,1,0:T(8,128)(2,1)}), bf16[16,24,3072]{2,1,0:T(8,128)(2,1)S(1)}, u32[]{:S(2)}, u32[]{:S(2)}) %all-to-all-start.2) | async-done | bytes 2359328 | tf_op jit(solution)/shard_map/all_to_all | solution.py:364
  276.5 1.6 copy-done.1
  278.0 3.6 %shard_map.111 = bf16[128,4096]{1,0:T(8,128)(2,1)} custom-call(f32[128,4096]{1,0:T(8,128)S(1)} %copy-done.1, f32[4,4096]{1,0:T(4,128)S(1)} %copy-done.9, s32[128,2]{1,0:T(8,128)S(1)} %fusion.3.cells_ref, f32[128,2]{1,0:T(8,128)S(1)} %bitcast.76, bf16[2,1,192,3072]{3,2,1,0:T(8,128)(2,1)S(1)} %bitcast.69, ...), custom_call_target="tpu_custom_call", output_to_operand_aliasing={{}: (5, {})} | custom-call | flops 603979776 | bytes 4718592 | tf_op jit(solution)/shard_map/pallas_call | solution.py:250
  (48 shorter events, 10.4 us)
Async XLA Ops:
  0.0 54.4 %collective-permute-start.4 = (bf16[1024,4096]{1,0:T(8,128)(2,1)}, bf16[1024,4096]{1,0:T(8,128)(2,1)}, u32[]{:S(2)}, u32[]{:S(2)}) collective-permute-start(bf16[1024,4096]{1,0:T(8,128)(2,1)} %mine_w.5), channel_id=1, source_target_pairs={{0,8},{8,0},{1,9},{9,1},{2,10},{10,2},{3,11},{11,3},{4,12},{12,4},... | collective-permute-start | bytes 25165832 | tf_op jit(solution)/shard_map/ppermute | solution.py:293
  0.5 161.6 %collective-permute-start.11 = (bf16[4096,1024]{1,0:T(8,128)(2,1)}, bf16[4096,1024]{1,0:T(8,128)(2,1)}, u32[]{:S(2)}, u32[]{:S(2)}) collective-permute-start(bf16[4096,1024]{1,0:T(8,128)(2,1)} %bitcast.77), channel_id=1, source_target_pairs={{0,8},{8,0},{1,9},{9,1},{2,10},{10,2},{3,11},{11,3},{4,12},{12,4},... | collective-permute-start | bytes 25165832 | tf_op jit(solution)/shard_map/ppermute | solution.py:293
  0.5 161.6 %collective-permute-start.12 = (bf16[4096,1024]{1,0:T(8,128)(2,1)}, bf16[4096,1024]{1,0:T(8,128)(2,1)}, u32[]{:S(2)}, u32[]{:S(2)}) collective-permute-start(bf16[4096,1024]{1,0:T(8,128)(2,1)} %bitcast.80), channel_id=1, source_target_pairs={{0,8},{8,0},{1,9},{9,1},{2,10},{10,2},{3,11},{11,3},{4,12},{12,4},... | collective-permute-start | bytes 25165832 | tf_op jit(solution)/shard_map/ppermute | solution.py:293
  2.2 11.6 %collective-permute-start = (bf16[3,128,256]{2,1,0:T(8,128)(2,1)S(1)}, bf16[3,128,256]{2,1,0:T(8,128)(2,1)S(1)}, u32[]{:S(2)}, u32[]{:S(2)}) collective-permute-start(bf16[3,128,256]{2,1,0:T(8,128)(2,1)S(1)} %get-tuple-element.45), channel_id=1, source_target_pairs={{0,8},{8,0},{16,24},{24,16},{1,9},{9,1},{17,25},{25,17},{2,10},{10... | collective-permute-start | bytes 589832 | tf_op jit(solution)/shard_map/ppermute | solution.py:314
  2.4 11.8 %collective-permute-start.1 = (bf16[3,128,256]{2,1,0:T(8,128)(2,1)S(1)}, bf16[3,128,256]{2,1,0:T(8,128)(2,1)S(1)}, u32[]{:S(2)}, u32[]{:S(2)}) collective-permute-start(bf16[3,128,256]{2,1,0:T(8,128)(2,1)S(1)} %get-tuple-element.44), channel_id=1, source_target_pairs={{0,16},{8,24},{16,0},{24,8},{1,17},{9,25},{17,1},{25,9},{2,18},{10... | collective-permute-start | bytes 589832 | tf_op jit(solution)/shard_map/ppermute | solution.py:314
  13.8 13.4 %collective-permute-start.5 = (bf16[3,128,768]{2,1,0:T(8,128)(2,1)S(1)}, bf16[3,128,768]{2,1,0:T(8,128)(2,1)S(1)}, u32[]{:S(2)}, u32[]{:S(2)}) collective-permute-start(bf16[3,128,768]{2,1,0:T(8,128)(2,1)S(1)} %get-tuple-element.40), channel_id=1, source_target_pairs={{0,8},{8,0},{16,24},{24,16},{1,9},{9,1},{17,25},{25,17},{2,10},{10... | collective-permute-start | bytes 1769480 | tf_op jit(solution)/shard_map/ppermute | solution.py:314
  14.2 16.5 %collective-permute-start.6 = (bf16[3,128,768]{2,1,0:T(8,128)(2,1)S(1)}, bf16[3,128,768]{2,1,0:T(8,128)(2,1)S(1)}, u32[]{:S(2)}, u32[]{:S(2)}) collective-permute-start(bf16[3,128,768]{2,1,0:T(8,128)(2,1)S(1)} %get-tuple-element.42), channel_id=1, source_target_pairs={{0,16},{8,24},{16,0},{24,8},{1,17},{9,25},{17,1},{25,9},{2,18},{10... | collective-permute-start | bytes 1769480 | tf_op jit(solution)/shard_map/ppermute | solution.py:314
  27.2 16.0 %collective-permute-start.7 = (bf16[3,128,768]{2,1,0:T(8,128)(2,1)S(1)}, bf16[3,128,768]{2,1,0:T(8,128)(2,1)S(1)}, u32[]{:S(2)}, u32[]{:S(2)}) collective-permute-start(bf16[3,128,768]{2,1,0:T(8,128)(2,1)S(1)} %get-tuple-element.39), channel_id=1, source_target_pairs={{0,24},{8,16},{16,8},{24,0},{1,25},{9,17},{17,9},{25,1},{2,26},{10... | collective-permute-start | bytes 1769480 | tf_op jit(solution)/shard_map/ppermute | solution.py:314
  30.7 160.8 %collective-permute-start.13 = (bf16[1024,4096]{1,0:T(8,128)(2,1)}, bf16[1024,4096]{1,0:T(8,128)(2,1)}, u32[]{:S(2)}, u32[]{:S(2)}) collective-permute-start(bf16[1024,4096]{1,0:T(8,128)(2,1)} %bitcast.83), channel_id=1, source_target_pairs={{0,8},{8,0},{1,9},{9,1},{2,10},{10,2},{3,11},{11,3},{4,12},{12,4},... | collective-permute-start | bytes 25165832 | tf_op jit(solution)/shard_map/ppermute | solution.py:293
  43.2 8.3 %collective-permute-start.2 = (bf16[3,128,256]{2,1,0:T(8,128)(2,1)S(1)}, bf16[3,128,256]{2,1,0:T(8,128)(2,1)S(1)}, u32[]{:S(2)}, u32[]{:S(2)}) collective-permute-start(bf16[3,128,256]{2,1,0:T(8,128)(2,1)S(1)} %get-tuple-element.43), channel_id=1, source_target_pairs={{0,24},{8,16},{16,8},{24,0},{1,25},{9,17},{17,9},{25,1},{2,26},{10... | collective-permute-start | bytes 589832 | tf_op jit(solution)/shard_map/ppermute | solution.py:314
  51.5 2.7 collective-permute-start.8
  54.2 9.2 %collective-permute-start.3 = (bf16[2,128,256]{2,1,0:T(8,128)(2,1)S(1)}, bf16[2,128,256]{2,1,0:T(8,128)(2,1)S(1)}, u32[]{:S(2)}, u32[]{:S(2)}) collective-permute-start(bf16[2,128,256]{2,1,0:T(8,128)(2,1)S(1)} %get-tuple-element.23), channel_id=1, source_target_pairs={{0,8},{8,0},{1,9},{9,1},{2,10},{10,2},{3,11},{11,3},{4,12},{12,4},... | collective-permute-start | bytes 393224 | tf_op jit(solution)/shard_map/ppermute | solution.py:293
  67.5 6.2 %copy-start.10 = (s32[1,128,2]{1,2,0:T(2,128)S(1)}, s32[1,128,2]{1,2,0:T(2,128)}, u32[]{:S(2)}) copy-start(s32[1,128,2]{1,2,0:T(2,128)} %param.14) | copy-start | bytes 3076
  67.5 6.3 %copy-start.11 = (s32[1,128,2]{1,2,0:T(2,128)S(1)}, s32[1,128,2]{1,2,0:T(2,128)}, u32[]{:S(2)}) copy-start(s32[1,128,2]{1,2,0:T(2,128)} %param.15) | copy-start | bytes 3076
  67.5 25.8 %copy-start.7 = (bf16[1,128,4096]{2,1,0:T(8,128)(2,1)S(1)}, bf16[1,128,4096]{2,1,0:T(8,128)(2,1)}, u32[]{:S(2)}) copy-start(bf16[1,128,4096]{2,1,0:T(8,128)(2,1)} %param.10) | copy-start | bytes 3145732
  67.5 25.8 %copy-start.9 = (f32[4,4096]{1,0:T(4,128)S(1)}, f32[4,4096]{1,0:T(4,128)}, u32[]{:S(2)}) copy-start(f32[4,4096]{1,0:T(4,128)} %mod_ref.5) | copy-start | bytes 196612
  67.5 15.1 %collective-permute-start.10 = (bf16[128,2048]{1,0:T(8,128)(2,1)}, bf16[128,2048]{1,0:T(8,128)(2,1)}, u32[]{:S(2)}, u32[]{:S(2)}) collective-permute-start(bf16[128,2048]{1,0:T(8,128)(2,1)} %get-tuple-element.29), channel_id=1, source_target_pairs={{0,16},{16,0},{1,17},{17,1},{2,18},{18,2},{3,19},{19,3},{4,20},{20... | collective-permute-start | bytes 1572872 | tf_op jit(solution)/shard_map/ppermute | solution.py:336
  72.2 21.0 %collective-permute-start.9 = (bf16[128,2048]{1,0:T(8,128)(2,1)}, bf16[128,2048]{1,0:T(8,128)(2,1)}, u32[]{:S(2)}, u32[]{:S(2)}) collective-permute-start(bf16[128,2048]{1,0:T(8,128)(2,1)} %get-tuple-element.28), channel_id=1, source_target_pairs={{0,16},{16,0},{1,17},{17,1},{2,18},{18,2},{3,19},{19,3},{4,20},{20... | collective-permute-start | bytes 1572872 | tf_op jit(solution)/shard_map/ppermute | solution.py:336
  97.5 60.8 %copy-start.8 = (bf16[384,1024]{1,0:T(8,128)(2,1)}, bf16[384,1024]{1,0:T(8,128)(2,1)S(1)}, u32[]{:S(2)}) copy-start(bf16[384,1024]{1,0:T(8,128)(2,1)S(1)} %get-tuple-element.31) | copy-start | bytes 2359300
  158.3 23.4 %all-to-all-start = ((bf16[16,24,1024]{2,1,0:T(8,128)(2,1)}), bf16[16,24,1024]{2,1,0:T(8,128)(2,1)S(1)}, u32[]{:S(2)}, u32[]{:S(2)}) async-start(bf16[16,24,1024]{2,1,0:T(8,128)(2,1)} %bitcast.74), calls=%async_computation | async-start | bytes 1572864 | tf_op jit(solution)/shard_map/all_to_all | solution.py:357
  178.1 1.2 copy-start.2
  179.4 1.2 copy-start.4
  180.5 1.1 copy-start.6
  181.7 1.4 copy-start.3
  183.1 1.4 copy-start.5
  195.7 25.7 %all-to-all-start.3 = ((bf16[16,24,1024]{2,1,0:T(8,128)(2,1)}), bf16[16,24,1024]{2,1,0:T(8,128)(2,1)S(1)}, u32[]{:S(2)}, u32[]{:S(2)}) async-start(bf16[16,24,1024]{2,1,0:T(8,128)(2,1)} %bitcast.30), calls=%async_computation.3 | async-start | bytes 1572864 | tf_op jit(solution)/shard_map/all_to_all | solution.py:364
  212.4 12.7 %copy-start.12 = (f32[1,128,2]{1,2,0:T(2,128)S(1)}, f32[1,128,2]{1,2,0:T(2,128)}, u32[]{:S(2)}) copy-start(f32[1,128,2]{1,2,0:T(2,128)} %param.16) | copy-start | bytes 3076
  221.4 55.0 %all-to-all-start.2 = ((bf16[16,24,3072]{2,1,0:T(8,128)(2,1)}), bf16[16,24,3072]{2,1,0:T(8,128)(2,1)S(1)}, u32[]{:S(2)}, u32[]{:S(2)}) async-start(bf16[16,24,3072]{2,1,0:T(8,128)(2,1)} %bitcast.28), calls=%async_computation.2 | async-start | bytes 4718592 | tf_op jit(solution)/shard_map/all_to_all | solution.py:364
  225.3 1.6 copy-start
  276.4 1.6 copy-start.1

commit v2 on v0

v2 whole, which is shorter than its diff:
```python
import functools
import math

import jax
import jax.numpy as jnp
from jax import lax
from jax.experimental import pallas as pl
from jax.experimental.pallas import tpu as pltpu
from jax.sharding import Mesh, PartitionSpec as P

HD = 128
LANES = 128
VMEM = pl.BlockSpec(memory_space=pltpu.VMEM)
LOW = pl.CostEstimate(flops=1024, bytes_accessed=1024, transcendentals=0)


def dot32(a, b):
    return jnp.dot(a, b, preferred_element_type=jnp.float32)


def grant(mebibytes):
    return pltpu.CompilerParams(vmem_limit_bytes=mebibytes * 1024 * 1024)


def after(value, token):
    return lax.optimization_barrier((value, token))[0]


FACTOR = math.log2(math.e) / math.sqrt(HD)


def score(queries, key_rows):
    return lax.dot_general(
        queries, key_rows, (((1,), (1,)), ((), ())), preferred_element_type=jnp.float32
    )


def weigh(scores, top):
    lifted = jnp.exp2((scores - top) * FACTOR)
    return lifted.astype(jnp.bfloat16), jnp.sum(lifted, axis=-1, keepdims=True)


def attend_first_kernel(*refs):
    *blocks, mixed_ref, top_ref, total_ref = refs
    for head in range(mixed_ref.shape[-1] // HD):
        cols = slice(head * HD, (head + 1) * HD)
        key_rows = jnp.concatenate([block[1, :, cols] for block in blocks], axis=0)
        value_rows = jnp.concatenate([block[2, :, cols] for block in blocks], axis=0)
        for i, block in enumerate(blocks):
            scores = score(block[0, :, cols], key_rows)
            top = jnp.max(scores, axis=-1, keepdims=True)
            weights, total = weigh(scores, top)
            mixed_ref[i, :, cols] = dot32(weights, value_rows)
            top_ref[i, :, head : head + 1] = top
            total_ref[i, :, head : head + 1] = total


def attend_first(blocks):
    _, tokens, width = blocks[0].shape
    count, heads = len(blocks), width // HD
    small = jax.ShapeDtypeStruct((count, tokens, heads), jnp.float32)
    return pl.pallas_call(
        attend_first_kernel,
        out_shape=(jax.ShapeDtypeStruct((count, tokens, width), jnp.float32), small, small),
        in_specs=[VMEM] * count,
        out_specs=(VMEM,) * 3,
        compiler_params=grant(28),
        cost_estimate=LOW,
    )(*blocks)


def attend_last_kernel(*refs):
    *blocks, mixed_ref, top_ref, total_ref, keep_ref, give_ref = refs
    last = len(blocks) - 1
    for head in range(keep_ref.shape[-1] // HD):
        cols = slice(head * HD, (head + 1) * HD)
        key_rows = jnp.concatenate([block[1, :, cols] for block in blocks], axis=0)
        value_rows = jnp.concatenate([block[2, :, cols] for block in blocks], axis=0)
        for i, block in enumerate(blocks):
            queries = block[0, :, cols]
            if i == last:
                scores = score(queries, key_rows)
                top = jnp.max(scores, axis=-1, keepdims=True)
                weights, total = weigh(scores, top)
                mixed = dot32(weights, value_rows)
            else:
                scores = score(queries, blocks[last][1, :, cols])
                old_top = top_ref[i, :, head : head + 1]
                top = jnp.maximum(old_top, jnp.max(scores, axis=-1, keepdims=True))
                scale = jnp.exp2((old_top - top) * FACTOR)
                weights, total = weigh(scores, top)
                total = total + total_ref[i, :, head : head + 1] * scale
                mixed = dot32(weights, blocks[last][2, :, cols])
                mixed = mixed + mixed_ref[i, :, cols] * scale
            out_ref = give_ref if i % 2 else keep_ref
            out_ref[i // 2, :, cols] = (mixed / total).astype(jnp.bfloat16)


def attend_last(blocks, partial_sums):
    _, tokens, width = blocks[0].shape
    count = len(blocks)
    out = jax.ShapeDtypeStruct((count // 2, tokens, width), jnp.bfloat16)
    return pl.pallas_call(
        attend_last_kernel,
        out_shape=(out, out),
        in_specs=[VMEM] * (count + 3),
        out_specs=(VMEM, VMEM),
        compiler_params=grant(28),
        cost_estimate=LOW,
    )(*blocks, *partial_sums)


def project_kernel(mine_ref, theirs_ref, mine_w, theirs_w, own_ref, *send_refs):
    n_x, tokens, width = mine_ref.shape
    mine = mine_ref[...].reshape(n_x * tokens, width)
    theirs = theirs_ref[...].reshape(n_x * tokens, width)
    total = dot32(mine, mine_w[...]) + dot32(theirs, theirs_w[...])
    own_ref[...] = total[:tokens]
    for i, send_ref in enumerate(send_refs):
        send_ref[...] = total[(i + 1) * tokens : (i + 2) * tokens].astype(jnp.bfloat16)


def project(mine, theirs, mine_w, theirs_w, start, size):
    n_x, tokens, depth = mine.shape
    tile = min(1024, size)
    first = start // tile
    whole = pl.BlockSpec((n_x, tokens, depth), lambda n: (0, 0, 0))
    weight = pl.BlockSpec((depth, tile), lambda n: (0, first + n))
    return pl.pallas_call(
        project_kernel,
        grid=(size // tile,),
        out_shape=[jax.ShapeDtypeStruct((tokens, size), jnp.float32)]
        + [jax.ShapeDtypeStruct((tokens, size), jnp.bfloat16)] * (n_x - 1),
        in_specs=[whole, whole, weight, weight],
        out_specs=[pl.BlockSpec((tokens, tile), lambda n: (0, n))] * n_x,
        compiler_params=grant(28),
        cost_estimate=LOW,
    )(mine, theirs, mine_w, theirs_w)


def residual_kernel(start, n_recv, old_size, latent_ref, mod_ref, own_ref, *refs):
    recv_refs, old_refs = refs[:n_recv], refs[n_recv:-2]
    residual_ref, stats_ref = refs[-2:]
    size = own_ref.shape[1]
    cut = slice(start, start + size)
    projected = own_ref[...]
    for recv_ref in recv_refs:
        projected = projected + recv_ref[...].astype(jnp.float32)
    part = latent_ref[:, cut].astype(jnp.float32) + mod_ref[0:1, cut] * projected
    residual_ref[...] = part
    mean = jnp.mean(part, axis=-1, keepdims=True)
    centered = part - mean
    square = jnp.sum(centered * centered, axis=-1, keepdims=True)
    for old_ref in old_refs:
        old_mean, old_square = old_ref[:, 0:1], old_ref[:, 1:2]
        gap = old_mean - mean
        width = size + old_size
        mean = mean + gap * (old_size / width)
        square = square + old_square + gap * gap * (size * old_size / width)
        square = lax.rsqrt(square / width + 1e-06)
    stats_ref[:, 0:1] = mean
    stats_ref[:, 1:2] = square


def residual_part(latent, modulation, own, received, olds, start):
    tokens, size = own.shape
    return pl.pallas_call(
        functools.partial(residual_kernel, start, len(received), start),
        out_shape=[
            jax.ShapeDtypeStruct((tokens, size), jnp.float32),
            jax.ShapeDtypeStruct((tokens, 2), jnp.float32),
        ],
        in_specs=[VMEM] * (3 + len(received) + len(olds)),
        out_specs=[VMEM] * 2,
        compiler_params=grant(28),
        cost_estimate=LOW,
    )(latent, modulation, own, *received, *olds)


def route_rows(cells_ref, sent_ref):
    tokens = cells_ref.shape[1]
    cells = lax.broadcasted_iota(jnp.int32, (sent_ref.shape[0], tokens), 0)
    return ((cells == cells_ref[0:1, :]) | (cells == cells_ref[1:2, :])).astype(jnp.bfloat16)


def pack_raw_kernel(cells_ref, part_ref, sent_ref):
    rows = part_ref[...].astype(jnp.bfloat16)
    sent_ref[...] = dot32(route_rows(cells_ref, sent_ref), rows).astype(jnp.bfloat16)


def pack_raw(cells, n_cells, part):
    return pl.pallas_call(
        pack_raw_kernel,
        out_shape=jax.ShapeDtypeStruct((n_cells, part.shape[1]), jnp.bfloat16),
        in_specs=[VMEM] * 2,
        out_specs=VMEM,
        compiler_params=grant(28),
        cost_estimate=LOW,
    )(cells, part)


def normed(part, mean, inverse, mod_ref, cut):
    rows = (part - mean) * inverse
    return (rows * (1.0 + mod_ref[2:3, cut]) + mod_ref[1:2, cut]).astype(jnp.bfloat16)


def pack_kernel(start, low, size, with_stats, mod_ref, cells_ref, stats_ref, part_ref, sent_ref):
    one_hot = route_rows(cells_ref, sent_ref)
    cut = slice(start + low, start + low + size)
    part = part_ref[:, low : low + size]
    moe_in = normed(part, stats_ref[:, 0:1], stats_ref[:, 1:2], mod_ref, cut)
    sent_ref[:, :size] = dot32(one_hot, moe_in).astype(jnp.bfloat16)
    if with_stats:
        tokens = part.shape[0]
        lane = lax.broadcasted_iota(jnp.int32, (tokens, LANES), 1)
        block = jnp.zeros((tokens, LANES), jnp.float32)
        for i in range(2):
            rest = stats_ref[:, i : i + 1]
            for j in range(3):
                piece = rest.astype(jnp.bfloat16).astype(jnp.float32)
                block = jnp.where(lane == 3 * i + j, piece, block)
                rest = rest - piece
        sent_ref[:, size:] = dot32(one_hot, block.astype(jnp.bfloat16)).astype(jnp.bfloat16)


def pack(modulation, cells, n_cells, stats, part, start, low, size, with_stats):
    wide = size + LANES if with_stats else size
    return pl.pallas_call(
        functools.partial(pack_kernel, start, low, size, with_stats),
        out_shape=jax.ShapeDtypeStruct((n_cells, wide), jnp.bfloat16),
        in_specs=[VMEM] * 4,
        out_specs=VMEM,
        compiler_params=grant(28),
        cost_estimate=LOW,
    )(modulation, cells, stats, part)


def ffn_first_kernel(mod_ref, raw_ref, rows_ref, *refs):
    weights, sums, raw_rows = refs[:4], refs[4:8], refs[8]
    size = raw_ref.shape[1]
    rest = weights[0].shape[0] - size

    @pl.when(pl.program_id(0) == 0)
    def _():
        pieces = rows_ref[:, rest : rest + LANES].astype(jnp.float32)
        mean, inverse = (
            pieces[:, i : i + 1] + pieces[:, i + 1 : i + 2] + pieces[:, i + 2 : i + 3]
            for i in (0, 3)
        )
        part = raw_ref[...].astype(jnp.float32)
        raw_rows[...] = normed(part, mean, inverse, mod_ref, slice(0, size))

    for weight, total_ref in zip(weights, sums):
        total_ref[...] = dot32(raw_rows[...], weight[:size]) + dot32(
            rows_ref[:, :rest], weight[size:]
        )


def ffn_first(modulation, raw, rows, weights):
    count, size = raw.shape
    units = weights[0].shape[1]
    tile = min(256, units)
    depth = size + rows.shape[1] - LANES
    weight = pl.BlockSpec((depth, tile), lambda n: (0, n))
    return pl.pallas_call(
        ffn_first_kernel,
        grid=(units // tile,),
        out_shape=[jax.ShapeDtypeStruct((count, units), jnp.float32)] * 4,
        in_specs=[
            pl.BlockSpec(modulation.shape, lambda n: (0, 0)),
            pl.BlockSpec(raw.shape, lambda n: (0, 0)),
            pl.BlockSpec(rows.shape, lambda n: (0, 0)),
        ]
        + [weight] * 4,
        out_specs=[pl.BlockSpec((count, tile), lambda n: (0, n))] * 4,
        scratch_shapes=[pltpu.VMEM(raw.shape, jnp.bfloat16)],
        compiler_params=grant(57),
        cost_estimate=LOW,
    )(modulation, raw, rows, *weights)


def ffn_last_kernel(rows_ref, *refs):
    weights, olds, outs = refs[:4], refs[4:8], refs[8:]
    rows = rows_ref[...]
    sums = [dot32(rows, weight[...]) + old[...] for weight, old in zip(weights, olds)]
    for gate, up, out_ref in zip(sums[:2], sums[2:], outs):
        out_ref[...] = (gate / (1.0 + jnp.exp(-gate)) * up).astype(jnp.bfloat16)


def ffn_last(rows, weights, olds):
    count, size = rows.shape
    depth, units = weights[0].shape
    tile = min(256, units)
    block = depth // size - 1
    weight = pl.BlockSpec((size, tile), lambda n: (block, n))
    part = pl.BlockSpec((count, tile), lambda n: (0, n))
    return pl.pallas_call(
        ffn_last_kernel,
        grid=(units // tile,),
        out_shape=[jax.ShapeDtypeStruct((count, units), jnp.bfloat16)] * 2,
        in_specs=[pl.BlockSpec((count, size), lambda n: (0, 0))] + [weight] * 4 + [part] * 4,
        out_specs=[part] * 2,
        compiler_params=grant(57),
        cost_estimate=LOW,
    )(rows, *weights, *olds)


def ffn_out_kernel(mine_ref, theirs_ref, mine_w, theirs_w, out_ref):
    total = dot32(mine_ref[...], mine_w[...]) + dot32(theirs_ref[...], theirs_w[...])
    out_ref[...] = total.astype(jnp.bfloat16)


def ffn_out(acts, weights, start, size):
    count, units = acts[0].shape
    tile = min(512, size)
    first = start // tile
    act = pl.BlockSpec((count, units), lambda n: (0, 0))
    weight = pl.BlockSpec((units, tile), lambda n: (0, first + n))
    return pl.pallas_call(
        ffn_out_kernel,
        grid=(size // tile,),
        out_shape=jax.ShapeDtypeStruct((count, size), jnp.bfloat16),
        in_specs=[act, act, weight, weight],
        out_specs=pl.BlockSpec((count, tile), lambda n: (0, n)),
        compiler_params=grant(57),
        cost_estimate=LOW,
    )(*acts, *weights)


def combine_kernel(residual_ref, mod_ref, cells_ref, gates_ref, back_ref, *refs):
    out_ref = refs[-1]
    tokens, tile = out_ref.shape
    _, copies, half, _ = back_ref.shape
    cells = lax.broadcasted_iota(jnp.int32, (tokens, 2 * half), 1)
    one_hot = jnp.concatenate(
        [(cells == cells_ref[:, i : i + 1]).astype(jnp.bfloat16) for i in range(2)], axis=0
    )
    picked = 0.0
    for i in range(copies):
        picked = picked + dot32(one_hot, back_ref[:, i].reshape(2 * half, tile))
    combined = gates_ref[:, 0:1] * picked[:tokens] + gates_ref[:, 1:2] * picked[tokens:]
    out_ref[...] = (residual_ref[...] + mod_ref[3:4, :] * combined).astype(jnp.bfloat16)


def combine(residual, modulation, cells, gates, back, start, previous):
    tokens, size = residual.shape
    width = modulation.shape[1]
    _, copies, half, _ = back.shape
    tile = min(1024, size)
    first = start // tile
    wide = pl.BlockSpec((tokens, tile), lambda n: (0, first + n))
    small = pl.BlockSpec((tokens, 2), lambda n: (0, 0))
    more = [] if previous is None else [previous]
    return pl.pallas_call(
        combine_kernel,
        grid=(size // tile,),
        out_shape=jax.ShapeDtypeStruct((tokens, width), jnp.bfloat16),
        in_specs=[
            pl.BlockSpec((tokens, tile), lambda n: (0, n)),
            pl.BlockSpec((4, tile), lambda n: (0, first + n)),
            small,
            small,
            pl.BlockSpec((2, copies, half, tile), lambda n: (0, 0, 0, n)),
        ]
        + [pl.BlockSpec(memory_space=pl.ANY)] * len(more),
        out_specs=wide,
        input_output_aliases={5: 0} if more else {},
        compiler_params=grant(28),
        cost_estimate=LOW,
    )(residual, modulation, cells, gates, back, *more)


def local(
    latent,
    attention_in,
    out_weight,
    modulation,
    route_experts,
    route_slots,
    route_gates,
    gate_weight,
    up_weight,
    down_weight,
):
    n_x = lax.axis_size("x")
    n_ep = lax.axis_size("ep")
    tokens = latent.shape[1]
    width = latent.shape[2]
    group_width = out_weight.shape[0]
    my_x = lax.axis_index("x")
    my_core = lax.axis_index("core")
    latent = latent[0]

    def other_core(value):
        return lax.ppermute(value, "core", [(0, 1), (1, 0)])

    def exchange(value):
        part = value.shape[-1]
        value = value.reshape(n_x * n_ep, -1, part)
        return lax.all_to_all(value, ("x", "ep"), split_axis=0, concat_axis=0, tiled=True)

    def shift(dx, dc):
        return [
            (2 * x + c, 2 * ((x + dx) % n_x) + (c ^ dc)) for x in range(n_x) for c in range(2)
        ]

    packed = jnp.transpose(attention_in[0], (1, 0, 2))
    pieces, blocks = [], []
    for dx in range(n_x):
        for dc in range(2):
            group = 2 * ((my_x + dx) % n_x) + (my_core ^ dc)
            piece = lax.dynamic_slice_in_dim(packed, group * group_width, group_width, axis=2)
            pieces.append(piece)
            if dx or dc:
                piece = lax.ppermute(piece, ("x", "core"), shift(dx, dc))
            blocks.append(piece)

    out_other = other_core(after(out_weight, pieces[1]))
    mine, given = attend_last(blocks, attend_first(blocks[:-1]))
    theirs = other_core(given)
    gate_mine, up_mine, down_mine = gate_weight[0], up_weight[0], down_weight[0]
    gate_other = other_core(after(gate_mine, theirs))
    up_other = other_core(after(up_mine, theirs))
    gates_up = (gate_mine, gate_other, up_mine, up_other)

    experts_count = 2 * n_ep
    capacity = max(2, 3 * tokens // experts_count)
    copies = n_x // 2
    n_cells = experts_count * capacity
    experts = route_experts[0]
    cells = ((experts % 2) * n_ep + experts // 2) * capacity + route_slots[0]
    row_cells = cells.T

    def dispatch(sent):
        part = sent.shape[1]
        sent = jnp.broadcast_to(
            sent.reshape(2, 1, n_ep, capacity, part), (2, copies, n_ep, capacity, part)
        )
        return exchange(sent).reshape(-1, part)

    quarter = width // 4
    cuts = ((0, quarter), (quarter, width - quarter))
    terms, received = [], []
    for start, size in cuts:
        own, *sends = project(mine, theirs, out_weight, out_other, start, size)
        mine = after(mine, own)
        if received:
            sends = after(sends, received[0])
        terms.append(own)
        received.append(
            [
                lax.ppermute(value, "x", [(x, (x - dx) % n_x) for x in range(n_x)])
                for dx, value in enumerate(sends, 1)
            ]
        )
    residual, stat = residual_part(latent, modulation, terms[0], received[0], [], 0)
    raw = pack_raw(row_cells, n_cells, residual)
    raw = dispatch(after(raw, terms[1]))
    own = after(terms[1], raw)
    rest, stats = residual_part(latent, modulation, own, received[1], [stat], quarter)
    residuals = [residual, rest]
    down_other = other_core(after(down_mine, stats))
    downs = (down_mine, down_other)

    sent = pack(modulation, row_cells, n_cells, stats, rest, quarter, 0, 2 * quarter, True)
    rows = dispatch(after(sent, raw))
    sent = pack(
        modulation, row_cells, n_cells, after(stats, sent), rest, quarter, 2 * quarter, quarter, False
    )
    last_rows = dispatch(after(sent, rows))
    sums = ffn_first(modulation, raw, rows, gates_up)
    acts = ffn_last(last_rows, gates_up, sums)

    out, token = None, acts
    for residual, (start, size) in zip(residuals, cuts):
        value = after(ffn_out(acts, downs, start, size), token)
        token = exchange(value)
        back = token.reshape(2, copies, n_ep * capacity, size)
        out = combine(residual, modulation, cells, route_gates[0], back, start, out)
    return out[None]


def solution(mesh):
    n_sp, n_ep = mesh.devices.shape
    chips = Mesh(mesh.devices.reshape(n_sp // 2, 2, n_ep), ("x", "core", "ep"))
    sp = ("x", "core")
    return jax.shard_map(
        local,
        mesh=chips,
        in_specs=(
            P("ep", sp, None),
            P("ep", sp, None, None),
            P(sp, None),
            P(),
            P("ep", sp, None),
            P("ep", sp, None),
            P("ep", sp, None),
            P("ep", None, sp),
            P("ep", None, sp),
            P("ep", sp, None),
        ),
        out_specs=P("ep", sp, None),
        check_vma=False,
    )
```

time: 497 us -> 282 us (0.57)
  blocking collectives: 186 us -> 0 us
  Pallas kernels: 0 us -> 73.9 us
  matrix products: 51.7 us -> 0 us
  waiting for transfers between devices: 187 us -> 156 us
  starting transfers between devices: 3.97 us -> 33.1 us
  local copies, waits for them, and re-layouts: 36.8 us -> 17.8 us
  other arithmetic: 17.5 us -> 0.07 us
  between operations: 13.5 us -> 0.19 us
    all_to_all x2 -> x0, blocking collectives: 186 us -> none  [the longest x1 144 us: local(): lax.all_to_all(spread, ('sp', 'ep'), split_axis=0, concat_axis=0, tiled=T...]
    pallas_call x0 -> x15, Pallas kernels: none -> 73.9 us  [the longest x1 16.8 us: ffn_first(): pl.pallas_call(ffn_first_kernel, grid=(units // tile,), out_shape=[jax.Sh...]
    dot_general x6 -> x0, matrix products: 51.7 us -> none  [the longest x1 22.4 us: feed_forward(): jnp.dot(activation, down_shard, preferred_element_type=jnp.float32)]
    reduce_scatter x1 -> x0, waiting for transfers between devices: 44.9 us -> none  [local(): lax.psum_scatter(jnp.dot(flat_heads, out_weight, preferred_element_type=j...]
    ppermute x0 -> x10, waiting for transfers between devices: none -> 36.4 us  [the longest x3 27.8 us: local(): piece = lax.ppermute(piece, ('x', 'core'), shift(dx, dc))]
    all_to_all x1 -> x5, waiting for transfers between devices: 142 us -> 120 us  [exchange(): lax.all_to_all(value, ('x', 'ep'), split_axis=0, concat_axis=0, tiled=True)]
    all_to_all x1 -> x5, starting transfers between devices: 3.97 us -> 24.9 us  [exchange(): lax.all_to_all(value, ('x', 'ep'), split_axis=0, concat_axis=0, tiled=True)]
    gather x2 -> x0, local copies, waits for them, and re-layouts: 14.3 us -> none  [local(): jnp.take(per_expert, cell_index.reshape(-1), axis=0)]
  transfers between devices with their start and end apart: 2 -> 15, of which waited for: 2 -> 10; matrix products, arithmetic and copies ran while one was open for 0% -> 0% of each run, Pallas kernels for 0% -> 22%
where the time goes in v2:
time: 282 us; the launch traced here: 281 us
  waiting for transfers between devices  156 us (55%)
  Pallas kernels  73.9 us (26%)
  starting transfers between devices  33.1 us (12%)
  local copies, waits for them, and re-layouts  17.8 us (6%)
    all_to_all x5, waiting for transfers between devices, exchange(): lax.all_to_all(value, ('x', 'ep'), split_axis=0, concat_axis=0, tiled=True)  120 us
    ppermute x3, waiting for transfers between devices, local(): piece = lax.ppermute(piece, ('x', 'core'), shift(dx, dc))  27.8 us
    all_to_all x5, starting transfers between devices, exchange(): lax.all_to_all(value, ('x', 'ep'), split_axis=0, concat_axis=0, tiled=True)  24.9 us
    pallas_call x1, Pallas kernels, ffn_first(): pl.pallas_call(ffn_first_kernel, grid=(units // tile,), out_shape=[jax.Sh...  16.8 us
    unnamed x41, local copies, waits for them, and re-layouts  15.5 us
    pallas_call x2, Pallas kernels, ffn_out(): pl.pallas_call(ffn_out_kernel, grid=(size // tile,), out_shape=jax.ShapeD...  15.3 us
    pallas_call x1, Pallas kernels, ffn_last(): pl.pallas_call(ffn_last_kernel, grid=(units // tile,), out_shape=[jax.Sha...  9.5 us
    pallas_call x1, Pallas kernels, attend_last(): pl.pallas_call(attend_last_kernel, out_shape=(out, out), in_specs=[VMEM]...  8.17 us
  transfers between devices with their start and end apart: 15, of which 10 were waited for; matrix products, arithmetic and copies ran while one was open for 0% of the time, Pallas kernels for 22%

profile of v2, /device:TPU:0, one launch (start us, length us, event | category | flops | bytes accessed | tf_op | source)
XLA Modules:
  0.0 281.2 jit_solution(17972028496552732727)
XLA Ops:
  0.0 2.3 dynamic-slice_bitcast_fusion
  2.9 2.9 %collective-permute-start.1 = (bf16[3,128,1024]{2,1,0:T(8,128)(2,1)S(1)}, bf16[3,128,1024]{2,1,0:T(8,128)(2,1)S(1)}, u32[]{:S(2)}, u32[]{:S(2)}) collective-permute-start(bf16[3,128,1024]{2,1,0:T(8,128)(2,1)S(1)} %get-tuple-element.72), channel_id=1, source_target_pairs={{0,16},{8,24},{16,0},{24,8},{1,17},{9,25},{17,1},{25,9},{2,18},{10... | collective-permute-start | bytes 2359304 | tf_op jit(solution)/shard_map/ppermute | solution.py:415
  5.8 4.5 %collective-permute-done.refs_1_ = bf16[3,128,1024]{2,1,0:T(8,128)(2,1)S(1)} collective-permute-done((bf16[3,128,1024]{2,1,0:T(8,128)(2,1)S(1)}, bf16[3,128,1024]{2,1,0:T(8,128)(2,1)S(1)}, u32[]{:S(2)}, u32[]{:S(2)}) %collective-permute-start) | collective-permute-done | bytes 786464 | tf_op jit(solution)/shard_map/ppermute | solution.py:415
  10.3 13.8 %collective-permute-done.1.refs_2_ = bf16[3,128,1024]{2,1,0:T(8,128)(2,1)S(1)} collective-permute-done((bf16[3,128,1024]{2,1,0:T(8,128)(2,1)S(1)}, bf16[3,128,1024]{2,1,0:T(8,128)(2,1)S(1)}, u32[]{:S(2)}, u32[]{:S(2)}) %collective-permute-start.1) | collective-permute-done | bytes 786464 | tf_op jit(solution)/shard_map/ppermute | solution.py:415
  24.2 6.2 %shard_map.100 = (f32[3,128,1024]{2,1,0:T(8,128)S(1)}, f32[3,128,8]{2,1,0:T(8,128)S(1)}, f32[3,128,8]{2,1,0:T(8,128)S(1)}) custom-call(bf16[3,128,1024]{2,1,0:T(8,128)(2,1)S(1)} %get-tuple-element.71.refs_0_, bf16[3,128,1024]{2,1,0:T(8,128)(2,1)S(1)} %collective-permute-done.refs_1_, bf16[3,128,1024]{2,1,0:T(8,128)(2,1)S(1)} %collective-permute-done.1.refs_2_), custom_call_target="tpu_custom_call" | custom-call | flops 1024 | bytes 1024 | tf_op jit(solution)/shard_map/pallas_call | solution.py:62
  30.4 9.5 %collective-permute-done.2.refs_3_ = bf16[3,128,1024]{2,1,0:T(8,128)(2,1)S(1)} collective-permute-done((bf16[3,128,1024]{2,1,0:T(8,128)(2,1)S(1)}, bf16[3,128,1024]{2,1,0:T(8,128)(2,1)S(1)}, u32[]{:S(2)}, u32[]{:S(2)}) %collective-permute-start.2) | collective-permute-done | bytes 786464 | tf_op jit(solution)/shard_map/ppermute | solution.py:415
  39.9 8.2 %shard_map.101 = (bf16[2,128,1024]{2,1,0:T(8,128)(2,1)S(1)}, bf16[2,128,1024]{2,1,0:T(8,128)(2,1)S(1)}) custom-call(bf16[3,128,1024]{2,1,0:T(8,128)(2,1)S(1)} %get-tuple-element.71.refs_0_, bf16[3,128,1024]{2,1,0:T(8,128)(2,1)S(1)} %collective-permute-done.refs_1_, bf16[3,128,1024]{2,1,0:T(8,128)(2,1)S(1)} %collective-permute-done.1.refs_2_, ...), custom_call_target="tpu_custom_call" | custom-call | flops 1024 | bytes 1024 | tf_op jit(solution)/shard_map/pallas_call | solution.py:103
  48.5 1.5 collective-permute-done.3.theirs_ref
  50.1 2.5 shard_map.102
  54.4 1.8 collective-permute-start.5
  56.5 3.4 %copy-done.1 = bf16[1024,4096]{1,0:T(8,128)(2,1)S(1)} copy-done((bf16[1024,4096]{1,0:T(8,128)(2,1)S(1)}, bf16[1024,4096]{1,0:T(8,128)(2,1)}, u32[]{:S(2)}) %copy-start.1) | copy-done | bytes 8388632
  59.9 3.4 %copy-done.3 = bf16[1024,4096]{1,0:T(8,128)(2,1)S(1)} copy-done((bf16[1024,4096]{1,0:T(8,128)(2,1)S(1)}, bf16[1024,4096]{1,0:T(8,128)(2,1)}, u32[]{:S(2)}) %copy-start.3) | copy-done | bytes 8388632
  64.4 4.7 %shard_map.103 = (f32[128,3072]{1,0:T(8,128)S(1)}, bf16[128,3072]{1,0:T(8,128)(2,1)S(1)}) custom-call(bf16[2,128,1024]{2,1,0:T(8,128)(2,1)S(1)} %get-tuple-element.44.mine_ref, bf16[2,128,1024]{2,1,0:T(8,128)(2,1)S(1)} %copy-done.8, bf16[1024,4096]{1,0:T(8,128)(2,1)S(1)} %copy-done.1, bf16[1024,4096]{1,0:T(8,128)(2,1)S(1)} %copy-done.3), custom_call_target="tpu_custom_call" | custom-call | flops 1024 | bytes 1024 | tf_op jit(solution)/shard_map/pallas_call | solution.py:129
  71.8 6.2 %all-to-all-start = ((bf16[16,24,1024]{2,1,0:T(8,128)(2,1)}), bf16[16,24,1024]{2,1,0:T(8,128)(2,1)}, u32[]{:S(2)}, u32[]{:S(2)}) async-start(bf16[16,24,1024]{2,1,0:T(8,128)(2,1)} %bitcast.14), calls=%async_computation | async-start | bytes 1572864 | tf_op jit(solution)/shard_map/all_to_all | solution.py:400
  78.0 1.9 collective-permute-start.6
  80.4 18.3 %all-to-all-done = bf16[16,24,1024]{2,1,0:T(8,128)(2,1)} async-done(((bf16[16,24,1024]{2,1,0:T(8,128)(2,1)}), bf16[16,24,1024]{2,1,0:T(8,128)(2,1)}, u32[]{:S(2)}, u32[]{:S(2)}) %all-to-all-start) | async-done | bytes 786464 | tf_op jit(solution)/shard_map/all_to_all | solution.py:400
  98.7 7.1 %collective-permute-done.6.refs_0_ = bf16[128,3072]{1,0:T(8,128)(2,1)S(1)} collective-permute-done((bf16[128,3072]{1,0:T(8,128)(2,1)S(1)}, bf16[128,3072]{1,0:T(8,128)(2,1)S(1)}, u32[]{:S(2)}, u32[]{:S(2)}) %collective-permute-start.6) | collective-permute-done | bytes 786464 | tf_op jit(solution)/shard_map/ppermute | solution.py:452
  106.6 1.4 copy-done.10
  109.9 1.9 shard_map.107
  111.8 5.6 %all-to-all-start.1 = ((bf16[16,24,2176]{2,1,0:T(8,128)(2,1)}), bf16[16,24,2176]{2,1,0:T(8,128)(2,1)}, u32[]{:S(2)}, u32[]{:S(2)}) async-start(bf16[16,24,2176]{2,1,0:T(8,128)(2,1)} %bitcast.17), calls=%async_computation.1 | async-start | bytes 3342336 | tf_op jit(solution)/shard_map/all_to_all | solution.py:400
  118.7 37.7 %all-to-all-done.1 = bf16[16,24,2176]{2,1,0:T(8,128)(2,1)} async-done(((bf16[16,24,2176]{2,1,0:T(8,128)(2,1)}), bf16[16,24,2176]{2,1,0:T(8,128)(2,1)}, u32[]{:S(2)}, u32[]{:S(2)}) %all-to-all-start.1) | async-done | bytes 1671200 | tf_op jit(solution)/shard_map/all_to_all | solution.py:400
  156.4 4.9 %all-to-all-start.2 = ((bf16[16,24,1024]{2,1,0:T(8,128)(2,1)}), bf16[16,24,1024]{2,1,0:T(8,128)(2,1)S(1)}, u32[]{:S(2)}, u32[]{:S(2)}) async-start(bf16[16,24,1024]{2,1,0:T(8,128)(2,1)} %bitcast.19), calls=%async_computation.2 | async-start | bytes 1572864 | tf_op jit(solution)/shard_map/all_to_all | solution.py:400
  161.4 16.8 %shard_map.109 = (f32[384,1024]{1,0:T(8,128)}, f32[384,1024]{1,0:T(8,128)}, f32[384,1024]{1,0:T(8,128)}, f32[384,1024]{1,0:T(8,128)}) custom-call(f32[4,4096]{1,0:T(4,128)} %mod_ref.13, bf16[384,1024]{1,0:T(8,128)(2,1)} %bitcast.15.raw_ref, bf16[384,2176]{1,0:T(8,128)(2,1)} %bitcast.18.rows_ref, bf16[4096,1024]{1,0:T(8,128)(2,1)} %bitcast.62, ...), custom_call_target="tpu_custom_call" | custom-call | flops 1024 | bytes 1024 | tf_op jit(solution)/shard_map/pallas_call | solution.py:265
  178.2 3.8 %all-to-all-done.2 = bf16[16,24,1024]{2,1,0:T(8,128)(2,1)S(1)} async-done(((bf16[16,24,1024]{2,1,0:T(8,128)(2,1)}), bf16[16,24,1024]{2,1,0:T(8,128)(2,1)S(1)}, u32[]{:S(2)}, u32[]{:S(2)}) %all-to-all-start.2) | async-done | bytes 786464 | tf_op jit(solution)/shard_map/all_to_all | solution.py:400
  182.8 9.5 %shard_map.110 = (bf16[384,1024]{1,0:T(8,128)(2,1)}, bf16[384,1024]{1,0:T(8,128)(2,1)}) custom-call(bf16[384,1024]{1,0:T(8,128)(2,1)} %bitcast.72, bf16[4096,1024]{1,0:T(8,128)(2,1)} %bitcast.63, bf16[4096,1024]{1,0:T(8,128)(2,1)} %collective-permute-done.7.refs_1_, bf16[4096,1024]{1,0:T(8,128)(2,1)} %bitcast.66, ...), custom_call_target="tpu_custom_call" | custom-call | flops 1024 | bytes 1024 | tf_op jit(solution)/shard_map/pallas_call | solution.py:297
  192.3 4.8 %shard_map.112 = bf16[384,1024]{1,0:T(8,128)(2,1)} custom-call(bf16[384,1024]{1,0:T(8,128)(2,1)} %get-tuple-element.64.mine_ref, bf16[384,1024]{1,0:T(8,128)(2,1)} %get-tuple-element.65.theirs_ref, bf16[1024,4096]{1,0:T(8,128)(2,1)} %bitcast.68, bf16[1024,4096]{1,0:T(8,128)(2,1)} %collective-permute-done.9.theirs_w), custom_call_target="tpu_custom_call" | custom-call | flops 1024 | bytes 1024 | tf_op jit(solution)/shard_map/pallas_call | solution.py:319
  197.1 3.6 %all-to-all-start.3 = ((bf16[16,24,1024]{2,1,0:T(8,128)(2,1)}), bf16[16,24,1024]{2,1,0:T(8,128)(2,1)S(1)}, u32[]{:S(2)}, u32[]{:S(2)}) async-start(bf16[16,24,1024]{2,1,0:T(8,128)(2,1)} %bitcast.71), calls=%async_computation.3 | async-start | bytes 1572864 | tf_op jit(solution)/shard_map/all_to_all | solution.py:400
  200.7 10.5 %shard_map.111 = bf16[384,3072]{1,0:T(8,128)(2,1)} custom-call(bf16[384,1024]{1,0:T(8,128)(2,1)} %get-tuple-element.64.mine_ref, bf16[384,1024]{1,0:T(8,128)(2,1)} %get-tuple-element.65.theirs_ref, bf16[1024,4096]{1,0:T(8,128)(2,1)} %bitcast.69, bf16[1024,4096]{1,0:T(8,128)(2,1)} %collective-permute-done.9.theirs_w), custom_call_target="tpu_custom_call" | custom-call | flops 1024 | bytes 1024 | tf_op jit(solution)/shard_map/pallas_call | solution.py:319
  211.2 9.8 %all-to-all-done.3 = bf16[16,24,1024]{2,1,0:T(8,128)(2,1)S(1)} async-done(((bf16[16,24,1024]{2,1,0:T(8,128)(2,1)}), bf16[16,24,1024]{2,1,0:T(8,128)(2,1)S(1)}, u32[]{:S(2)}, u32[]{:S(2)}) %all-to-all-start.3) | async-done | bytes 786464 | tf_op jit(solution)/shard_map/all_to_all | solution.py:400
  221.0 4.6 %all-to-all-start.4 = ((bf16[16,24,3072]{2,1,0:T(8,128)(2,1)}), bf16[16,24,3072]{2,1,0:T(8,128)(2,1)}, u32[]{:S(2)}, u32[]{:S(2)}) async-start(bf16[16,24,3072]{2,1,0:T(8,128)(2,1)} %bitcast.70), calls=%async_computation.4 | async-start | bytes 4718592 | tf_op jit(solution)/shard_map/all_to_all | solution.py:400
  226.9 50.1 %all-to-all-done.4 = bf16[16,24,3072]{2,1,0:T(8,128)(2,1)} async-done(((bf16[16,24,3072]{2,1,0:T(8,128)(2,1)}), bf16[16,24,3072]{2,1,0:T(8,128)(2,1)}, u32[]{:S(2)}, u32[]{:S(2)}) %all-to-all-start.4) | async-done | bytes 2359328 | tf_op jit(solution)/shard_map/all_to_all | solution.py:400
  277.1 4.1 %shard_map.114 = bf16[128,4096]{1,0:T(8,128)(2,1)} custom-call(f32[128,3072]{1,0:T(8,128)S(1)} %get-tuple-element.53.part_ref.residual_ref, f32[4,4096]{1,0:T(4,128)S(1)} %copy-done.6, s32[128,2]{1,0:T(8,128)S(1)} %fusion.3.cells_ref, f32[128,2]{1,0:T(8,128)S(1)} %bitcast.60, ...), custom_call_target="tpu_custom_call", output_to_operand_aliasing={{}: (5, {})} | custom-call | flops 1024 | bytes 1024 | tf_op jit(solution)/shard_map/pallas_call | solution.py:354
  (57 shorter events, 13.7 us)
Async XLA Ops:
  0.0 50.1 %copy-start = (bf16[1024,4096]{1,0:T(8,128)(2,1)S(1)}, bf16[1024,4096]{1,0:T(8,128)(2,1)}, u32[]{:S(2)}) copy-start(bf16[1024,4096]{1,0:T(8,128)(2,1)} %mine_w.3) | copy-start | bytes 25165828
  2.3 47.7 %collective-permute-start.4 = (bf16[1024,4096]{1,0:T(8,128)(2,1)}, bf16[1024,4096]{1,0:T(8,128)(2,1)S(1)}, u32[]{:S(2)}, u32[]{:S(2)}) collective-permute-start(bf16[1024,4096]{1,0:T(8,128)(2,1)} %mine_w.3), channel_id=1, source_target_pairs={{0,8},{8,0},{1,9},{9,1},{2,10},{10,2},{3,11},{11,3},{4,12},{12,4},... | collective-permute-start | bytes 25165832 | tf_op jit(solution)/shard_map/ppermute | solution.py:395
  2.8 7.5 %collective-permute-start = (bf16[3,128,1024]{2,1,0:T(8,128)(2,1)S(1)}, bf16[3,128,1024]{2,1,0:T(8,128)(2,1)S(1)}, u32[]{:S(2)}, u32[]{:S(2)}) collective-permute-start(bf16[3,128,1024]{2,1,0:T(8,128)(2,1)S(1)} %get-tuple-element.70), channel_id=1, source_target_pairs={{0,8},{8,0},{16,24},{24,16},{1,9},{9,1},{17,25},{25,17},{2,10},{10... | collective-permute-start | bytes 2359304 | tf_op jit(solution)/shard_map/ppermute | solution.py:415
  2.9 21.3 %collective-permute-start.1 = (bf16[3,128,1024]{2,1,0:T(8,128)(2,1)S(1)}, bf16[3,128,1024]{2,1,0:T(8,128)(2,1)S(1)}, u32[]{:S(2)}, u32[]{:S(2)}) collective-permute-start(bf16[3,128,1024]{2,1,0:T(8,128)(2,1)S(1)} %get-tuple-element.72), channel_id=1, source_target_pairs={{0,16},{8,24},{16,0},{24,8},{1,17},{9,25},{17,1},{25,9},{2,18},{10... | collective-permute-start | bytes 2359304 | tf_op jit(solution)/shard_map/ppermute | solution.py:415
  5.8 34.1 %collective-permute-start.2 = (bf16[3,128,1024]{2,1,0:T(8,128)(2,1)S(1)}, bf16[3,128,1024]{2,1,0:T(8,128)(2,1)S(1)}, u32[]{:S(2)}, u32[]{:S(2)}) collective-permute-start(bf16[3,128,1024]{2,1,0:T(8,128)(2,1)S(1)} %get-tuple-element.69), channel_id=1, source_target_pairs={{0,24},{8,16},{16,8},{24,0},{1,25},{9,17},{17,9},{25,1},{2,26},{10... | collective-permute-start | bytes 2359304 | tf_op jit(solution)/shard_map/ppermute | solution.py:415
  48.1 2.0 collective-permute-start.3
  50.1 2.6 copy-start.7
  50.1 3.5 %copy-start.2 = (bf16[1024,4096]{1,0:T(8,128)(2,1)}, bf16[1024,4096]{1,0:T(8,128)(2,1)S(1)}, u32[]{:S(2)}) copy-start(bf16[1024,4096]{1,0:T(8,128)(2,1)S(1)} %collective-permute-done.4.theirs_w) | copy-start | bytes 25165828
  50.1 6.1 %copy-start.16 = (s32[1,128,2]{1,2,0:T(2,128)S(1)}, s32[1,128,2]{1,2,0:T(2,128)}, u32[]{:S(2)}) copy-start(s32[1,128,2]{1,2,0:T(2,128)} %param.15) | copy-start | bytes 3076
  50.1 6.2 %copy-start.17 = (s32[1,128,2]{1,2,0:T(2,128)S(1)}, s32[1,128,2]{1,2,0:T(2,128)}, u32[]{:S(2)}) copy-start(s32[1,128,2]{1,2,0:T(2,128)} %param.14) | copy-start | bytes 3076
  54.4 15.9 %collective-permute-start.5 = (bf16[128,1024]{1,0:T(8,128)(2,1)}, bf16[128,1024]{1,0:T(8,128)(2,1)S(1)}, u32[]{:S(2)}, u32[]{:S(2)}) collective-permute-start(bf16[128,1024]{1,0:T(8,128)(2,1)} %get-tuple-element.46), channel_id=1, source_target_pairs={{0,16},{16,0},{1,17},{17,1},{2,18},{18,2},{3,19},{19,3},{4,20},{20... | collective-permute-start | bytes 786440 | tf_op jit(solution)/shard_map/ppermute | solution.py:452
  56.5 3.4 %copy-start.1 = (bf16[1024,4096]{1,0:T(8,128)(2,1)S(1)}, bf16[1024,4096]{1,0:T(8,128)(2,1)}, u32[]{:S(2)}) copy-start(bf16[1024,4096]{1,0:T(8,128)(2,1)} %mine_w.3) | copy-start | bytes 25165828
  59.9 3.4 %copy-start.3 = (bf16[1024,4096]{1,0:T(8,128)(2,1)S(1)}, bf16[1024,4096]{1,0:T(8,128)(2,1)}, u32[]{:S(2)}) copy-start(bf16[1024,4096]{1,0:T(8,128)(2,1)} %copy-done.2) | copy-start | bytes 25165828
  63.3 1.0 copy-start.8
  64.4 5.9 %copy-start.4 = (bf16[1,128,4096]{2,1,0:T(8,128)(2,1)S(1)}, bf16[1,128,4096]{2,1,0:T(8,128)(2,1)}, u32[]{:S(2)}) copy-start(bf16[1,128,4096]{2,1,0:T(8,128)(2,1)} %param.10) | copy-start | bytes 3145732
  64.4 5.9 %copy-start.5 = (f32[4,4096]{1,0:T(4,128)S(1)}, f32[4,4096]{1,0:T(4,128)}, u32[]{:S(2)}) copy-start(f32[4,4096]{1,0:T(4,128)} %mod_ref.13) | copy-start | bytes 196612
  64.4 5.9 %copy-start.14 = (f32[128,1024]{1,0:T(8,128)S(1)}, f32[128,1024]{1,0:T(8,128)}, u32[]{:S(2)}) copy-start(f32[128,1024]{1,0:T(8,128)} %copy-done.13) | copy-start | bytes 1572868
  69.1 1.2 copy-start.9
  71.8 26.9 %all-to-all-start = ((bf16[16,24,1024]{2,1,0:T(8,128)(2,1)}), bf16[16,24,1024]{2,1,0:T(8,128)(2,1)}, u32[]{:S(2)}, u32[]{:S(2)}) async-start(bf16[16,24,1024]{2,1,0:T(8,128)(2,1)} %bitcast.14), calls=%async_computation | async-start | bytes 1572864 | tf_op jit(solution)/shard_map/all_to_all | solution.py:400
  78.0 27.7 %collective-permute-start.6 = (bf16[128,3072]{1,0:T(8,128)(2,1)S(1)}, bf16[128,3072]{1,0:T(8,128)(2,1)S(1)}, u32[]{:S(2)}, u32[]{:S(2)}) collective-permute-start(bf16[128,3072]{1,0:T(8,128)(2,1)S(1)} %get-tuple-element.51), channel_id=1, source_target_pairs={{0,16},{16,0},{1,17},{17,1},{2,18},{18,2},{3,19},{19,3},{4,20},{20... | collective-permute-start | bytes 2359304 | tf_op jit(solution)/shard_map/ppermute | solution.py:452
  79.9 81.5 %collective-permute-start.7 = (bf16[4096,1024]{1,0:T(8,128)(2,1)}, bf16[4096,1024]{1,0:T(8,128)(2,1)}, u32[]{:S(2)}, u32[]{:S(2)}) collective-permute-start(bf16[4096,1024]{1,0:T(8,128)(2,1)} %bitcast.61), channel_id=1, source_target_pairs={{0,8},{8,0},{1,9},{9,1},{2,10},{10,2},{3,11},{11,3},{4,12},{12,4},... | collective-permute-start | bytes 25165832 | tf_op jit(solution)/shard_map/ppermute | solution.py:395
  79.9 81.5 %collective-permute-start.8 = (bf16[4096,1024]{1,0:T(8,128)(2,1)}, bf16[4096,1024]{1,0:T(8,128)(2,1)}, u32[]{:S(2)}, u32[]{:S(2)}) collective-permute-start(bf16[4096,1024]{1,0:T(8,128)(2,1)} %bitcast.64), channel_id=1, source_target_pairs={{0,8},{8,0},{1,9},{9,1},{2,10},{10,2},{3,11},{11,3},{4,12},{12,4},... | collective-permute-start | bytes 25165832 | tf_op jit(solution)/shard_map/ppermute | solution.py:395
  105.8 0.9 copy-start.11
  106.6 1.4 copy-start.10
  108.0 1.1 copy-start.12
  109.8 82.5 %collective-permute-start.9 = (bf16[1024,4096]{1,0:T(8,128)(2,1)}, bf16[1024,4096]{1,0:T(8,128)(2,1)}, u32[]{:S(2)}, u32[]{:S(2)}) collective-permute-start(bf16[1024,4096]{1,0:T(8,128)(2,1)} %bitcast.67), channel_id=1, source_target_pairs={{0,8},{8,0},{1,9},{9,1},{2,10},{10,2},{3,11},{11,3},{4,12},{12,4},... | collective-permute-start | bytes 25165832 | tf_op jit(solution)/shard_map/ppermute | solution.py:395
  111.8 44.7 %all-to-all-start.1 = ((bf16[16,24,2176]{2,1,0:T(8,128)(2,1)}), bf16[16,24,2176]{2,1,0:T(8,128)(2,1)}, u32[]{:S(2)}, u32[]{:S(2)}) async-start(bf16[16,24,2176]{2,1,0:T(8,128)(2,1)} %bitcast.17), calls=%async_computation.1 | async-start | bytes 3342336 | tf_op jit(solution)/shard_map/all_to_all | solution.py:400
  156.4 25.5 %all-to-all-start.2 = ((bf16[16,24,1024]{2,1,0:T(8,128)(2,1)}), bf16[16,24,1024]{2,1,0:T(8,128)(2,1)S(1)}, u32[]{:S(2)}, u32[]{:S(2)}) async-start(bf16[16,24,1024]{2,1,0:T(8,128)(2,1)} %bitcast.19), calls=%async_computation.2 | async-start | bytes 1572864 | tf_op jit(solution)/shard_map/all_to_all | solution.py:400
  197.1 23.9 %all-to-all-start.3 = ((bf16[16,24,1024]{2,1,0:T(8,128)(2,1)}), bf16[16,24,1024]{2,1,0:T(8,128)(2,1)S(1)}, u32[]{:S(2)}, u32[]{:S(2)}) async-start(bf16[16,24,1024]{2,1,0:T(8,128)(2,1)} %bitcast.71), calls=%async_computation.3 | async-start | bytes 1572864 | tf_op jit(solution)/shard_map/all_to_all | solution.py:400
  221.0 4.6 %copy-start.18 = (f32[1,128,2]{1,2,0:T(2,128)S(1)}, f32[1,128,2]{1,2,0:T(2,128)}, u32[]{:S(2)}) copy-start(f32[1,128,2]{1,2,0:T(2,128)} %param.16) | copy-start | bytes 3076
  221.0 4.7 %copy-start.6 = (f32[4,4096]{1,0:T(4,128)S(1)}, f32[4,4096]{1,0:T(4,128)}, u32[]{:S(2)}) copy-start(f32[4,4096]{1,0:T(4,128)} %mod_ref.13) | copy-start | bytes 196612
  221.0 56.0 %all-to-all-start.4 = ((bf16[16,24,3072]{2,1,0:T(8,128)(2,1)}), bf16[16,24,3072]{2,1,0:T(8,128)(2,1)}, u32[]{:S(2)}, u32[]{:S(2)}) async-start(bf16[16,24,3072]{2,1,0:T(8,128)(2,1)} %bitcast.70), calls=%async_computation.4 | async-start | bytes 4718592 | tf_op jit(solution)/shard_map/all_to_all | solution.py:400
  (2 other events, 1.7 us)

commit v3 on v2

v3 whole, which is shorter than its diff:
```python
import functools
import math

import jax
import jax.numpy as jnp
from jax import lax
from jax.experimental import pallas as pl
from jax.experimental.pallas import tpu as pltpu
from jax.sharding import Mesh, PartitionSpec as P

HD = 128
VMEM = pl.BlockSpec(memory_space=pltpu.VMEM)
LOW = pl.CostEstimate(flops=1024, bytes_accessed=1024, transcendentals=0)


def dot32(a, b):
    return jnp.dot(a, b, preferred_element_type=jnp.float32)


def grant(mebibytes):
    return pltpu.CompilerParams(vmem_limit_bytes=mebibytes * 1024 * 1024)


def after(value, token):
    return lax.optimization_barrier((value, token))[0]


def attention_kernel(n_blocks, *refs):
    blocks = refs[:n_blocks]
    keep_ref, give_ref = refs[n_blocks:]
    tokens = keep_ref.shape[1]
    factor = math.log2(math.e) / math.sqrt(HD)
    for head in range(keep_ref.shape[-1] // HD):
        cols = slice(head * HD, (head + 1) * HD)
        queries, key_rows, value_rows = (
            jnp.concatenate([block[i, :, cols] for block in blocks], axis=0) for i in range(3)
        )
        scores = lax.dot_general(
            queries, key_rows, (((1,), (1,)), ((), ())), preferred_element_type=jnp.float32
        )
        lifted = jnp.exp2((scores - jnp.max(scores, axis=-1, keepdims=True)) * factor)
        total = jnp.sum(lifted, axis=-1, keepdims=True)
        mixed = (dot32(lifted.astype(jnp.bfloat16), value_rows) / total).astype(jnp.bfloat16)
        for i in range(n_blocks):
            out_ref = give_ref if i % 2 else keep_ref
            out_ref[i // 2, :, cols] = mixed[i * tokens : (i + 1) * tokens]


def attend(blocks):
    _, tokens, width = blocks[0].shape
    count = len(blocks)
    out = jax.ShapeDtypeStruct((count // 2, tokens, width), jnp.bfloat16)
    return pl.pallas_call(
        functools.partial(attention_kernel, count),
        out_shape=(out, out),
        in_specs=[VMEM] * count,
        out_specs=(VMEM, VMEM),
        compiler_params=grant(28),
        cost_estimate=LOW,
    )(*blocks)


def project_kernel(mine_ref, theirs_ref, mine_w, theirs_w, *refs):
    n_x, tokens, width = mine_ref.shape
    mine = mine_ref[...].reshape(n_x * tokens, width)
    theirs = theirs_ref[...].reshape(n_x * tokens, width)
    total = dot32(mine, mine_w[...]) + dot32(theirs, theirs_w[...])

    def write(outs):
        outs[0][...] = total[:tokens]
        for i, send_ref in enumerate(outs[1:], 1):
            send_ref[...] = total[i * tokens : (i + 1) * tokens].astype(jnp.bfloat16)

    half = pl.num_programs(0) // 2

    @pl.when(pl.program_id(0) < half)
    def _():
        write(refs[:n_x])

    @pl.when(pl.program_id(0) >= half)
    def _():
        write(refs[n_x:])


def project(mine, theirs, mine_w, theirs_w):
    n_x, tokens, depth = mine.shape
    width = mine_w.shape[1]
    tile = width // 4
    whole = pl.BlockSpec((n_x, tokens, depth), lambda n: (0, 0, 0))
    weight = pl.BlockSpec((depth, tile), lambda n: (0, n))
    out_shape, out_specs = [], []
    for place in (lambda n: (0, jnp.minimum(n, 1)), lambda n: (0, jnp.maximum(n - 2, 0))):
        for i in range(n_x):
            kind = jnp.bfloat16 if i else jnp.float32
            out_shape.append(jax.ShapeDtypeStruct((tokens, width // 2), kind))
            out_specs.append(pl.BlockSpec((tokens, tile), place))
    outs = pl.pallas_call(
        project_kernel,
        grid=(4,),
        out_shape=out_shape,
        in_specs=[whole, whole, weight, weight],
        out_specs=out_specs,
        compiler_params=grant(28),
        cost_estimate=LOW,
    )(mine, theirs, mine_w, theirs_w)
    return outs[:n_x], outs[n_x:]


def residual_kernel(start, n_recv, old_size, latent_ref, mod_ref, own_ref, *refs):
    recv_refs, old_refs = refs[:n_recv], refs[n_recv:-2]
    residual_ref, stats_ref = refs[-2:]
    size = own_ref.shape[1]
    cut = slice(start, start + size)
    projected = own_ref[...]
    for recv_ref in recv_refs:
        projected = projected + recv_ref[...].astype(jnp.float32)
    part = latent_ref[:, cut].astype(jnp.float32) + mod_ref[0:1, cut] * projected
    residual_ref[...] = part
    mean = jnp.mean(part, axis=-1, keepdims=True)
    centered = part - mean
    square = jnp.sum(centered * centered, axis=-1, keepdims=True)
    for old_ref in old_refs:
        old_mean, old_square = old_ref[:, 0:1], old_ref[:, 1:2]
        gap = old_mean - mean
        width = size + old_size
        mean = mean + gap * (old_size / width)
        square = square + old_square + gap * gap * (size * old_size / width)
        square = lax.rsqrt(square / width + 1e-06)
    stats_ref[:, 0:1] = mean
    stats_ref[:, 1:2] = square


def residual_part(latent, modulation, own, received, olds, start):
    tokens, size = own.shape
    return pl.pallas_call(
        functools.partial(residual_kernel, start, len(received), start),
        out_shape=[
            jax.ShapeDtypeStruct((tokens, size), jnp.float32),
            jax.ShapeDtypeStruct((tokens, 2), jnp.float32),
        ],
        in_specs=[VMEM] * (3 + len(received) + len(olds)),
        out_specs=[VMEM] * 2,
        compiler_params=grant(28),
        cost_estimate=LOW,
    )(latent, modulation, own, *received, *olds)


def pack_kernel(start, stop, mod_ref, cells_ref, stats_ref, *refs):
    *part_refs, sent_ref = refs
    tokens, size = part_refs[0].shape
    cells = lax.broadcasted_iota(jnp.int32, (sent_ref.shape[0], tokens), 0)
    one_hot = ((cells == cells_ref[0:1, :]) | (cells == cells_ref[1:2, :])).astype(jnp.bfloat16)
    for i, part_ref in enumerate(part_refs):
        low, high = max(start, i * size), min(stop, (i + 1) * size)
        if low < high:
            cut = slice(low, high)
            part = part_ref[:, low - i * size : high - i * size]
            normed = (part - stats_ref[:, 0:1]) * stats_ref[:, 1:2]
            moe_in = (normed * (1.0 + mod_ref[2:3, cut]) + mod_ref[1:2, cut]).astype(jnp.bfloat16)
            sent_ref[:, low - start : high - start] = dot32(one_hot, moe_in).astype(jnp.bfloat16)


def pack(modulation, cells, n_cells, stats, parts, start, stop):
    return pl.pallas_call(
        functools.partial(pack_kernel, start, stop),
        out_shape=jax.ShapeDtypeStruct((n_cells, stop - start), jnp.bfloat16),
        in_specs=[VMEM] * (3 + len(parts)),
        out_specs=VMEM,
        compiler_params=grant(28),
        cost_estimate=LOW,
    )(modulation, cells, stats, *parts)


def ffn_in_kernel(first, last, rows_ref, *refs):
    weights, refs = refs[:4], refs[4:]
    sums = [dot32(rows_ref[...], weight[...]) for weight in weights]
    if not first:
        olds, refs = refs[:4], refs[4:]
        sums = [total + old[...] for total, old in zip(sums, olds)]
    if last:
        for gate, up, out_ref in zip(sums[:2], sums[2:], refs):
            out_ref[...] = (gate / (1.0 + jnp.exp(-gate)) * up).astype(jnp.bfloat16)
    else:
        for total, out_ref in zip(sums, refs):
            out_ref[...] = total


def ffn_in(rows, weights, olds, start, last):
    count, size = rows.shape
    units = weights[0].shape[1]
    tile = min(256, units)
    block = start // size
    weight = pl.BlockSpec((size, tile), lambda n: (block, n))
    part = pl.BlockSpec((count, tile), lambda n: (0, n))
    outs = 2 if last else 4
    kind = jnp.bfloat16 if last else jnp.float32
    return pl.pallas_call(
        functools.partial(ffn_in_kernel, not olds, last),
        grid=(units // tile,),
        out_shape=[jax.ShapeDtypeStruct((count, units), kind)] * outs,
        in_specs=[pl.BlockSpec((count, size), lambda n: (0, 0))] + [weight] * 4 + [part] * len(olds),
        out_specs=[part] * outs,
        compiler_params=grant(57),
        cost_estimate=LOW,
    )(rows, *weights, *olds)


def ffn_out_kernel(mine_ref, theirs_ref, mine_w, theirs_w, out_ref):
    total = dot32(mine_ref[...], mine_w[...]) + dot32(theirs_ref[...], theirs_w[...])
    out_ref[...] = total.astype(jnp.bfloat16)


def ffn_out(acts, weights, start, size):
    count, units = acts[0].shape
    tile = min(1024, size)
    first = start // tile
    act = pl.BlockSpec((count, units), lambda n: (0, 0))
    weight = pl.BlockSpec((units, tile), lambda n: (0, first + n))
    return pl.pallas_call(
        ffn_out_kernel,
        grid=(size // tile,),
        out_shape=jax.ShapeDtypeStruct((count, size), jnp.bfloat16),
        in_specs=[act, act, weight, weight],
        out_specs=pl.BlockSpec((count, tile), lambda n: (0, n)),
        compiler_params=grant(57),
        cost_estimate=LOW,
    )(*acts, *weights)


def combine_kernel(first, turn, early_ref, late_ref, mod_ref, cells_ref, gates_ref, back_ref, *refs):
    out_ref = refs[-1]
    tokens, tile = out_ref.shape
    _, copies, half, _ = back_ref.shape
    cells = lax.broadcasted_iota(jnp.int32, (tokens, 2 * half), 1)
    one_hot = jnp.concatenate(
        [(cells == cells_ref[:, i : i + 1]).astype(jnp.bfloat16) for i in range(2)], axis=0
    )
    picked = 0.0
    for i in range(copies):
        picked = picked + dot32(one_hot, back_ref[:, i].reshape(2 * half, tile))
    combined = gates_ref[:, 0:1] * picked[:tokens] + gates_ref[:, 1:2] * picked[tokens:]
    is_early = first + pl.program_id(0) < turn
    residual = jnp.where(is_early, early_ref[...], late_ref[...])
    out_ref[...] = (residual + mod_ref[3:4, :] * combined).astype(jnp.bfloat16)


def combine(residuals, modulation, cells, gates, back, start, previous):
    tokens, part = residuals[0].shape
    width = modulation.shape[1]
    _, copies, half, size = back.shape
    tile = min(1024, size)
    first, turn = start // tile, part // tile
    small = pl.BlockSpec((tokens, 2), lambda n: (0, 0))
    more = [] if previous is None else [previous]
    return pl.pallas_call(
        functools.partial(combine_kernel, first, turn),
        grid=(size // tile,),
        out_shape=jax.ShapeDtypeStruct((tokens, width), jnp.bfloat16),
        in_specs=[
            pl.BlockSpec((tokens, tile), lambda n: (0, jnp.minimum(first + n, turn - 1))),
            pl.BlockSpec((tokens, tile), lambda n: (0, jnp.maximum(first + n - turn, 0))),
            pl.BlockSpec((4, tile), lambda n: (0, first + n)),
            small,
            small,
            pl.BlockSpec((2, copies, half, tile), lambda n: (0, 0, 0, n)),
        ]
        + [pl.BlockSpec(memory_space=pl.ANY)] * len(more),
        out_specs=pl.BlockSpec((tokens, tile), lambda n: (0, first + n)),
        input_output_aliases={6: 0} if more else {},
        compiler_params=grant(28),
        cost_estimate=LOW,
    )(*residuals, modulation, cells, gates, back, *more)


def local(
    latent,
    attention_in,
    out_weight,
    modulation,
    route_experts,
    route_slots,
    route_gates,
    gate_weight,
    up_weight,
    down_weight,
):
    n_x = lax.axis_size("x")
    n_ep = lax.axis_size("ep")
    tokens = latent.shape[1]
    width = latent.shape[2]
    group_width = out_weight.shape[0]
    my_x = lax.axis_index("x")
    my_core = lax.axis_index("core")
    latent = latent[0]

    def other_core(value):
        return lax.ppermute(value, "core", [(0, 1), (1, 0)])

    def exchange(value):
        part = value.shape[-1]
        value = value.reshape(n_x * n_ep, -1, part)
        return lax.all_to_all(value, ("x", "ep"), split_axis=0, concat_axis=0, tiled=True)

    def shift(dx, dc):
        return [
            (2 * x + c, 2 * ((x + dx) % n_x) + (c ^ dc)) for x in range(n_x) for c in range(2)
        ]

    packed = jnp.transpose(attention_in[0], (1, 0, 2))
    pieces, blocks = [], []
    for dx in range(n_x):
        for dc in range(2):
            group = 2 * ((my_x + dx) % n_x) + (my_core ^ dc)
            piece = lax.dynamic_slice_in_dim(packed, group * group_width, group_width, axis=2)
            pieces.append(piece)
            if dx or dc:
                piece = lax.ppermute(piece, ("x", "core"), shift(dx, dc))
            blocks.append(piece)

    out_other = other_core(after(out_weight, pieces[1]))
    mine, given = attend(blocks)
    theirs = other_core(given)
    gate_mine, up_mine, down_mine = gate_weight[0], up_weight[0], down_weight[0]
    gate_other = other_core(after(gate_mine, theirs))
    up_other = other_core(after(up_mine, theirs))
    gates_up = (gate_mine, gate_other, up_mine, up_other)

    experts_count = 2 * n_ep
    capacity = max(2, 3 * tokens // experts_count)
    copies = n_x // 2
    n_cells = experts_count * capacity
    experts = route_experts[0]
    cells = ((experts % 2) * n_ep + experts // 2) * capacity + route_slots[0]
    row_cells = cells.T

    def dispatch(sent):
        part = sent.shape[1]
        sent = jnp.broadcast_to(
            sent.reshape(2, 1, n_ep, capacity, part), (2, copies, n_ep, capacity, part)
        )
        return exchange(sent).reshape(-1, part)

    residuals, stats = [], []
    for i, (own, *sends) in enumerate(project(mine, theirs, out_weight, out_other)):
        received = [
            lax.ppermute(value, "x", [(x, (x - dx) % n_x) for x in range(n_x)])
            for dx, value in enumerate(sends, 1)
        ]
        residual, stat = residual_part(latent, modulation, own, received, stats, i * width // 2)
        residuals.append(residual)
        stats.append(stat)
    down_other = other_core(after(down_mine, stats[1]))
    downs = (down_mine, down_other)

    quarter = width // 4
    rows, sums, token = None, (), stats[1]
    for start, stop in ((0, width - quarter), (width - quarter, width)):
        row = after(stats[1], token)
        token = pack(modulation, row_cells, n_cells, row, residuals, start, stop)
        rows = dispatch(token if rows is None else after(token, rows))
        sums = ffn_in(rows, gates_up, sums, start, stop == width)
    acts = sums

    out, token = None, acts
    for start, size in ((0, quarter), (quarter, width - quarter)):
        value = after(ffn_out(acts, downs, start, size), token)
        token = exchange(value)
        back = token.reshape(2, copies, n_ep * capacity, size)
        out = combine(residuals, modulation, cells, route_gates[0], back, start, out)
    return out[None]


def solution(mesh):
    n_sp, n_ep = mesh.devices.shape
    chips = Mesh(mesh.devices.reshape(n_sp // 2, 2, n_ep), ("x", "core", "ep"))
    sp = ("x", "core")
    return jax.shard_map(
        local,
        mesh=chips,
        in_specs=(
            P("ep", sp, None),
            P("ep", sp, None, None),
            P(sp, None),
            P(),
            P("ep", sp, None),
            P("ep", sp, None),
            P("ep", sp, None),
            P("ep", None, sp),
            P("ep", None, sp),
            P("ep", sp, None),
        ),
        out_specs=P("ep", sp, None),
        check_vma=False,
    )
```

time: 282 us -> 267 us (0.947)
  waiting for transfers between devices: 156 us -> 174 us
  Pallas kernels: 73.9 us -> 59.7 us
  local copies, waits for them, and re-layouts: 17.8 us -> 5.14 us
  starting transfers between devices: 33.1 us -> 27.8 us
    ppermute x2, waiting for transfers between devices: 7.05 us -> 22.5 us  [local(): lax.ppermute(value, 'x', [(x, (x - dx) % n_x) for x in range(n_x)])]
    pallas_call x11 -> x8, Pallas kernels: 57.8 us -> 43.2 us  [the longest x2 25.9 us: ffn_in(): pl.pallas_call(functools.partial(ffn_in_kernel, not olds, last), grid=(un...]
    unnamed x41 -> x19, local copies, waits for them, and re-layouts: 15.5 us -> 2.75 us
    ppermute x3, waiting for transfers between devices: 27.8 us -> 34.1 us  [local(): piece = lax.ppermute(piece, ('x', 'core'), shift(dx, dc))]
    all_to_all x5 -> x4, waiting for transfers between devices: 120 us -> 116 us  [exchange(): lax.all_to_all(value, ('x', 'ep'), split_axis=0, concat_axis=0, tiled=True)]
    all_to_all x5 -> x4, starting transfers between devices: 24.9 us -> 21.2 us  [exchange(): lax.all_to_all(value, ('x', 'ep'), split_axis=0, concat_axis=0, tiled=True)]
  transfers between devices with their start and end apart: 15 -> 14, of which waited for: 10 -> 10; matrix products, arithmetic and copies ran while one was open for 0% -> 0% of each run, Pallas kernels for 22% -> 16%
where the time goes in v3:
time: 267 us
  waiting for transfers between devices  174 us (65%)
  Pallas kernels  59.7 us (22%)
  starting transfers between devices  27.8 us (10%)
  local copies, waits for them, and re-layouts  5.14 us (2%)
    all_to_all x4, waiting for transfers between devices, exchange(): lax.all_to_all(value, ('x', 'ep'), split_axis=0, concat_axis=0, tiled=True)  116 us
    ppermute x3, waiting for transfers between devices, local(): piece = lax.ppermute(piece, ('x', 'core'), shift(dx, dc))  34.1 us
    pallas_call x2, Pallas kernels, ffn_in(): pl.pallas_call(functools.partial(ffn_in_kernel, not olds, last), grid=(un...  25.9 us
    ppermute x2, waiting for transfers between devices, local(): lax.ppermute(value, 'x', [(x, (x - dx) % n_x) for x in range(n_x)])  22.5 us
    all_to_all x4, starting transfers between devices, exchange(): lax.all_to_all(value, ('x', 'ep'), split_axis=0, concat_axis=0, tiled=True)  21.2 us
    pallas_call x2, Pallas kernels, ffn_out(): pl.pallas_call(ffn_out_kernel, grid=(size // tile,), out_shape=jax.ShapeD...  15.7 us
    pallas_call x1, Pallas kernels, project(): pl.pallas_call(project_kernel, grid=(4,), out_shape=out_shape, in_specs=[...  6.65 us
    pallas_call x2, Pallas kernels, combine(): pl.pallas_call(functools.partial(combine_kernel, first, turn), grid=(size...  5.35 us
  transfers between devices with their start and end apart: 14, of which 10 were waited for; matrix products, arithmetic and copies ran while one was open for 0% of the time, Pallas kernels for 16%

profile of v3, /device:TPU:0, one launch (start us, length us, event | category | flops | bytes accessed | tf_op | source)
XLA Modules:
  0.0 266.8 jit_solution(12648934545419839298)
XLA Ops:
  0.0 2.3 dynamic-slice_bitcast_fusion
  2.3 0.5 collective-permute-start.4
  2.9 2.9 %collective-permute-start.1 = (bf16[3,128,1024]{2,1,0:T(8,128)(2,1)S(1)}, bf16[3,128,1024]{2,1,0:T(8,128)(2,1)S(1)}, u32[]{:S(2)}, u32[]{:S(2)}) collective-permute-start(bf16[3,128,1024]{2,1,0:T(8,128)(2,1)S(1)} %get-tuple-element.58), channel_id=1, source_target_pairs={{0,16},{8,24},{16,0},{24,8},{1,17},{9,25},{17,1},{25,9},{2,18},{10... | collective-permute-start | bytes 2359304 | tf_op jit(solution)/shard_map/ppermute | solution.py:317
  5.9 4.5 %collective-permute-done.refs_1_ = bf16[3,128,1024]{2,1,0:T(8,128)(2,1)S(1)} collective-permute-done((bf16[3,128,1024]{2,1,0:T(8,128)(2,1)S(1)}, bf16[3,128,1024]{2,1,0:T(8,128)(2,1)S(1)}, u32[]{:S(2)}, u32[]{:S(2)}) %collective-permute-start) | collective-permute-done | bytes 786464 | tf_op jit(solution)/shard_map/ppermute | solution.py:317
  10.4 13.8 %collective-permute-done.1.refs_2_ = bf16[3,128,1024]{2,1,0:T(8,128)(2,1)S(1)} collective-permute-done((bf16[3,128,1024]{2,1,0:T(8,128)(2,1)S(1)}, bf16[3,128,1024]{2,1,0:T(8,128)(2,1)S(1)}, u32[]{:S(2)}, u32[]{:S(2)}) %collective-permute-start.1) | collective-permute-done | bytes 786464 | tf_op jit(solution)/shard_map/ppermute | solution.py:317
  24.2 15.7 %collective-permute-done.2.refs_3_ = bf16[3,128,1024]{2,1,0:T(8,128)(2,1)S(1)} collective-permute-done((bf16[3,128,1024]{2,1,0:T(8,128)(2,1)S(1)}, bf16[3,128,1024]{2,1,0:T(8,128)(2,1)S(1)}, u32[]{:S(2)}, u32[]{:S(2)}) %collective-permute-start.2) | collective-permute-done | bytes 786464 | tf_op jit(solution)/shard_map/ppermute | solution.py:317
  39.9 3.0 %shard_map.100 = (bf16[2,128,1024]{2,1,0:T(8,128)(2,1)S(1)}, bf16[2,128,1024]{2,1,0:T(8,128)(2,1)S(1)}) custom-call(bf16[3,128,1024]{2,1,0:T(8,128)(2,1)S(1)} %get-tuple-element.57.refs_0_, bf16[3,128,1024]{2,1,0:T(8,128)(2,1)S(1)} %collective-permute-done.refs_1_, bf16[3,128,1024]{2,1,0:T(8,128)(2,1)S(1)} %collective-permute-done.1.refs_2_, ...), custom_call_target="tpu_custom_call" | custom-call | flops 1024 | bytes 1024 | tf_op jit(solution)/shard_map/pallas_call | solution.py:53
  42.9 0.4 collective-permute-start.3
  43.4 1.5 collective-permute-done.3.theirs_ref
  44.9 6.7 %shard_map.101 = (f32[128,2048]{1,0:T(8,128)S(1)}, bf16[128,2048]{1,0:T(8,128)(2,1)S(1)}, f32[128,2048]{1,0:T(8,128)S(1)}, bf16[128,2048]{1,0:T(8,128)(2,1)S(1)}) custom-call(bf16[2,128,1024]{2,1,0:T(8,128)(2,1)S(1)} %get-tuple-element.30.mine_ref, bf16[2,128,1024]{2,1,0:T(8,128)(2,1)S(1)} %collective-permute-done.3.theirs_ref, ...), custom_call_target="tpu_custom_call" | custom-call | flops 1024 | bytes 1024 | tf_op jit(solution)/shard_map/pallas_call | solution.py:97
  51.6 1.8 collective-permute-start.5
  53.7 0.5 collective-permute-start.8
  54.2 12.2 %collective-permute-done.5.refs_0_ = bf16[128,2048]{1,0:T(8,128)(2,1)S(1)} collective-permute-done((bf16[128,2048]{1,0:T(8,128)(2,1)S(1)}, bf16[128,2048]{1,0:T(8,128)(2,1)S(1)}, u32[]{:S(2)}, u32[]{:S(2)}) %collective-permute-start.5) | collective-permute-done | bytes 524320 | tf_op jit(solution)/shard_map/ppermute | solution.py:346
  66.8 10.3 %collective-permute-done.6.refs_0_ = bf16[128,2048]{1,0:T(8,128)(2,1)S(1)} collective-permute-done((bf16[128,2048]{1,0:T(8,128)(2,1)S(1)}, bf16[128,2048]{1,0:T(8,128)(2,1)S(1)}, u32[]{:S(2)}, u32[]{:S(2)}) %collective-permute-start.6) | collective-permute-done | bytes 524320 | tf_op jit(solution)/shard_map/ppermute | solution.py:346
  78.0 0.9 shard_map.104
  78.9 1.5 copy-done
  80.4 7.2 %all-to-all-start = ((bf16[16,24,3072]{2,1,0:T(8,128)(2,1)}), bf16[16,24,3072]{2,1,0:T(8,128)(2,1)}, u32[]{:S(2)}, u32[]{:S(2)}) async-start(bf16[16,24,3072]{2,1,0:T(8,128)(2,1)} %bitcast.53), calls=%async_computation | async-start | bytes 4718592 | tf_op jit(solution)/shard_map/all_to_all | solution.py:302
  87.6 1.4 shard_map.105
  88.9 51.5 %all-to-all-done = bf16[16,24,3072]{2,1,0:T(8,128)(2,1)} async-done(((bf16[16,24,3072]{2,1,0:T(8,128)(2,1)}), bf16[16,24,3072]{2,1,0:T(8,128)(2,1)}, u32[]{:S(2)}, u32[]{:S(2)}) %all-to-all-start) | async-done | bytes 2359328 | tf_op jit(solution)/shard_map/all_to_all | solution.py:302
  140.5 5.9 %all-to-all-start.1 = ((bf16[16,24,1024]{2,1,0:T(8,128)(2,1)}), bf16[16,24,1024]{2,1,0:T(8,128)(2,1)S(1)}, u32[]{:S(2)}, u32[]{:S(2)}) async-start(bf16[16,24,1024]{2,1,0:T(8,128)(2,1)} %bitcast.16), calls=%async_computation.1 | async-start | bytes 1572864 | tf_op jit(solution)/shard_map/all_to_all | solution.py:302
  146.4 16.4 %shard_map.106 = (f32[384,1024]{1,0:T(8,128)}, f32[384,1024]{1,0:T(8,128)}, f32[384,1024]{1,0:T(8,128)}, f32[384,1024]{1,0:T(8,128)}) custom-call(bf16[384,3072]{1,0:T(8,128)(2,1)} %bitcast.15.rows_ref, bf16[4096,1024]{1,0:T(8,128)(2,1)} %bitcast.18.refs_0_, bf16[4096,1024]{1,0:T(8,128)(2,1)} %collective-permute-done.7.refs_1_, ...), custom_call_target="tpu_custom_call" | custom-call | flops 1024 | bytes 1024 | tf_op jit(solution)/shard_map/pallas_call | solution.py:197
  162.8 4.2 %all-to-all-done.1 = bf16[16,24,1024]{2,1,0:T(8,128)(2,1)S(1)} async-done(((bf16[16,24,1024]{2,1,0:T(8,128)(2,1)}), bf16[16,24,1024]{2,1,0:T(8,128)(2,1)S(1)}, u32[]{:S(2)}, u32[]{:S(2)}) %all-to-all-start.1) | async-done | bytes 786464 | tf_op jit(solution)/shard_map/all_to_all | solution.py:302
  167.0 0.9 copy-done.4
  167.9 9.5 %shard_map.107 = (bf16[384,1024]{1,0:T(8,128)(2,1)}, bf16[384,1024]{1,0:T(8,128)(2,1)}) custom-call(bf16[384,1024]{1,0:T(8,128)(2,1)} %bitcast.62, bf16[4096,1024]{1,0:T(8,128)(2,1)} %bitcast.18.refs_0_, bf16[4096,1024]{1,0:T(8,128)(2,1)} %collective-permute-done.7.refs_1_, bf16[4096,1024]{1,0:T(8,128)(2,1)} %bitcast.19.refs_2_, ...), custom_call_target="tpu_custom_call" | custom-call | flops 1024 | bytes 1024 | tf_op jit(solution)/shard_map/pallas_call | solution.py:197
  177.4 5.4 %shard_map.109 = bf16[384,1024]{1,0:T(8,128)(2,1)} custom-call(bf16[384,1024]{1,0:T(8,128)(2,1)} %get-tuple-element.50.mine_ref, bf16[384,1024]{1,0:T(8,128)(2,1)} %get-tuple-element.51.theirs_ref, bf16[1024,4096]{1,0:T(8,128)(2,1)} %bitcast.20.mine_w, bf16[1024,4096]{1,0:T(8,128)(2,1)} %collective-permute-done.9.theirs_w), custom_call_target="tpu_custom_call" | custom-call | flops 1024 | bytes 1024 | tf_op jit(solution)/shard_map/pallas_call | solution.py:219
  182.8 3.6 %all-to-all-start.2 = ((bf16[16,24,1024]{2,1,0:T(8,128)(2,1)}), bf16[16,24,1024]{2,1,0:T(8,128)(2,1)S(1)}, u32[]{:S(2)}, u32[]{:S(2)}) async-start(bf16[16,24,1024]{2,1,0:T(8,128)(2,1)} %bitcast.61), calls=%async_computation.2 | async-start | bytes 1572864 | tf_op jit(solution)/shard_map/all_to_all | solution.py:302
  186.4 10.3 %shard_map.108 = bf16[384,3072]{1,0:T(8,128)(2,1)} custom-call(bf16[384,1024]{1,0:T(8,128)(2,1)} %get-tuple-element.50.mine_ref, bf16[384,1024]{1,0:T(8,128)(2,1)} %get-tuple-element.51.theirs_ref, bf16[1024,4096]{1,0:T(8,128)(2,1)} %bitcast.20.mine_w, bf16[1024,4096]{1,0:T(8,128)(2,1)} %collective-permute-done.9.theirs_w), custom_call_target="tpu_custom_call" | custom-call | flops 1024 | bytes 1024 | tf_op jit(solution)/shard_map/pallas_call | solution.py:219
  196.8 9.9 %all-to-all-done.2 = bf16[16,24,1024]{2,1,0:T(8,128)(2,1)S(1)} async-done(((bf16[16,24,1024]{2,1,0:T(8,128)(2,1)}), bf16[16,24,1024]{2,1,0:T(8,128)(2,1)S(1)}, u32[]{:S(2)}, u32[]{:S(2)}) %all-to-all-start.2) | async-done | bytes 786464 | tf_op jit(solution)/shard_map/all_to_all | solution.py:302
  206.7 4.5 %all-to-all-start.3 = ((bf16[16,24,3072]{2,1,0:T(8,128)(2,1)}), bf16[16,24,3072]{2,1,0:T(8,128)(2,1)}, u32[]{:S(2)}, u32[]{:S(2)}) async-start(bf16[16,24,3072]{2,1,0:T(8,128)(2,1)} %bitcast.60), calls=%async_computation.3 | async-start | bytes 4718592 | tf_op jit(solution)/shard_map/all_to_all | solution.py:302
  211.3 1.2 shard_map.110.refs_0_
  212.5 50.1 %all-to-all-done.3 = bf16[16,24,3072]{2,1,0:T(8,128)(2,1)} async-done(((bf16[16,24,3072]{2,1,0:T(8,128)(2,1)}), bf16[16,24,3072]{2,1,0:T(8,128)(2,1)}, u32[]{:S(2)}, u32[]{:S(2)}) %all-to-all-start.3) | async-done | bytes 2359328 | tf_op jit(solution)/shard_map/all_to_all | solution.py:302
  262.6 4.2 %shard_map.111 = bf16[128,4096]{1,0:T(8,128)(2,1)} custom-call(f32[128,2048]{1,0:T(8,128)S(1)} %get-tuple-element.35.refs_0_.early_ref, f32[128,2048]{1,0:T(8,128)S(1)} %get-tuple-element.39.refs_1_.late_ref, f32[4,4096]{1,0:T(4,128)S(1)} %copy-done.3, s32[128,2]{1,0:T(8,128)S(1)} %fusion.3.cells_ref, ...), custom_call_target="tpu_custom_call", output_to_operand_aliasing={{}: (6, {})} | custom-call | flops 1024 | bytes 1024 | tf_op jit(solution)/shard_map/pallas_call | solution.py:255
  (30 shorter events, 1.8 us)
Async XLA Ops:
  0.0 44.9 %copy-start.1 = (bf16[1024,4096]{1,0:T(8,128)(2,1)S(1)}, bf16[1024,4096]{1,0:T(8,128)(2,1)}, u32[]{:S(2)}) copy-start(bf16[1024,4096]{1,0:T(8,128)(2,1)} %mine_w.1) | copy-start | bytes 25165828
  2.3 42.6 %collective-permute-start.4 = (bf16[1024,4096]{1,0:T(8,128)(2,1)}, bf16[1024,4096]{1,0:T(8,128)(2,1)S(1)}, u32[]{:S(2)}, u32[]{:S(2)}) collective-permute-start(bf16[1024,4096]{1,0:T(8,128)(2,1)} %mine_w.1), channel_id=1, source_target_pairs={{0,8},{8,0},{1,9},{9,1},{2,10},{10,2},{3,11},{11,3},{4,12},{12,4},... | collective-permute-start | bytes 25165832 | tf_op jit(solution)/shard_map/ppermute | solution.py:297
  2.9 7.5 %collective-permute-start = (bf16[3,128,1024]{2,1,0:T(8,128)(2,1)S(1)}, bf16[3,128,1024]{2,1,0:T(8,128)(2,1)S(1)}, u32[]{:S(2)}, u32[]{:S(2)}) collective-permute-start(bf16[3,128,1024]{2,1,0:T(8,128)(2,1)S(1)} %get-tuple-element.56), channel_id=1, source_target_pairs={{0,8},{8,0},{16,24},{24,16},{1,9},{9,1},{17,25},{25,17},{2,10},{10... | collective-permute-start | bytes 2359304 | tf_op jit(solution)/shard_map/ppermute | solution.py:317
  2.9 21.3 %collective-permute-start.1 = (bf16[3,128,1024]{2,1,0:T(8,128)(2,1)S(1)}, bf16[3,128,1024]{2,1,0:T(8,128)(2,1)S(1)}, u32[]{:S(2)}, u32[]{:S(2)}) collective-permute-start(bf16[3,128,1024]{2,1,0:T(8,128)(2,1)S(1)} %get-tuple-element.58), channel_id=1, source_target_pairs={{0,16},{8,24},{16,0},{24,8},{1,17},{9,25},{17,1},{25,9},{2,18},{10... | collective-permute-start | bytes 2359304 | tf_op jit(solution)/shard_map/ppermute | solution.py:317
  5.9 34.1 %collective-permute-start.2 = (bf16[3,128,1024]{2,1,0:T(8,128)(2,1)S(1)}, bf16[3,128,1024]{2,1,0:T(8,128)(2,1)S(1)}, u32[]{:S(2)}, u32[]{:S(2)}) collective-permute-start(bf16[3,128,1024]{2,1,0:T(8,128)(2,1)S(1)} %get-tuple-element.55), channel_id=1, source_target_pairs={{0,24},{8,16},{16,8},{24,0},{1,25},{9,17},{17,9},{25,1},{2,26},{10... | collective-permute-start | bytes 2359304 | tf_op jit(solution)/shard_map/ppermute | solution.py:317
  42.9 2.0 collective-permute-start.3
  44.9 21.5 %copy-start.2 = (bf16[1,128,4096]{2,1,0:T(8,128)(2,1)S(1)}, bf16[1,128,4096]{2,1,0:T(8,128)(2,1)}, u32[]{:S(2)}) copy-start(bf16[1,128,4096]{2,1,0:T(8,128)(2,1)} %param.10) | copy-start | bytes 3145732
  44.9 21.5 %copy-start.3 = (f32[4,4096]{1,0:T(4,128)S(1)}, f32[4,4096]{1,0:T(4,128)}, u32[]{:S(2)}) copy-start(f32[4,4096]{1,0:T(4,128)} %mod_ref.11) | copy-start | bytes 196612
  51.6 26.0 %copy-start.5 = (s32[1,128,2]{1,2,0:T(2,128)S(1)}, s32[1,128,2]{1,2,0:T(2,128)}, u32[]{:S(2)}) copy-start(s32[1,128,2]{1,2,0:T(2,128)} %param.15) | copy-start | bytes 3076
  51.6 26.1 %copy-start.6 = (s32[1,128,2]{1,2,0:T(2,128)S(1)}, s32[1,128,2]{1,2,0:T(2,128)}, u32[]{:S(2)}) copy-start(s32[1,128,2]{1,2,0:T(2,128)} %param.14) | copy-start | bytes 3076
  51.6 14.8 %collective-permute-start.5 = (bf16[128,2048]{1,0:T(8,128)(2,1)S(1)}, bf16[128,2048]{1,0:T(8,128)(2,1)S(1)}, u32[]{:S(2)}, u32[]{:S(2)}) collective-permute-start(bf16[128,2048]{1,0:T(8,128)(2,1)S(1)} %get-tuple-element.34), channel_id=1, source_target_pairs={{0,16},{16,0},{1,17},{17,1},{2,18},{18,2},{3,19},{19,3},{4,20},{20... | collective-permute-start | bytes 1572872 | tf_op jit(solution)/shard_map/ppermute | solution.py:346
  53.4 23.7 %collective-permute-start.6 = (bf16[128,2048]{1,0:T(8,128)(2,1)S(1)}, bf16[128,2048]{1,0:T(8,128)(2,1)S(1)}, u32[]{:S(2)}, u32[]{:S(2)}) collective-permute-start(bf16[128,2048]{1,0:T(8,128)(2,1)S(1)} %get-tuple-element.37), channel_id=1, source_target_pairs={{0,16},{16,0},{1,17},{17,1},{2,18},{18,2},{3,19},{19,3},{4,20},{20... | collective-permute-start | bytes 1572872 | tf_op jit(solution)/shard_map/ppermute | solution.py:346
  53.7 92.7 %collective-permute-start.7 = (bf16[4096,1024]{1,0:T(8,128)(2,1)}, bf16[4096,1024]{1,0:T(8,128)(2,1)}, u32[]{:S(2)}, u32[]{:S(2)}) collective-permute-start(bf16[4096,1024]{1,0:T(8,128)(2,1)} %bitcast.18.refs_0_), channel_id=1, source_target_pairs={{0,8},{8,0},{1,9},{9,1},{2,10},{10,2},{3,11},{11,3},{4,12},{12,4},... | collective-permute-start | bytes 25165832 | tf_op jit(solution)/shard_map/ppermute | solution.py:297
  53.7 92.7 %collective-permute-start.8 = (bf16[4096,1024]{1,0:T(8,128)(2,1)}, bf16[4096,1024]{1,0:T(8,128)(2,1)}, u32[]{:S(2)}, u32[]{:S(2)}) collective-permute-start(bf16[4096,1024]{1,0:T(8,128)(2,1)} %bitcast.19.refs_2_), channel_id=1, source_target_pairs={{0,8},{8,0},{1,9},{9,1},{2,10},{10,2},{3,11},{11,3},{4,12},{12,4},... | collective-permute-start | bytes 25165832 | tf_op jit(solution)/shard_map/ppermute | solution.py:297
  77.5 99.9 %collective-permute-start.9 = (bf16[1024,4096]{1,0:T(8,128)(2,1)}, bf16[1024,4096]{1,0:T(8,128)(2,1)}, u32[]{:S(2)}, u32[]{:S(2)}) collective-permute-start(bf16[1024,4096]{1,0:T(8,128)(2,1)} %bitcast.20.mine_w), channel_id=1, source_target_pairs={{0,8},{8,0},{1,9},{9,1},{2,10},{10,2},{3,11},{11,3},{4,12},{12,4},... | collective-permute-start | bytes 25165832 | tf_op jit(solution)/shard_map/ppermute | solution.py:297
  78.9 1.5 copy-start
  80.4 60.1 %all-to-all-start = ((bf16[16,24,3072]{2,1,0:T(8,128)(2,1)}), bf16[16,24,3072]{2,1,0:T(8,128)(2,1)}, u32[]{:S(2)}, u32[]{:S(2)}) async-start(bf16[16,24,3072]{2,1,0:T(8,128)(2,1)} %bitcast.53), calls=%async_computation | async-start | bytes 4718592 | tf_op jit(solution)/shard_map/all_to_all | solution.py:302
  140.5 26.5 %all-to-all-start.1 = ((bf16[16,24,1024]{2,1,0:T(8,128)(2,1)}), bf16[16,24,1024]{2,1,0:T(8,128)(2,1)S(1)}, u32[]{:S(2)}, u32[]{:S(2)}) async-start(bf16[16,24,1024]{2,1,0:T(8,128)(2,1)} %bitcast.16), calls=%async_computation.1 | async-start | bytes 1572864 | tf_op jit(solution)/shard_map/all_to_all | solution.py:302
  167.0 0.9 copy-start.4
  182.8 23.9 %all-to-all-start.2 = ((bf16[16,24,1024]{2,1,0:T(8,128)(2,1)}), bf16[16,24,1024]{2,1,0:T(8,128)(2,1)S(1)}, u32[]{:S(2)}, u32[]{:S(2)}) async-start(bf16[16,24,1024]{2,1,0:T(8,128)(2,1)} %bitcast.61), calls=%async_computation.2 | async-start | bytes 1572864 | tf_op jit(solution)/shard_map/all_to_all | solution.py:302
  196.7 14.4 %copy-start.7 = (f32[1,128,2]{1,2,0:T(2,128)S(1)}, f32[1,128,2]{1,2,0:T(2,128)}, u32[]{:S(2)}) copy-start(f32[1,128,2]{1,2,0:T(2,128)} %param.16) | copy-start | bytes 3076
  206.7 55.9 %all-to-all-start.3 = ((bf16[16,24,3072]{2,1,0:T(8,128)(2,1)}), bf16[16,24,3072]{2,1,0:T(8,128)(2,1)}, u32[]{:S(2)}, u32[]{:S(2)}) async-start(bf16[16,24,3072]{2,1,0:T(8,128)(2,1)} %bitcast.60), calls=%async_computation.3 | async-start | bytes 4718592 | tf_op jit(solution)/shard_map/all_to_all | solution.py:302

commit v4 on v3

--- a/solution.py
+++ b/solution.py
@@ -171,38 +171,81 @@
     )(modulation, cells, stats, *parts)
 
 
-def ffn_in_kernel(first, last, rows_ref, *refs):
-    weights, refs = refs[:4], refs[4:]
-    sums = [dot32(rows_ref[...], weight[...]) for weight in weights]
-    if not first:
-        olds, refs = refs[:4], refs[4:]
-        sums = [total + old[...] for total, old in zip(sums, olds)]
-    if last:
-        for gate, up, out_ref in zip(sums[:2], sums[2:], refs):
-            out_ref[...] = (gate / (1.0 + jnp.exp(-gate)) * up).astype(jnp.bfloat16)
-    else:
-        for total, out_ref in zip(sums, refs):
-            out_ref[...] = total
-
-
-def ffn_in(rows, weights, olds, start, last):
+def ffn_first_kernel(rows_ref, *refs):
+    for weight, out_ref in zip(refs[:4], refs[4:]):
+        out_ref[...] = dot32(rows_ref[...], weight[...])
+
+
+def ffn_first(rows, weights):
     count, size = rows.shape
     units = weights[0].shape[1]
     tile = min(256, units)
-    block = start // size
-    weight = pl.BlockSpec((size, tile), lambda n: (block, n))
-    part = pl.BlockSpec((count, tile), lambda n: (0, n))
-    outs = 2 if last else 4
-    kind = jnp.bfloat16 if last else jnp.float32
-    return pl.pallas_call(
-        functools.partial(ffn_in_kernel, not olds, last),
+    return pl.pallas_call(
+        ffn_first_kernel,
         grid=(units // tile,),
-        out_shape=[jax.ShapeDtypeStruct((count, units), kind)] * outs,
-        in_specs=[pl.BlockSpec((count, size), lambda n: (0, 0))] + [weight] * 4 + [part] * len(olds),
-        out_specs=[part] * outs,
+        out_shape=[jax.ShapeDtypeStruct((count, units), jnp.float32)] * 4,
+        in_specs=[pl.BlockSpec((count, size), lambda n: (0, 0))]
+        + [pl.BlockSpec((size, tile), lambda n: (0, n))] * 4,
+        out_specs=[pl.BlockSpec((count, tile), lambda n: (0, n))] * 4,
         compiler_params=grant(57),
         cost_estimate=LOW,
-    )(rows, *weights, *olds)
+    )(rows, *weights)
+
+
+def ffn_tail_kernel(head, rows_ref, *refs):
+    weights, sums, downs = refs[:4], refs[4:8], refs[8:10]
+    acts, value_ref = refs[10:12], refs[12]
+    weight_buf, sum_buf, down_buf, sems = refs[13:]
+    size = rows_ref.shape[1]
+    low = weights[0].shape[0] - size
+    order = (0, 2, 1, 3)
+    copies = {}
+    for i in order:
+        copies["sum", i] = pltpu.make_async_copy(sums[i], sum_buf.at[i], sems.at[i])
+        copies["weight", i] = pltpu.make_async_copy(
+            weights[i].at[pl.ds(low, size), :], weight_buf.at[i], sems.at[4 + i]
+        )
+    for i in range(2):
+        copies["down", i] = pltpu.make_async_copy(
+            downs[i].at[:, pl.ds(0, head)], down_buf.at[i], sems.at[8 + i]
+        )
+    for copy in copies.values():
+        copy.start()
+    rows = rows_ref[...]
+
+    def total(i):
+        copies["sum", i].wait()
+        copies["weight", i].wait()
+        return dot32(rows, weight_buf[i]) + sum_buf[i]
+
+    for i in range(2):
+        gate = total(i)
+        acts[i][...] = (gate / (1.0 + jnp.exp(-gate)) * total(2 + i)).astype(jnp.bfloat16)
+    for i in range(2):
+        copies["down", i].wait()
+    value = dot32(acts[0][...], down_buf[0]) + dot32(acts[1][...], down_buf[1])
+    value_ref[...] = value.astype(jnp.bfloat16)
+
+
+def ffn_tail(rows, weights, sums, downs, head):
+    count, size = rows.shape
+    units = weights[0].shape[1]
+    anywhere = pl.BlockSpec(memory_space=pl.ANY)
+    act = jax.ShapeDtypeStruct((count, units), jnp.bfloat16)
+    return pl.pallas_call(
+        functools.partial(ffn_tail_kernel, head),
+        out_shape=[act, act, jax.ShapeDtypeStruct((count, head), jnp.bfloat16)],
+        in_specs=[VMEM] + [anywhere] * 10,
+        out_specs=[VMEM] * 3,
+        scratch_shapes=[
+            pltpu.VMEM((4, size, units), jnp.bfloat16),
+            pltpu.VMEM((4, count, units), jnp.float32),
+            pltpu.VMEM((2, units, head), jnp.bfloat16),
+            pltpu.SemaphoreType.DMA((10,)),
+        ],
+        compiler_params=grant(57),
+        cost_estimate=LOW,
+    )(rows, *weights, *sums, *downs)
 
 
 def ffn_out_kernel(mine_ref, theirs_ref, mine_w, theirs_w, out_ref):
@@ -227,49 +270,41 @@
     )(*acts, *weights)
 
 
-def combine_kernel(first, turn, early_ref, late_ref, mod_ref, cells_ref, gates_ref, back_ref, *refs):
-    out_ref = refs[-1]
-    tokens, tile = out_ref.shape
-    _, copies, half, _ = back_ref.shape
+def combine_kernel(start, early_ref, late_ref, mod_ref, cells_ref, gates_ref, back_ref, *refs):
+    *before, out_ref = refs
+    tokens, part = early_ref.shape
+    _, copies, half, size = back_ref.shape
+    low = 0
+    if before:
+        low = start
+        out_ref[:, :low] = before[0][...]
     cells = lax.broadcasted_iota(jnp.int32, (tokens, 2 * half), 1)
     one_hot = jnp.concatenate(
         [(cells == cells_ref[:, i : i + 1]).astype(jnp.bfloat16) for i in range(2)], axis=0
     )
-    picked = 0.0
-    for i in range(copies):
-        picked = picked + dot32(one_hot, back_ref[:, i].reshape(2 * half, tile))
-    combined = gates_ref[:, 0:1] * picked[:tokens] + gates_ref[:, 1:2] * picked[tokens:]
-    is_early = first + pl.program_id(0) < turn
-    residual = jnp.where(is_early, early_ref[...], late_ref[...])
-    out_ref[...] = (residual + mod_ref[3:4, :] * combined).astype(jnp.bfloat16)
-
-
-def combine(residuals, modulation, cells, gates, back, start, previous):
-    tokens, part = residuals[0].shape
-    width = modulation.shape[1]
-    _, copies, half, size = back.shape
-    tile = min(1024, size)
-    first, turn = start // tile, part // tile
-    small = pl.BlockSpec((tokens, 2), lambda n: (0, 0))
-    more = [] if previous is None else [previous]
-    return pl.pallas_call(
-        functools.partial(combine_kernel, first, turn),
-        grid=(size // tile,),
-        out_shape=jax.ShapeDtypeStruct((tokens, width), jnp.bfloat16),
-        in_specs=[
-            pl.BlockSpec((tokens, tile), lambda n: (0, jnp.minimum(first + n, turn - 1))),
-            pl.BlockSpec((tokens, tile), lambda n: (0, jnp.maximum(first + n - turn, 0))),
-            pl.BlockSpec((4, tile), lambda n: (0, first + n)),
-            small,
-            small,
-            pl.BlockSpec((2, copies, half, tile), lambda n: (0, 0, 0, n)),
-        ]
-        + [pl.BlockSpec(memory_space=pl.ANY)] * len(more),
-        out_specs=pl.BlockSpec((tokens, tile), lambda n: (0, first + n)),
-        input_output_aliases={6: 0} if more else {},
+    for ref, begin in ((early_ref, 0), (late_ref, part)):
+        first, last = max(start, begin), min(start + size, begin + part)
+        if first < last:
+            picked = 0.0
+            for i in range(copies):
+                rows = back_ref[:, i, :, first - start : last - start]
+                picked = picked + dot32(one_hot, rows.reshape(2 * half, last - first))
+            combined = gates_ref[:, 0:1] * picked[:tokens] + gates_ref[:, 1:2] * picked[tokens:]
+            total = ref[:, first - begin : last - begin] + mod_ref[3:4, first:last] * combined
+            out_ref[:, first - start + low : last - start + low] = total.astype(jnp.bfloat16)
+
+
+def combine(residuals, modulation, cells, gates, back, start, before):
+    tokens = residuals[0].shape[0]
+    size = back.shape[3] + sum(value.shape[1] for value in before)
+    return pl.pallas_call(
+        functools.partial(combine_kernel, start),
+        out_shape=jax.ShapeDtypeStruct((tokens, size), jnp.bfloat16),
+        in_specs=[VMEM] * (6 + len(before)),
+        out_specs=VMEM,
         compiler_params=grant(28),
         cost_estimate=LOW,
-    )(*residuals, modulation, cells, gates, back, *more)
+    )(*residuals, modulation, cells, gates, back, *before)
 
 
 def local(
@@ -353,20 +388,23 @@
     downs = (down_mine, down_other)
 
     quarter = width // 4
-    rows, sums, token = None, (), stats[1]
-    for start, stop in ((0, width - quarter), (width - quarter, width)):
-        row = after(stats[1], token)
-        token = pack(modulation, row_cells, n_cells, row, residuals, start, stop)
-        rows = dispatch(token if rows is None else after(token, rows))
-        sums = ffn_in(rows, gates_up, sums, start, stop == width)
-    acts = sums
-
-    out, token = None, acts
-    for start, size in ((0, quarter), (quarter, width - quarter)):
-        value = after(ffn_out(acts, downs, start, size), token)
-        token = exchange(value)
-        back = token.reshape(2, copies, n_ep * capacity, size)
-        out = combine(residuals, modulation, cells, route_gates[0], back, start, out)
+    sent = pack(modulation, row_cells, n_cells, stats[1], residuals, 0, width - quarter)
+    rows = dispatch(sent)
+    sums = ffn_first(rows, gates_up)
+    sent = pack(
+        modulation, row_cells, n_cells, after(stats[1], sent), residuals, width - quarter, width
+    )
+    rows = dispatch(after(sent, rows))
+    *acts, value = ffn_tail(rows, gates_up, sums, downs, quarter)
+
+    def give_back(value):
+        return exchange(value).reshape(2, copies, n_ep * capacity, value.shape[1])
+
+    gates = route_gates[0]
+    back = give_back(value)
+    done = combine(residuals, modulation, cells, gates, back, 0, [])
+    back = give_back(after(ffn_out(acts, downs, quarter, width - quarter), back))
+    out = combine(residuals, modulation, cells, gates, back, quarter, [done])
     return out[None]
 
 

time: 267 us -> 262 us (0.981)
  Pallas kernels: 59.7 us -> 54 us
    pallas_call x2 -> x1, Pallas kernels: 15.7 us -> 10.3 us  [ffn_out(): pl.pallas_call(ffn_out_kernel, grid=(size // tile,), out_shape=jax.ShapeD...]
  transfers between devices with their start and end apart: 14 -> 14, of which waited for: 10 -> 9; matrix products, arithmetic and copies ran while one was open for 0% -> 0% of each run, Pallas kernels for 16% -> 13%
where the time goes in v4:
time: 262 us
  waiting for transfers between devices  175 us (67%)
  Pallas kernels  54 us (21%)
  starting transfers between devices  27.2 us (10%)
  local copies, waits for them, and re-layouts  5.14 us (2%)
    all_to_all x4, waiting for transfers between devices, exchange(): lax.all_to_all(value, ('x', 'ep'), split_axis=0, concat_axis=0, tiled=True)  116 us
    ppermute x3, waiting for transfers between devices, local(): piece = lax.ppermute(piece, ('x', 'core'), shift(dx, dc))  34.8 us
    ppermute x2, waiting for transfers between devices, local(): lax.ppermute(value, 'x', [(x, (x - dx) % n_x) for x in range(n_x)])  22.3 us
    all_to_all x4, starting transfers between devices, exchange(): lax.all_to_all(value, ('x', 'ep'), split_axis=0, concat_axis=0, tiled=True)  21.1 us
    pallas_call x1, Pallas kernels, ffn_first(): pl.pallas_call(ffn_first_kernel, grid=(units // tile,), out_shape=[jax.Sh...  16.4 us
    pallas_call x1, Pallas kernels, ffn_tail(): pl.pallas_call(functools.partial(ffn_tail_kernel, head), out_shape=[act,...  10.4 us
    pallas_call x1, Pallas kernels, ffn_out(): pl.pallas_call(ffn_out_kernel, grid=(size // tile,), out_shape=jax.ShapeD...  10.3 us
    pallas_call x1, Pallas kernels, project(): pl.pallas_call(project_kernel, grid=(4,), out_shape=out_shape, in_specs=[...  6.65 us
  transfers between devices with their start and end apart: 14, of which 9 were waited for; matrix products, arithmetic and copies ran while one was open for 0% of the time, Pallas kernels for 13%

profile of v4, /device:TPU:0, one launch (start us, length us, event | category | flops | bytes accessed | tf_op | source)
XLA Modules:
  0.0 262.0 jit_solution(11618647448381311913)
XLA Ops:
  0.0 2.3 dynamic-slice_bitcast_fusion
  2.3 0.5 collective-permute-start.4
  2.9 2.6 collective-permute-start.2
  5.6 17.7 %collective-permute-done.2.refs_3_ = bf16[3,128,1024]{2,1,0:T(8,128)(2,1)S(1)} collective-permute-done((bf16[3,128,1024]{2,1,0:T(8,128)(2,1)S(1)}, bf16[3,128,1024]{2,1,0:T(8,128)(2,1)S(1)}, u32[]{:S(2)}, u32[]{:S(2)}) %collective-permute-start.2) | collective-permute-done | bytes 786464 | tf_op jit(solution)/shard_map/ppermute | solution.py:352
  23.4 17.1 %collective-permute-done.1.refs_2_ = bf16[3,128,1024]{2,1,0:T(8,128)(2,1)S(1)} collective-permute-done((bf16[3,128,1024]{2,1,0:T(8,128)(2,1)S(1)}, bf16[3,128,1024]{2,1,0:T(8,128)(2,1)S(1)}, u32[]{:S(2)}, u32[]{:S(2)}) %collective-permute-start.1) | collective-permute-done | bytes 786464 | tf_op jit(solution)/shard_map/ppermute | solution.py:352
  40.4 3.0 %shard_map.100 = (bf16[2,128,1024]{2,1,0:T(8,128)(2,1)S(1)}, bf16[2,128,1024]{2,1,0:T(8,128)(2,1)S(1)}) custom-call(bf16[3,128,1024]{2,1,0:T(8,128)(2,1)S(1)} %get-tuple-element.55.refs_0_, bf16[3,128,1024]{2,1,0:T(8,128)(2,1)S(1)} %collective-permute-done.refs_1_, bf16[3,128,1024]{2,1,0:T(8,128)(2,1)S(1)} %collective-permute-done.1.refs_2_, ...), custom_call_target="tpu_custom_call" | custom-call | flops 1024 | bytes 1024 | tf_op jit(solution)/shard_map/pallas_call | solution.py:53
  43.5 1.9 collective-permute-done.3.theirs_ref
  45.4 6.7 %shard_map.101 = (f32[128,2048]{1,0:T(8,128)S(1)}, bf16[128,2048]{1,0:T(8,128)(2,1)S(1)}, f32[128,2048]{1,0:T(8,128)S(1)}, bf16[128,2048]{1,0:T(8,128)(2,1)S(1)}) custom-call(bf16[2,128,1024]{2,1,0:T(8,128)(2,1)S(1)} %get-tuple-element.29.mine_ref, bf16[2,128,1024]{2,1,0:T(8,128)(2,1)S(1)} %collective-permute-done.3.theirs_ref, ...), custom_call_target="tpu_custom_call" | custom-call | flops 1024 | bytes 1024 | tf_op jit(solution)/shard_map/pallas_call | solution.py:97
  52.1 1.8 collective-permute-start.5
  53.9 0.3 collective-permute-start.6
  54.2 0.5 collective-permute-start.8
  54.7 12.2 %collective-permute-done.5.refs_0_ = bf16[128,2048]{1,0:T(8,128)(2,1)S(1)} collective-permute-done((bf16[128,2048]{1,0:T(8,128)(2,1)S(1)}, bf16[128,2048]{1,0:T(8,128)(2,1)S(1)}, u32[]{:S(2)}, u32[]{:S(2)}) %collective-permute-start.5) | collective-permute-done | bytes 524320 | tf_op jit(solution)/shard_map/ppermute | solution.py:381
  66.9 0.4 shard_map.102
  67.3 10.0 %collective-permute-done.6.refs_0_ = bf16[128,2048]{1,0:T(8,128)(2,1)S(1)} collective-permute-done((bf16[128,2048]{1,0:T(8,128)(2,1)S(1)}, bf16[128,2048]{1,0:T(8,128)(2,1)S(1)}, u32[]{:S(2)}, u32[]{:S(2)}) %collective-permute-start.6) | collective-permute-done | bytes 524320 | tf_op jit(solution)/shard_map/ppermute | solution.py:381
  77.3 0.4 shard_map.103
  78.2 0.9 shard_map.104
  79.1 1.5 copy-done
  80.6 7.1 %all-to-all-start = ((bf16[16,24,3072]{2,1,0:T(8,128)(2,1)}), bf16[16,24,3072]{2,1,0:T(8,128)(2,1)}, u32[]{:S(2)}, u32[]{:S(2)}) async-start(bf16[16,24,3072]{2,1,0:T(8,128)(2,1)} %bitcast.53), calls=%async_computation | async-start | bytes 4718592 | tf_op jit(solution)/shard_map/all_to_all | solution.py:337
  87.8 1.4 shard_map.105
  89.2 51.5 %all-to-all-done = bf16[16,24,3072]{2,1,0:T(8,128)(2,1)} async-done(((bf16[16,24,3072]{2,1,0:T(8,128)(2,1)}), bf16[16,24,3072]{2,1,0:T(8,128)(2,1)}, u32[]{:S(2)}, u32[]{:S(2)}) %all-to-all-start) | async-done | bytes 2359328 | tf_op jit(solution)/shard_map/all_to_all | solution.py:337
  140.7 5.9 %all-to-all-start.1 = ((bf16[16,24,1024]{2,1,0:T(8,128)(2,1)}), bf16[16,24,1024]{2,1,0:T(8,128)(2,1)S(1)}, u32[]{:S(2)}, u32[]{:S(2)}) async-start(bf16[16,24,1024]{2,1,0:T(8,128)(2,1)} %bitcast.16), calls=%async_computation.1 | async-start | bytes 1572864 | tf_op jit(solution)/shard_map/all_to_all | solution.py:337
  146.6 16.4 %shard_map.106 = (f32[384,1024]{1,0:T(8,128)}, f32[384,1024]{1,0:T(8,128)}, f32[384,1024]{1,0:T(8,128)}, f32[384,1024]{1,0:T(8,128)}) custom-call(bf16[384,3072]{1,0:T(8,128)(2,1)} %bitcast.15.rows_ref, bf16[4096,1024]{1,0:T(8,128)(2,1)} %bitcast.18.refs_0_, bf16[4096,1024]{1,0:T(8,128)(2,1)} %collective-permute-done.7.refs_1_, ...), custom_call_target="tpu_custom_call" | custom-call | flops 1024 | bytes 1024 | tf_op jit(solution)/shard_map/pallas_call | solution.py:183
  163.0 4.2 %all-to-all-done.1 = bf16[16,24,1024]{2,1,0:T(8,128)(2,1)S(1)} async-done(((bf16[16,24,1024]{2,1,0:T(8,128)(2,1)}), bf16[16,24,1024]{2,1,0:T(8,128)(2,1)S(1)}, u32[]{:S(2)}, u32[]{:S(2)}) %all-to-all-start.1) | async-done | bytes 786464 | tf_op jit(solution)/shard_map/all_to_all | solution.py:337
  167.2 0.9 copy-done.4
  168.1 10.4 %shard_map.107 = (bf16[384,1024]{1,0:T(8,128)(2,1)}, bf16[384,1024]{1,0:T(8,128)(2,1)}, bf16[384,1024]{1,0:T(8,128)(2,1)}) custom-call(bf16[384,1024]{1,0:T(8,128)(2,1)} %bitcast.61, bf16[4096,1024]{1,0:T(8,128)(2,1)} %bitcast.18.refs_0_, bf16[4096,1024]{1,0:T(8,128)(2,1)} %collective-permute-done.7.refs_1_, bf16[4096,1024]{1,0:T(8,128)(2,1)} %bitcast.19.refs_2_, ...), custom_call_target="tpu_custom_call" | custom-call | flops 1024 | bytes 1024 | tf_op jit(solution)/shard_map/pallas_call | solution.py:235
  178.5 3.6 %all-to-all-start.2 = ((bf16[16,24,1024]{2,1,0:T(8,128)(2,1)}), bf16[16,24,1024]{2,1,0:T(8,128)(2,1)S(1)}, u32[]{:S(2)}, u32[]{:S(2)}) async-start(bf16[16,24,1024]{2,1,0:T(8,128)(2,1)} %bitcast.62), calls=%async_computation.2 | async-start | bytes 1572864 | tf_op jit(solution)/shard_map/all_to_all | solution.py:337
  182.1 10.3 %shard_map.108 = bf16[384,3072]{1,0:T(8,128)(2,1)} custom-call(bf16[384,1024]{1,0:T(8,128)(2,1)} %get-tuple-element.49.mine_ref, bf16[384,1024]{1,0:T(8,128)(2,1)} %get-tuple-element.50.theirs_ref, bf16[1024,4096]{1,0:T(8,128)(2,1)} %bitcast.20.refs_8_.mine_w, bf16[1024,4096]{1,0:T(8,128)(2,1)} %collective-permute-done.9.refs_9_.theirs_w), custom_call_target="tpu_custom_call" | custom-call | flops 1024 | bytes 1024 | tf_op jit(solution)/shard_map/pallas_call | solution.py:262
  192.4 9.9 %all-to-all-done.2 = bf16[16,24,1024]{2,1,0:T(8,128)(2,1)S(1)} async-done(((bf16[16,24,1024]{2,1,0:T(8,128)(2,1)}), bf16[16,24,1024]{2,1,0:T(8,128)(2,1)S(1)}, u32[]{:S(2)}, u32[]{:S(2)}) %all-to-all-start.2) | async-done | bytes 786464 | tf_op jit(solution)/shard_map/all_to_all | solution.py:337
  202.4 4.5 %all-to-all-start.3 = ((bf16[16,24,3072]{2,1,0:T(8,128)(2,1)}), bf16[16,24,3072]{2,1,0:T(8,128)(2,1)}, u32[]{:S(2)}, u32[]{:S(2)}) async-start(bf16[16,24,3072]{2,1,0:T(8,128)(2,1)} %bitcast.60), calls=%async_computation.3 | async-start | bytes 4718592 | tf_op jit(solution)/shard_map/all_to_all | solution.py:337
  207.0 0.5 shard_map.109.refs_0_
  207.5 50.8 %all-to-all-done.3 = bf16[16,24,3072]{2,1,0:T(8,128)(2,1)} async-done(((bf16[16,24,3072]{2,1,0:T(8,128)(2,1)}), bf16[16,24,3072]{2,1,0:T(8,128)(2,1)}, u32[]{:S(2)}, u32[]{:S(2)}) %all-to-all-start.3) | async-done | bytes 2359328 | tf_op jit(solution)/shard_map/all_to_all | solution.py:337
  258.3 3.7 %shard_map.110 = bf16[128,4096]{1,0:T(8,128)(2,1)} custom-call(f32[128,2048]{1,0:T(8,128)S(1)} %get-tuple-element.34.refs_0_.early_ref, f32[128,2048]{1,0:T(8,128)S(1)} %get-tuple-element.38.refs_1_.late_ref, f32[4,4096]{1,0:T(4,128)S(1)} %copy-done.3, s32[128,2]{1,0:T(8,128)S(1)} %fusion.3.cells_ref, f32[128,2]{1,0:T(8,128)S(1)} %bitcast.59, ...), custom_call_target="tpu_custom_call" | custom-call | flops 1024 | bytes 1024 | tf_op jit(solution)/shard_map/pallas_call | solution.py:300
  (29 shorter events, 0.8 us)
Async XLA Ops:
  0.0 45.4 %copy-start.1 = (bf16[1024,4096]{1,0:T(8,128)(2,1)S(1)}, bf16[1024,4096]{1,0:T(8,128)(2,1)}, u32[]{:S(2)}) copy-start(bf16[1024,4096]{1,0:T(8,128)(2,1)} %mine_w.1) | copy-start | bytes 25165828
  2.3 43.0 %collective-permute-start.4 = (bf16[1024,4096]{1,0:T(8,128)(2,1)}, bf16[1024,4096]{1,0:T(8,128)(2,1)S(1)}, u32[]{:S(2)}, u32[]{:S(2)}) collective-permute-start(bf16[1024,4096]{1,0:T(8,128)(2,1)} %mine_w.1), channel_id=1, source_target_pairs={{0,8},{8,0},{1,9},{9,1},{2,10},{10,2},{3,11},{11,3},{4,12},{12,4},... | collective-permute-start | bytes 25165832 | tf_op jit(solution)/shard_map/ppermute | solution.py:332
  2.9 20.5 %collective-permute-start.2 = (bf16[3,128,1024]{2,1,0:T(8,128)(2,1)S(1)}, bf16[3,128,1024]{2,1,0:T(8,128)(2,1)S(1)}, u32[]{:S(2)}, u32[]{:S(2)}) collective-permute-start(bf16[3,128,1024]{2,1,0:T(8,128)(2,1)S(1)} %get-tuple-element.53), channel_id=1, source_target_pairs={{0,24},{8,16},{16,8},{24,0},{1,25},{9,17},{17,9},{25,1},{2,26},{10... | collective-permute-start | bytes 2359304 | tf_op jit(solution)/shard_map/ppermute | solution.py:352
  5.5 34.9 %collective-permute-start.1 = (bf16[3,128,1024]{2,1,0:T(8,128)(2,1)S(1)}, bf16[3,128,1024]{2,1,0:T(8,128)(2,1)S(1)}, u32[]{:S(2)}, u32[]{:S(2)}) collective-permute-start(bf16[3,128,1024]{2,1,0:T(8,128)(2,1)S(1)} %get-tuple-element.56), channel_id=1, source_target_pairs={{0,16},{8,24},{16,0},{24,8},{1,17},{9,25},{17,1},{25,9},{2,18},{10... | collective-permute-start | bytes 2359304 | tf_op jit(solution)/shard_map/ppermute | solution.py:352
  5.5 34.9 %collective-permute-start = (bf16[3,128,1024]{2,1,0:T(8,128)(2,1)S(1)}, bf16[3,128,1024]{2,1,0:T(8,128)(2,1)S(1)}, u32[]{:S(2)}, u32[]{:S(2)}) collective-permute-start(bf16[3,128,1024]{2,1,0:T(8,128)(2,1)S(1)} %get-tuple-element.54), channel_id=1, source_target_pairs={{0,8},{8,0},{16,24},{24,16},{1,9},{9,1},{17,25},{25,17},{2,10},{10... | collective-permute-start | bytes 2359304 | tf_op jit(solution)/shard_map/ppermute | solution.py:352
  43.4 2.0 collective-permute-start.3
  45.4 21.5 %copy-start.2 = (bf16[1,128,4096]{2,1,0:T(8,128)(2,1)S(1)}, bf16[1,128,4096]{2,1,0:T(8,128)(2,1)}, u32[]{:S(2)}) copy-start(bf16[1,128,4096]{2,1,0:T(8,128)(2,1)} %param.10) | copy-start | bytes 3145732
  45.4 21.5 %copy-start.3 = (f32[4,4096]{1,0:T(4,128)S(1)}, f32[4,4096]{1,0:T(4,128)}, u32[]{:S(2)}) copy-start(f32[4,4096]{1,0:T(4,128)} %mod_ref.11) | copy-start | bytes 196612
  52.1 25.8 %copy-start.5 = (s32[1,128,2]{1,2,0:T(2,128)S(1)}, s32[1,128,2]{1,2,0:T(2,128)}, u32[]{:S(2)}) copy-start(s32[1,128,2]{1,2,0:T(2,128)} %param.14) | copy-start | bytes 3076
  52.1 25.9 %copy-start.6 = (s32[1,128,2]{1,2,0:T(2,128)S(1)}, s32[1,128,2]{1,2,0:T(2,128)}, u32[]{:S(2)}) copy-start(s32[1,128,2]{1,2,0:T(2,128)} %param.15) | copy-start | bytes 3076
  52.1 14.8 %collective-permute-start.5 = (bf16[128,2048]{1,0:T(8,128)(2,1)S(1)}, bf16[128,2048]{1,0:T(8,128)(2,1)S(1)}, u32[]{:S(2)}, u32[]{:S(2)}) collective-permute-start(bf16[128,2048]{1,0:T(8,128)(2,1)S(1)} %get-tuple-element.33), channel_id=1, source_target_pairs={{0,16},{16,0},{1,17},{17,1},{2,18},{18,2},{3,19},{19,3},{4,20},{20... | collective-permute-start | bytes 1572872 | tf_op jit(solution)/shard_map/ppermute | solution.py:381
  53.9 23.5 %collective-permute-start.6 = (bf16[128,2048]{1,0:T(8,128)(2,1)S(1)}, bf16[128,2048]{1,0:T(8,128)(2,1)S(1)}, u32[]{:S(2)}, u32[]{:S(2)}) collective-permute-start(bf16[128,2048]{1,0:T(8,128)(2,1)S(1)} %get-tuple-element.36), channel_id=1, source_target_pairs={{0,16},{16,0},{1,17},{17,1},{2,18},{18,2},{3,19},{19,3},{4,20},{20... | collective-permute-start | bytes 1572872 | tf_op jit(solution)/shard_map/ppermute | solution.py:381
  54.2 92.4 %collective-permute-start.7 = (bf16[4096,1024]{1,0:T(8,128)(2,1)}, bf16[4096,1024]{1,0:T(8,128)(2,1)}, u32[]{:S(2)}, u32[]{:S(2)}) collective-permute-start(bf16[4096,1024]{1,0:T(8,128)(2,1)} %bitcast.18.refs_0_), channel_id=1, source_target_pairs={{0,8},{8,0},{1,9},{9,1},{2,10},{10,2},{3,11},{11,3},{4,12},{12,4},... | collective-permute-start | bytes 25165832 | tf_op jit(solution)/shard_map/ppermute | solution.py:332
  54.2 92.5 %collective-permute-start.8 = (bf16[4096,1024]{1,0:T(8,128)(2,1)}, bf16[4096,1024]{1,0:T(8,128)(2,1)}, u32[]{:S(2)}, u32[]{:S(2)}) collective-permute-start(bf16[4096,1024]{1,0:T(8,128)(2,1)} %bitcast.19.refs_2_), channel_id=1, source_target_pairs={{0,8},{8,0},{1,9},{9,1},{2,10},{10,2},{3,11},{11,3},{4,12},{12,4},... | collective-permute-start | bytes 25165832 | tf_op jit(solution)/shard_map/ppermute | solution.py:332
  77.8 89.4 %collective-permute-start.9 = (bf16[1024,4096]{1,0:T(8,128)(2,1)}, bf16[1024,4096]{1,0:T(8,128)(2,1)}, u32[]{:S(2)}, u32[]{:S(2)}) collective-permute-start(bf16[1024,4096]{1,0:T(8,128)(2,1)} %bitcast.20.refs_8_.mine_w), channel_id=1, source_target_pairs={{0,8},{8,0},{1,9},{9,1},{2,10},{10,2},{3,11},{11,3},{4,12},{12,4},... | collective-permute-start | bytes 25165832 | tf_op jit(solution)/shard_map/ppermute | solution.py:332
  79.1 1.5 copy-start
  80.6 60.0 %all-to-all-start = ((bf16[16,24,3072]{2,1,0:T(8,128)(2,1)}), bf16[16,24,3072]{2,1,0:T(8,128)(2,1)}, u32[]{:S(2)}, u32[]{:S(2)}) async-start(bf16[16,24,3072]{2,1,0:T(8,128)(2,1)} %bitcast.53), calls=%async_computation | async-start | bytes 4718592 | tf_op jit(solution)/shard_map/all_to_all | solution.py:337
  140.7 26.5 %all-to-all-start.1 = ((bf16[16,24,1024]{2,1,0:T(8,128)(2,1)}), bf16[16,24,1024]{2,1,0:T(8,128)(2,1)S(1)}, u32[]{:S(2)}, u32[]{:S(2)}) async-start(bf16[16,24,1024]{2,1,0:T(8,128)(2,1)} %bitcast.16), calls=%async_computation.1 | async-start | bytes 1572864 | tf_op jit(solution)/shard_map/all_to_all | solution.py:337
  167.2 0.9 copy-start.4
  178.5 23.9 %all-to-all-start.2 = ((bf16[16,24,1024]{2,1,0:T(8,128)(2,1)}), bf16[16,24,1024]{2,1,0:T(8,128)(2,1)S(1)}, u32[]{:S(2)}, u32[]{:S(2)}) async-start(bf16[16,24,1024]{2,1,0:T(8,128)(2,1)} %bitcast.62), calls=%async_computation.2 | async-start | bytes 1572864 | tf_op jit(solution)/shard_map/all_to_all | solution.py:337
  192.4 14.4 %copy-start.7 = (f32[1,128,2]{1,2,0:T(2,128)S(1)}, f32[1,128,2]{1,2,0:T(2,128)}, u32[]{:S(2)}) copy-start(f32[1,128,2]{1,2,0:T(2,128)} %param.16) | copy-start | bytes 3076
  202.4 55.9 %all-to-all-start.3 = ((bf16[16,24,3072]{2,1,0:T(8,128)(2,1)}), bf16[16,24,3072]{2,1,0:T(8,128)(2,1)}, u32[]{:S(2)}, u32[]{:S(2)}) async-start(bf16[16,24,3072]{2,1,0:T(8,128)(2,1)} %bitcast.60), calls=%async_computation.3 | async-start | bytes 4718592 | tf_op jit(solution)/shard_map/all_to_all | solution.py:337

commit v5 on v4

--- a/solution.py
+++ b/solution.py
@@ -145,27 +145,50 @@
     )(latent, modulation, own, *received, *olds)
 
 
-def pack_kernel(start, stop, mod_ref, cells_ref, stats_ref, *refs):
-    *part_refs, sent_ref = refs
+def pieces_of(start, stop, size, step):
+    cuts = []
+    low = start
+    while low < stop:
+        high = min(stop, low + step, (low // size + 1) * size)
+        cuts.append((low, high))
+        low = high
+    return cuts
+
+
+def pack_kernel(cuts, mod_ref, cells_ref, stats_ref, *refs):
+    *part_refs, sent_ref, buf, sems = refs
+    start = cuts[0][0]
     tokens, size = part_refs[0].shape
-    cells = lax.broadcasted_iota(jnp.int32, (sent_ref.shape[0], tokens), 0)
+    cells = lax.broadcasted_iota(jnp.int32, (buf.shape[0], tokens), 0)
     one_hot = ((cells == cells_ref[0:1, :]) | (cells == cells_ref[1:2, :])).astype(jnp.bfloat16)
-    for i, part_ref in enumerate(part_refs):
-        low, high = max(start, i * size), min(stop, (i + 1) * size)
-        if low < high:
-            cut = slice(low, high)
-            part = part_ref[:, low - i * size : high - i * size]
-            normed = (part - stats_ref[:, 0:1]) * stats_ref[:, 1:2]
-            moe_in = (normed * (1.0 + mod_ref[2:3, cut]) + mod_ref[1:2, cut]).astype(jnp.bfloat16)
-            sent_ref[:, low - start : high - start] = dot32(one_hot, moe_in).astype(jnp.bfloat16)
+    copies = []
+    for i, (low, high) in enumerate(cuts):
+        cut = slice(low, high)
+        begin = low // size * size
+        part = part_refs[low // size][:, low - begin : high - begin]
+        normed = (part - stats_ref[:, 0:1]) * stats_ref[:, 1:2]
+        moe_in = (normed * (1.0 + mod_ref[2:3, cut]) + mod_ref[1:2, cut]).astype(jnp.bfloat16)
+        place = pl.ds(low - start, high - low)
+        buf[:, place] = dot32(one_hot, moe_in).astype(jnp.bfloat16)
+        copies.append(
+            pltpu.make_async_copy(buf.at[:, place], sent_ref.at[:, place], sems.at[i])
+        )
+        copies[-1].start()
+    for copy in copies:
+        copy.wait()
 
 
 def pack(modulation, cells, n_cells, stats, parts, start, stop):
-    return pl.pallas_call(
-        functools.partial(pack_kernel, start, stop),
+    cuts = pieces_of(start, stop, parts[0].shape[1], 1024)
+    return pl.pallas_call(
+        functools.partial(pack_kernel, cuts),
         out_shape=jax.ShapeDtypeStruct((n_cells, stop - start), jnp.bfloat16),
         in_specs=[VMEM] * (3 + len(parts)),
-        out_specs=VMEM,
+        out_specs=pl.BlockSpec(memory_space=pltpu.HBM),
+        scratch_shapes=[
+            pltpu.VMEM((n_cells, stop - start), jnp.bfloat16),
+            pltpu.SemaphoreType.DMA((len(cuts),)),
+        ],
         compiler_params=grant(28),
         cost_estimate=LOW,
     )(modulation, cells, stats, *parts)
@@ -187,7 +210,7 @@
         in_specs=[pl.BlockSpec((count, size), lambda n: (0, 0))]
         + [pl.BlockSpec((size, tile), lambda n: (0, n))] * 4,
         out_specs=[pl.BlockSpec((count, tile), lambda n: (0, n))] * 4,
-        compiler_params=grant(57),
+        compiler_params=grant(54),
         cost_estimate=LOW,
     )(rows, *weights)
 
@@ -243,7 +266,7 @@
             pltpu.VMEM((2, units, head), jnp.bfloat16),
             pltpu.SemaphoreType.DMA((10,)),
         ],
-        compiler_params=grant(57),
+        compiler_params=grant(54),
         cost_estimate=LOW,
     )(rows, *weights, *sums, *downs)
 
@@ -270,38 +293,68 @@
     )(*acts, *weights)
 
 
-def combine_kernel(start, early_ref, late_ref, mod_ref, cells_ref, gates_ref, back_ref, *refs):
-    *before, out_ref = refs
+def combine_kernel(cuts, early_ref, late_ref, mod_ref, cells_ref, gates_ref, back_ref, *refs):
+    *before, out_ref, back_buf, out_buf, load_sems, store_sems = refs
     tokens, part = early_ref.shape
-    _, copies, half, size = back_ref.shape
-    low = 0
+    _, copies, half, _ = back_ref.shape
+    start = cuts[0][0]
+    shift = start if before else 0
+    loads, stores = [], []
+    for i, (low, high) in enumerate(cuts):
+        place = pl.ds(low - start, high - low)
+        loads.append(
+            pltpu.make_async_copy(
+                back_ref.at[:, :, :, place], back_buf.at[:, :, :, place], load_sems.at[i]
+            )
+        )
+        loads[-1].start()
     if before:
-        low = start
-        out_ref[:, :low] = before[0][...]
+        place = pl.ds(0, shift)
+        stores.append(
+            pltpu.make_async_copy(before[0], out_ref.at[:, place], store_sems.at[len(cuts)])
+        )
+        stores[-1].start()
     cells = lax.broadcasted_iota(jnp.int32, (tokens, 2 * half), 1)
     one_hot = jnp.concatenate(
         [(cells == cells_ref[:, i : i + 1]).astype(jnp.bfloat16) for i in range(2)], axis=0
     )
-    for ref, begin in ((early_ref, 0), (late_ref, part)):
-        first, last = max(start, begin), min(start + size, begin + part)
-        if first < last:
-            picked = 0.0
-            for i in range(copies):
-                rows = back_ref[:, i, :, first - start : last - start]
-                picked = picked + dot32(one_hot, rows.reshape(2 * half, last - first))
-            combined = gates_ref[:, 0:1] * picked[:tokens] + gates_ref[:, 1:2] * picked[tokens:]
-            total = ref[:, first - begin : last - begin] + mod_ref[3:4, first:last] * combined
-            out_ref[:, first - start + low : last - start + low] = total.astype(jnp.bfloat16)
+    for i, (low, high) in enumerate(cuts):
+        loads[i].wait()
+        picked = 0.0
+        for j in range(copies):
+            rows = back_buf[:, j, :, low - start : high - start]
+            picked = picked + dot32(one_hot, rows.reshape(2 * half, high - low))
+        combined = gates_ref[:, 0:1] * picked[:tokens] + gates_ref[:, 1:2] * picked[tokens:]
+        ref = late_ref if low >= part else early_ref
+        begin = low // part * part
+        total = ref[:, low - begin : high - begin] + mod_ref[3:4, low:high] * combined
+        place = pl.ds(low - start, high - low)
+        out_buf[:, place] = total.astype(jnp.bfloat16)
+        target = pl.ds(low - start + shift, high - low)
+        stores.append(
+            pltpu.make_async_copy(out_buf.at[:, place], out_ref.at[:, target], store_sems.at[i])
+        )
+        stores[-1].start()
+    for store in stores:
+        store.wait()
 
 
 def combine(residuals, modulation, cells, gates, back, start, before):
-    tokens = residuals[0].shape[0]
-    size = back.shape[3] + sum(value.shape[1] for value in before)
-    return pl.pallas_call(
-        functools.partial(combine_kernel, start),
-        out_shape=jax.ShapeDtypeStruct((tokens, size), jnp.bfloat16),
-        in_specs=[VMEM] * (6 + len(before)),
-        out_specs=VMEM,
+    tokens, part = residuals[0].shape
+    size = back.shape[3]
+    cuts = pieces_of(start, start + size, part, 1024)
+    width = size + sum(value.shape[1] for value in before)
+    return pl.pallas_call(
+        functools.partial(combine_kernel, cuts),
+        out_shape=jax.ShapeDtypeStruct((tokens, width), jnp.bfloat16),
+        in_specs=[VMEM] * 5 + [pl.BlockSpec(memory_space=pl.ANY)] + [VMEM] * len(before),
+        out_specs=pl.BlockSpec(memory_space=pl.ANY),
+        scratch_shapes=[
+            pltpu.VMEM(back.shape, jnp.bfloat16),
+            pltpu.VMEM((tokens, size), jnp.bfloat16),
+            pltpu.SemaphoreType.DMA((len(cuts),)),
+            pltpu.SemaphoreType.DMA((len(cuts) + 1,)),
+        ],
         compiler_params=grant(28),
         cost_estimate=LOW,
     )(*residuals, modulation, cells, gates, back, *before)

time: 262 us -> 263 us (level)
  no operation moved by 1% of the time
where the time goes in v5:
time: 263 us; the launch traced here: 262 us
  waiting for transfers between devices  175 us (67%)
  Pallas kernels  54.5 us (21%)
  starting transfers between devices  27.2 us (10%)
  local copies, waits for them, and re-layouts  5.14 us (2%)
    all_to_all x4, waiting for transfers between devices, exchange(): lax.all_to_all(value, ('x', 'ep'), split_axis=0, concat_axis=0, tiled=True)  116 us
    ppermute x3, waiting for transfers between devices, local(): piece = lax.ppermute(piece, ('x', 'core'), shift(dx, dc))  34.8 us
    ppermute x2, waiting for transfers between devices, local(): lax.ppermute(value, 'x', [(x, (x - dx) % n_x) for x in range(n_x)])  22.3 us
    all_to_all x4, starting transfers between devices, exchange(): lax.all_to_all(value, ('x', 'ep'), split_axis=0, concat_axis=0, tiled=True)  21.1 us
    pallas_call x1, Pallas kernels, ffn_first(): pl.pallas_call(ffn_first_kernel, grid=(units // tile,), out_shape=[jax.Sh...  16.4 us
    pallas_call x1, Pallas kernels, ffn_tail(): pl.pallas_call(functools.partial(ffn_tail_kernel, head), out_shape=[act,...  10.4 us
    pallas_call x1, Pallas kernels, ffn_out(): pl.pallas_call(ffn_out_kernel, grid=(size // tile,), out_shape=jax.ShapeD...  10.3 us
    pallas_call x1, Pallas kernels, project(): pl.pallas_call(project_kernel, grid=(4,), out_shape=out_shape, in_specs=[...  6.65 us
  transfers between devices with their start and end apart: 14, of which 9 were waited for; matrix products, arithmetic and copies ran while one was open for 0% of the time, Pallas kernels for 13%

profile of v5, /device:TPU:0, one launch (start us, length us, event | category | flops | bytes accessed | tf_op | source)
XLA Modules:
  0.0 262.5 jit_solution(6937207329811215567)
XLA Ops:
  0.0 2.3 dynamic-slice_bitcast_fusion
  2.3 0.5 collective-permute-start.4
  2.9 2.6 collective-permute-start.2
  5.6 17.7 %collective-permute-done.2.refs_3_ = bf16[3,128,1024]{2,1,0:T(8,128)(2,1)S(1)} collective-permute-done((bf16[3,128,1024]{2,1,0:T(8,128)(2,1)S(1)}, bf16[3,128,1024]{2,1,0:T(8,128)(2,1)S(1)}, u32[]{:S(2)}, u32[]{:S(2)}) %collective-permute-start.2) | collective-permute-done | bytes 786464 | tf_op jit(solution)/shard_map/ppermute | solution.py:405
  23.4 17.1 %collective-permute-done.1.refs_2_ = bf16[3,128,1024]{2,1,0:T(8,128)(2,1)S(1)} collective-permute-done((bf16[3,128,1024]{2,1,0:T(8,128)(2,1)S(1)}, bf16[3,128,1024]{2,1,0:T(8,128)(2,1)S(1)}, u32[]{:S(2)}, u32[]{:S(2)}) %collective-permute-start.1) | collective-permute-done | bytes 786464 | tf_op jit(solution)/shard_map/ppermute | solution.py:405
  40.4 3.0 %shard_map.100 = (bf16[2,128,1024]{2,1,0:T(8,128)(2,1)S(1)}, bf16[2,128,1024]{2,1,0:T(8,128)(2,1)S(1)}) custom-call(bf16[3,128,1024]{2,1,0:T(8,128)(2,1)S(1)} %get-tuple-element.55.refs_0_, bf16[3,128,1024]{2,1,0:T(8,128)(2,1)S(1)} %collective-permute-done.refs_1_, bf16[3,128,1024]{2,1,0:T(8,128)(2,1)S(1)} %collective-permute-done.1.refs_2_, ...), custom_call_target="tpu_custom_call" | custom-call | flops 1024 | bytes 1024 | tf_op jit(solution)/shard_map/pallas_call | solution.py:53
  43.5 1.9 collective-permute-done.3.theirs_ref
  45.4 6.7 %shard_map.101 = (f32[128,2048]{1,0:T(8,128)S(1)}, bf16[128,2048]{1,0:T(8,128)(2,1)S(1)}, f32[128,2048]{1,0:T(8,128)S(1)}, bf16[128,2048]{1,0:T(8,128)(2,1)S(1)}) custom-call(bf16[2,128,1024]{2,1,0:T(8,128)(2,1)S(1)} %get-tuple-element.29.mine_ref, bf16[2,128,1024]{2,1,0:T(8,128)(2,1)S(1)} %collective-permute-done.3.theirs_ref, ...), custom_call_target="tpu_custom_call" | custom-call | flops 1024 | bytes 1024 | tf_op jit(solution)/shard_map/pallas_call | solution.py:97
  52.1 1.8 collective-permute-start.5
  53.9 0.3 collective-permute-start.6
  54.2 0.5 collective-permute-start.8
  54.7 12.2 %collective-permute-done.5.refs_0_ = bf16[128,2048]{1,0:T(8,128)(2,1)S(1)} collective-permute-done((bf16[128,2048]{1,0:T(8,128)(2,1)S(1)}, bf16[128,2048]{1,0:T(8,128)(2,1)S(1)}, u32[]{:S(2)}, u32[]{:S(2)}) %collective-permute-start.5) | collective-permute-done | bytes 524320 | tf_op jit(solution)/shard_map/ppermute | solution.py:434
  66.9 0.4 shard_map.102
  67.3 10.0 %collective-permute-done.6.refs_0_ = bf16[128,2048]{1,0:T(8,128)(2,1)S(1)} collective-permute-done((bf16[128,2048]{1,0:T(8,128)(2,1)S(1)}, bf16[128,2048]{1,0:T(8,128)(2,1)S(1)}, u32[]{:S(2)}, u32[]{:S(2)}) %collective-permute-start.6) | collective-permute-done | bytes 524320 | tf_op jit(solution)/shard_map/ppermute | solution.py:434
  77.3 0.4 shard_map.103
  78.2 1.6 shard_map.104
  79.8 1.5 copy-done
  81.3 7.1 %all-to-all-start = ((bf16[16,24,3072]{2,1,0:T(8,128)(2,1)}), bf16[16,24,3072]{2,1,0:T(8,128)(2,1)}, u32[]{:S(2)}, u32[]{:S(2)}) async-start(bf16[16,24,3072]{2,1,0:T(8,128)(2,1)} %bitcast.53), calls=%async_computation | async-start | bytes 4718592 | tf_op jit(solution)/shard_map/all_to_all | solution.py:390
  88.5 1.4 shard_map.105
  89.9 51.5 %all-to-all-done = bf16[16,24,3072]{2,1,0:T(8,128)(2,1)} async-done(((bf16[16,24,3072]{2,1,0:T(8,128)(2,1)}), bf16[16,24,3072]{2,1,0:T(8,128)(2,1)}, u32[]{:S(2)}, u32[]{:S(2)}) %all-to-all-start) | async-done | bytes 2359328 | tf_op jit(solution)/shard_map/all_to_all | solution.py:390
  141.4 5.9 %all-to-all-start.1 = ((bf16[16,24,1024]{2,1,0:T(8,128)(2,1)}), bf16[16,24,1024]{2,1,0:T(8,128)(2,1)S(1)}, u32[]{:S(2)}, u32[]{:S(2)}) async-start(bf16[16,24,1024]{2,1,0:T(8,128)(2,1)} %bitcast.16), calls=%async_computation.1 | async-start | bytes 1572864 | tf_op jit(solution)/shard_map/all_to_all | solution.py:390
  147.3 16.4 %shard_map.106 = (f32[384,1024]{1,0:T(8,128)}, f32[384,1024]{1,0:T(8,128)}, f32[384,1024]{1,0:T(8,128)}, f32[384,1024]{1,0:T(8,128)}) custom-call(bf16[384,3072]{1,0:T(8,128)(2,1)} %bitcast.15.rows_ref, bf16[4096,1024]{1,0:T(8,128)(2,1)} %bitcast.18.refs_0_, bf16[4096,1024]{1,0:T(8,128)(2,1)} %collective-permute-done.7.refs_1_, ...), custom_call_target="tpu_custom_call" | custom-call | flops 1024 | bytes 1024 | tf_op jit(solution)/shard_map/pallas_call | solution.py:206
  163.7 4.2 %all-to-all-done.1 = bf16[16,24,1024]{2,1,0:T(8,128)(2,1)S(1)} async-done(((bf16[16,24,1024]{2,1,0:T(8,128)(2,1)}), bf16[16,24,1024]{2,1,0:T(8,128)(2,1)S(1)}, u32[]{:S(2)}, u32[]{:S(2)}) %all-to-all-start.1) | async-done | bytes 786464 | tf_op jit(solution)/shard_map/all_to_all | solution.py:390
  167.9 0.9 copy-done.4
  168.8 10.4 %shard_map.107 = (bf16[384,1024]{1,0:T(8,128)(2,1)}, bf16[384,1024]{1,0:T(8,128)(2,1)}, bf16[384,1024]{1,0:T(8,128)(2,1)}) custom-call(bf16[384,1024]{1,0:T(8,128)(2,1)} %bitcast.61, bf16[4096,1024]{1,0:T(8,128)(2,1)} %bitcast.18.refs_0_, bf16[4096,1024]{1,0:T(8,128)(2,1)} %collective-permute-done.7.refs_1_, bf16[4096,1024]{1,0:T(8,128)(2,1)} %bitcast.19.refs_2_, ...), custom_call_target="tpu_custom_call" | custom-call | flops 1024 | bytes 1024 | tf_op jit(solution)/shard_map/pallas_call | solution.py:258
  179.2 3.6 %all-to-all-start.2 = ((bf16[16,24,1024]{2,1,0:T(8,128)(2,1)}), bf16[16,24,1024]{2,1,0:T(8,128)(2,1)S(1)}, u32[]{:S(2)}, u32[]{:S(2)}) async-start(bf16[16,24,1024]{2,1,0:T(8,128)(2,1)} %bitcast.62), calls=%async_computation.2 | async-start | bytes 1572864 | tf_op jit(solution)/shard_map/all_to_all | solution.py:390
  182.8 10.3 %shard_map.108 = bf16[384,3072]{1,0:T(8,128)(2,1)} custom-call(bf16[384,1024]{1,0:T(8,128)(2,1)} %get-tuple-element.49.mine_ref, bf16[384,1024]{1,0:T(8,128)(2,1)} %get-tuple-element.50.theirs_ref, bf16[1024,4096]{1,0:T(8,128)(2,1)} %bitcast.20.refs_8_.mine_w, bf16[1024,4096]{1,0:T(8,128)(2,1)} %collective-permute-done.9.refs_9_.theirs_w), custom_call_target="tpu_custom_call" | custom-call | flops 1024 | bytes 1024 | tf_op jit(solution)/shard_map/pallas_call | solution.py:285
  193.1 9.9 %all-to-all-done.2 = bf16[16,24,1024]{2,1,0:T(8,128)(2,1)S(1)} async-done(((bf16[16,24,1024]{2,1,0:T(8,128)(2,1)}), bf16[16,24,1024]{2,1,0:T(8,128)(2,1)S(1)}, u32[]{:S(2)}, u32[]{:S(2)}) %all-to-all-start.2) | async-done | bytes 786464 | tf_op jit(solution)/shard_map/all_to_all | solution.py:390
  203.1 4.5 %all-to-all-start.3 = ((bf16[16,24,3072]{2,1,0:T(8,128)(2,1)}), bf16[16,24,3072]{2,1,0:T(8,128)(2,1)}, u32[]{:S(2)}, u32[]{:S(2)}) async-start(bf16[16,24,3072]{2,1,0:T(8,128)(2,1)} %bitcast.60), calls=%async_computation.3 | async-start | bytes 4718592 | tf_op jit(solution)/shard_map/all_to_all | solution.py:390
  207.7 0.7 shard_map.109.refs_0_
  208.3 50.7 %all-to-all-done.3 = bf16[16,24,3072]{2,1,0:T(8,128)(2,1)} async-done(((bf16[16,24,3072]{2,1,0:T(8,128)(2,1)}), bf16[16,24,3072]{2,1,0:T(8,128)(2,1)}, u32[]{:S(2)}, u32[]{:S(2)}) %all-to-all-start.3) | async-done | bytes 2359328 | tf_op jit(solution)/shard_map/all_to_all | solution.py:390
  259.0 3.4 %shard_map.110 = bf16[128,4096]{1,0:T(8,128)(2,1)} custom-call(f32[128,2048]{1,0:T(8,128)S(1)} %get-tuple-element.34.refs_0_.early_ref, f32[128,2048]{1,0:T(8,128)S(1)} %get-tuple-element.38.refs_1_.late_ref, f32[4,4096]{1,0:T(4,128)S(1)} %copy-done.3, s32[128,2]{1,0:T(8,128)S(1)} %fusion.3.cells_ref, f32[128,2]{1,0:T(8,128)S(1)} %bitcast.59, ...), custom_call_target="tpu_custom_call" | custom-call | flops 1024 | bytes 1024 | tf_op jit(solution)/shard_map/pallas_call | solution.py:347
  (29 shorter events, 0.8 us)
Async XLA Ops:
  0.0 45.4 %copy-start.1 = (bf16[1024,4096]{1,0:T(8,128)(2,1)S(1)}, bf16[1024,4096]{1,0:T(8,128)(2,1)}, u32[]{:S(2)}) copy-start(bf16[1024,4096]{1,0:T(8,128)(2,1)} %mine_w.1) | copy-start | bytes 25165828
  2.3 43.0 %collective-permute-start.4 = (bf16[1024,4096]{1,0:T(8,128)(2,1)}, bf16[1024,4096]{1,0:T(8,128)(2,1)S(1)}, u32[]{:S(2)}, u32[]{:S(2)}) collective-permute-start(bf16[1024,4096]{1,0:T(8,128)(2,1)} %mine_w.1), channel_id=1, source_target_pairs={{0,8},{8,0},{1,9},{9,1},{2,10},{10,2},{3,11},{11,3},{4,12},{12,4},... | collective-permute-start | bytes 25165832 | tf_op jit(solution)/shard_map/ppermute | solution.py:385
  2.9 20.5 %collective-permute-start.2 = (bf16[3,128,1024]{2,1,0:T(8,128)(2,1)S(1)}, bf16[3,128,1024]{2,1,0:T(8,128)(2,1)S(1)}, u32[]{:S(2)}, u32[]{:S(2)}) collective-permute-start(bf16[3,128,1024]{2,1,0:T(8,128)(2,1)S(1)} %get-tuple-element.53), channel_id=1, source_target_pairs={{0,24},{8,16},{16,8},{24,0},{1,25},{9,17},{17,9},{25,1},{2,26},{10... | collective-permute-start | bytes 2359304 | tf_op jit(solution)/shard_map/ppermute | solution.py:405
  5.5 34.9 %collective-permute-start.1 = (bf16[3,128,1024]{2,1,0:T(8,128)(2,1)S(1)}, bf16[3,128,1024]{2,1,0:T(8,128)(2,1)S(1)}, u32[]{:S(2)}, u32[]{:S(2)}) collective-permute-start(bf16[3,128,1024]{2,1,0:T(8,128)(2,1)S(1)} %get-tuple-element.56), channel_id=1, source_target_pairs={{0,16},{8,24},{16,0},{24,8},{1,17},{9,25},{17,1},{25,9},{2,18},{10... | collective-permute-start | bytes 2359304 | tf_op jit(solution)/shard_map/ppermute | solution.py:405
  5.5 34.9 %collective-permute-start = (bf16[3,128,1024]{2,1,0:T(8,128)(2,1)S(1)}, bf16[3,128,1024]{2,1,0:T(8,128)(2,1)S(1)}, u32[]{:S(2)}, u32[]{:S(2)}) collective-permute-start(bf16[3,128,1024]{2,1,0:T(8,128)(2,1)S(1)} %get-tuple-element.54), channel_id=1, source_target_pairs={{0,8},{8,0},{16,24},{24,16},{1,9},{9,1},{17,25},{25,17},{2,10},{10... | collective-permute-start | bytes 2359304 | tf_op jit(solution)/shard_map/ppermute | solution.py:405
  43.4 2.0 collective-permute-start.3
  45.4 21.5 %copy-start.2 = (bf16[1,128,4096]{2,1,0:T(8,128)(2,1)S(1)}, bf16[1,128,4096]{2,1,0:T(8,128)(2,1)}, u32[]{:S(2)}) copy-start(bf16[1,128,4096]{2,1,0:T(8,128)(2,1)} %param.10) | copy-start | bytes 3145732
  45.4 21.5 %copy-start.3 = (f32[4,4096]{1,0:T(4,128)S(1)}, f32[4,4096]{1,0:T(4,128)}, u32[]{:S(2)}) copy-start(f32[4,4096]{1,0:T(4,128)} %mod_ref.11) | copy-start | bytes 196612
  52.1 25.8 %copy-start.5 = (s32[1,128,2]{1,2,0:T(2,128)S(1)}, s32[1,128,2]{1,2,0:T(2,128)}, u32[]{:S(2)}) copy-start(s32[1,128,2]{1,2,0:T(2,128)} %param.14) | copy-start | bytes 3076
  52.1 25.9 %copy-start.6 = (s32[1,128,2]{1,2,0:T(2,128)S(1)}, s32[1,128,2]{1,2,0:T(2,128)}, u32[]{:S(2)}) copy-start(s32[1,128,2]{1,2,0:T(2,128)} %param.15) | copy-start | bytes 3076
  52.1 14.8 %collective-permute-start.5 = (bf16[128,2048]{1,0:T(8,128)(2,1)S(1)}, bf16[128,2048]{1,0:T(8,128)(2,1)S(1)}, u32[]{:S(2)}, u32[]{:S(2)}) collective-permute-start(bf16[128,2048]{1,0:T(8,128)(2,1)S(1)} %get-tuple-element.33), channel_id=1, source_target_pairs={{0,16},{16,0},{1,17},{17,1},{2,18},{18,2},{3,19},{19,3},{4,20},{20... | collective-permute-start | bytes 1572872 | tf_op jit(solution)/shard_map/ppermute | solution.py:434
  53.9 23.5 %collective-permute-start.6 = (bf16[128,2048]{1,0:T(8,128)(2,1)S(1)}, bf16[128,2048]{1,0:T(8,128)(2,1)S(1)}, u32[]{:S(2)}, u32[]{:S(2)}) collective-permute-start(bf16[128,2048]{1,0:T(8,128)(2,1)S(1)} %get-tuple-element.36), channel_id=1, source_target_pairs={{0,16},{16,0},{1,17},{17,1},{2,18},{18,2},{3,19},{19,3},{4,20},{20... | collective-permute-start | bytes 1572872 | tf_op jit(solution)/shard_map/ppermute | solution.py:434
  54.2 93.1 %collective-permute-start.7 = (bf16[4096,1024]{1,0:T(8,128)(2,1)}, bf16[4096,1024]{1,0:T(8,128)(2,1)}, u32[]{:S(2)}, u32[]{:S(2)}) collective-permute-start(bf16[4096,1024]{1,0:T(8,128)(2,1)} %bitcast.18.refs_0_), channel_id=1, source_target_pairs={{0,8},{8,0},{1,9},{9,1},{2,10},{10,2},{3,11},{11,3},{4,12},{12,4},... | collective-permute-start | bytes 25165832 | tf_op jit(solution)/shard_map/ppermute | solution.py:385
  54.2 93.2 %collective-permute-start.8 = (bf16[4096,1024]{1,0:T(8,128)(2,1)}, bf16[4096,1024]{1,0:T(8,128)(2,1)}, u32[]{:S(2)}, u32[]{:S(2)}) collective-permute-start(bf16[4096,1024]{1,0:T(8,128)(2,1)} %bitcast.19.refs_2_), channel_id=1, source_target_pairs={{0,8},{8,0},{1,9},{9,1},{2,10},{10,2},{3,11},{11,3},{4,12},{12,4},... | collective-permute-start | bytes 25165832 | tf_op jit(solution)/shard_map/ppermute | solution.py:385
  77.8 90.1 %collective-permute-start.9 = (bf16[1024,4096]{1,0:T(8,128)(2,1)}, bf16[1024,4096]{1,0:T(8,128)(2,1)}, u32[]{:S(2)}, u32[]{:S(2)}) collective-permute-start(bf16[1024,4096]{1,0:T(8,128)(2,1)} %bitcast.20.refs_8_.mine_w), channel_id=1, source_target_pairs={{0,8},{8,0},{1,9},{9,1},{2,10},{10,2},{3,11},{11,3},{4,12},{12,4},... | collective-permute-start | bytes 25165832 | tf_op jit(solution)/shard_map/ppermute | solution.py:385
  79.8 1.5 copy-start
  81.3 60.0 %all-to-all-start = ((bf16[16,24,3072]{2,1,0:T(8,128)(2,1)}), bf16[16,24,3072]{2,1,0:T(8,128)(2,1)}, u32[]{:S(2)}, u32[]{:S(2)}) async-start(bf16[16,24,3072]{2,1,0:T(8,128)(2,1)} %bitcast.53), calls=%async_computation | async-start | bytes 4718592 | tf_op jit(solution)/shard_map/all_to_all | solution.py:390
  141.4 26.5 %all-to-all-start.1 = ((bf16[16,24,1024]{2,1,0:T(8,128)(2,1)}), bf16[16,24,1024]{2,1,0:T(8,128)(2,1)S(1)}, u32[]{:S(2)}, u32[]{:S(2)}) async-start(bf16[16,24,1024]{2,1,0:T(8,128)(2,1)} %bitcast.16), calls=%async_computation.1 | async-start | bytes 1572864 | tf_op jit(solution)/shard_map/all_to_all | solution.py:390
  167.9 0.9 copy-start.4
  179.2 23.9 %all-to-all-start.2 = ((bf16[16,24,1024]{2,1,0:T(8,128)(2,1)}), bf16[16,24,1024]{2,1,0:T(8,128)(2,1)S(1)}, u32[]{:S(2)}, u32[]{:S(2)}) async-start(bf16[16,24,1024]{2,1,0:T(8,128)(2,1)} %bitcast.62), calls=%async_computation.2 | async-start | bytes 1572864 | tf_op jit(solution)/shard_map/all_to_all | solution.py:390
  193.1 14.4 %copy-start.7 = (f32[1,128,2]{1,2,0:T(2,128)S(1)}, f32[1,128,2]{1,2,0:T(2,128)}, u32[]{:S(2)}) copy-start(f32[1,128,2]{1,2,0:T(2,128)} %param.16) | copy-start | bytes 3076
  203.1 55.9 %all-to-all-start.3 = ((bf16[16,24,3072]{2,1,0:T(8,128)(2,1)}), bf16[16,24,3072]{2,1,0:T(8,128)(2,1)}, u32[]{:S(2)}, u32[]{:S(2)}) async-start(bf16[16,24,3072]{2,1,0:T(8,128)(2,1)} %bitcast.60), calls=%async_computation.3 | async-start | bytes 4718592 | tf_op jit(solution)/shard_map/all_to_all | solution.py:390

commit v6 on v5

--- a/solution.py
+++ b/solution.py
@@ -155,40 +155,27 @@
     return cuts
 
 
-def pack_kernel(cuts, mod_ref, cells_ref, stats_ref, *refs):
-    *part_refs, sent_ref, buf, sems = refs
-    start = cuts[0][0]
+def pack_kernel(start, stop, mod_ref, cells_ref, stats_ref, *refs):
+    *part_refs, sent_ref = refs
     tokens, size = part_refs[0].shape
-    cells = lax.broadcasted_iota(jnp.int32, (buf.shape[0], tokens), 0)
+    cells = lax.broadcasted_iota(jnp.int32, (sent_ref.shape[0], tokens), 0)
     one_hot = ((cells == cells_ref[0:1, :]) | (cells == cells_ref[1:2, :])).astype(jnp.bfloat16)
-    copies = []
-    for i, (low, high) in enumerate(cuts):
-        cut = slice(low, high)
-        begin = low // size * size
-        part = part_refs[low // size][:, low - begin : high - begin]
-        normed = (part - stats_ref[:, 0:1]) * stats_ref[:, 1:2]
-        moe_in = (normed * (1.0 + mod_ref[2:3, cut]) + mod_ref[1:2, cut]).astype(jnp.bfloat16)
-        place = pl.ds(low - start, high - low)
-        buf[:, place] = dot32(one_hot, moe_in).astype(jnp.bfloat16)
-        copies.append(
-            pltpu.make_async_copy(buf.at[:, place], sent_ref.at[:, place], sems.at[i])
-        )
-        copies[-1].start()
-    for copy in copies:
-        copy.wait()
+    for i, part_ref in enumerate(part_refs):
+        low, high = max(start, i * size), min(stop, (i + 1) * size)
+        if low < high:
+            cut = slice(low, high)
+            part = part_ref[:, low - i * size : high - i * size]
+            normed = (part - stats_ref[:, 0:1]) * stats_ref[:, 1:2]
+            moe_in = (normed * (1.0 + mod_ref[2:3, cut]) + mod_ref[1:2, cut]).astype(jnp.bfloat16)
+            sent_ref[:, low - start : high - start] = dot32(one_hot, moe_in).astype(jnp.bfloat16)
 
 
 def pack(modulation, cells, n_cells, stats, parts, start, stop):
-    cuts = pieces_of(start, stop, parts[0].shape[1], 1024)
-    return pl.pallas_call(
-        functools.partial(pack_kernel, cuts),
+    return pl.pallas_call(
+        functools.partial(pack_kernel, start, stop),
         out_shape=jax.ShapeDtypeStruct((n_cells, stop - start), jnp.bfloat16),
         in_specs=[VMEM] * (3 + len(parts)),
-        out_specs=pl.BlockSpec(memory_space=pltpu.HBM),
-        scratch_shapes=[
-            pltpu.VMEM((n_cells, stop - start), jnp.bfloat16),
-            pltpu.SemaphoreType.DMA((len(cuts),)),
-        ],
+        out_specs=VMEM,
         compiler_params=grant(28),
         cost_estimate=LOW,
     )(modulation, cells, stats, *parts)
@@ -221,17 +208,16 @@
     weight_buf, sum_buf, down_buf, sems = refs[13:]
     size = rows_ref.shape[1]
     low = weights[0].shape[0] - size
-    order = (0, 2, 1, 3)
     copies = {}
-    for i in order:
+    for i in (0, 2, 1, 3):
         copies["sum", i] = pltpu.make_async_copy(sums[i], sum_buf.at[i], sems.at[i])
         copies["weight", i] = pltpu.make_async_copy(
             weights[i].at[pl.ds(low, size), :], weight_buf.at[i], sems.at[4 + i]
         )
-    for i in range(2):
-        copies["down", i] = pltpu.make_async_copy(
-            downs[i].at[:, pl.ds(0, head)], down_buf.at[i], sems.at[8 + i]
-        )
+        if i >= 2:
+            copies["down", i - 2] = pltpu.make_async_copy(
+                downs[i - 2].at[:, pl.ds(0, head)], down_buf.at[i - 2], sems.at[6 + i]
+            )
     for copy in copies.values():
         copy.start()
     rows = rows_ref[...]
@@ -241,12 +227,12 @@
         copies["weight", i].wait()
         return dot32(rows, weight_buf[i]) + sum_buf[i]
 
+    value = 0.0
     for i in range(2):
         gate = total(i)
         acts[i][...] = (gate / (1.0 + jnp.exp(-gate)) * total(2 + i)).astype(jnp.bfloat16)
-    for i in range(2):
         copies["down", i].wait()
-    value = dot32(acts[0][...], down_buf[0]) + dot32(acts[1][...], down_buf[1])
+        value = value + dot32(acts[i][...], down_buf[i])
     value_ref[...] = value.astype(jnp.bfloat16)
 
 

time: 263 us -> 263 us (level)
  no operation moved by 1% of the time
where the time goes in v6:
time: 263 us; the launch traced here: 262 us
  waiting for transfers between devices  175 us (67%)
  Pallas kernels  54.4 us (21%)
  starting transfers between devices  27.2 us (10%)
  local copies, waits for them, and re-layouts  5.14 us (2%)
    all_to_all x4, waiting for transfers between devices, exchange(): lax.all_to_all(value, ('x', 'ep'), split_axis=0, concat_axis=0, tiled=True)  116 us
    ppermute x3, waiting for transfers between devices, local(): piece = lax.ppermute(piece, ('x', 'core'), shift(dx, dc))  34.8 us
    ppermute x2, waiting for transfers between devices, local(): lax.ppermute(value, 'x', [(x, (x - dx) % n_x) for x in range(n_x)])  22.3 us
    all_to_all x4, starting transfers between devices, exchange(): lax.all_to_all(value, ('x', 'ep'), split_axis=0, concat_axis=0, tiled=True)  21.1 us
    pallas_call x1, Pallas kernels, ffn_first(): pl.pallas_call(ffn_first_kernel, grid=(units // tile,), out_shape=[jax.Sh...  16.4 us
    pallas_call x1, Pallas kernels, ffn_tail(): pl.pallas_call(functools.partial(ffn_tail_kernel, head), out_shape=[act,...  10.9 us
    pallas_call x1, Pallas kernels, ffn_out(): pl.pallas_call(ffn_out_kernel, grid=(size // tile,), out_shape=jax.ShapeD...  10.3 us
    pallas_call x1, Pallas kernels, project(): pl.pallas_call(project_kernel, grid=(4,), out_shape=out_shape, in_specs=[...  6.65 us
  transfers between devices with their start and end apart: 14, of which 9 were waited for; matrix products, arithmetic and copies ran while one was open for 0% of the time, Pallas kernels for 13%

profile of v6, /device:TPU:0, one launch (start us, length us, event | category | flops | bytes accessed | tf_op | source)
XLA Modules:
  0.0 262.3 jit_solution(12583165868444668717)
XLA Ops:
  0.0 2.3 dynamic-slice_bitcast_fusion
  2.3 0.5 collective-permute-start.4
  2.9 2.6 collective-permute-start.2
  5.6 17.7 %collective-permute-done.2.refs_3_ = bf16[3,128,1024]{2,1,0:T(8,128)(2,1)S(1)} collective-permute-done((bf16[3,128,1024]{2,1,0:T(8,128)(2,1)S(1)}, bf16[3,128,1024]{2,1,0:T(8,128)(2,1)S(1)}, u32[]{:S(2)}, u32[]{:S(2)}) %collective-permute-start.2) | collective-permute-done | bytes 786464 | tf_op jit(solution)/shard_map/ppermute | solution.py:391
  23.4 17.1 %collective-permute-done.1.refs_2_ = bf16[3,128,1024]{2,1,0:T(8,128)(2,1)S(1)} collective-permute-done((bf16[3,128,1024]{2,1,0:T(8,128)(2,1)S(1)}, bf16[3,128,1024]{2,1,0:T(8,128)(2,1)S(1)}, u32[]{:S(2)}, u32[]{:S(2)}) %collective-permute-start.1) | collective-permute-done | bytes 786464 | tf_op jit(solution)/shard_map/ppermute | solution.py:391
  40.4 3.0 %shard_map.100 = (bf16[2,128,1024]{2,1,0:T(8,128)(2,1)S(1)}, bf16[2,128,1024]{2,1,0:T(8,128)(2,1)S(1)}) custom-call(bf16[3,128,1024]{2,1,0:T(8,128)(2,1)S(1)} %get-tuple-element.55.refs_0_, bf16[3,128,1024]{2,1,0:T(8,128)(2,1)S(1)} %collective-permute-done.refs_1_, bf16[3,128,1024]{2,1,0:T(8,128)(2,1)S(1)} %collective-permute-done.1.refs_2_, ...), custom_call_target="tpu_custom_call" | custom-call | flops 1024 | bytes 1024 | tf_op jit(solution)/shard_map/pallas_call | solution.py:53
  43.5 1.9 collective-permute-done.3.theirs_ref
  45.4 6.7 %shard_map.101 = (f32[128,2048]{1,0:T(8,128)S(1)}, bf16[128,2048]{1,0:T(8,128)(2,1)S(1)}, f32[128,2048]{1,0:T(8,128)S(1)}, bf16[128,2048]{1,0:T(8,128)(2,1)S(1)}) custom-call(bf16[2,128,1024]{2,1,0:T(8,128)(2,1)S(1)} %get-tuple-element.29.mine_ref, bf16[2,128,1024]{2,1,0:T(8,128)(2,1)S(1)} %collective-permute-done.3.theirs_ref, ...), custom_call_target="tpu_custom_call" | custom-call | flops 1024 | bytes 1024 | tf_op jit(solution)/shard_map/pallas_call | solution.py:97
  52.1 1.8 collective-permute-start.5
  53.9 0.3 collective-permute-start.6
  54.2 0.5 collective-permute-start.8
  54.7 12.2 %collective-permute-done.5.refs_0_ = bf16[128,2048]{1,0:T(8,128)(2,1)S(1)} collective-permute-done((bf16[128,2048]{1,0:T(8,128)(2,1)S(1)}, bf16[128,2048]{1,0:T(8,128)(2,1)S(1)}, u32[]{:S(2)}, u32[]{:S(2)}) %collective-permute-start.5) | collective-permute-done | bytes 524320 | tf_op jit(solution)/shard_map/ppermute | solution.py:420
  66.9 0.4 shard_map.102
  67.3 10.0 %collective-permute-done.6.refs_0_ = bf16[128,2048]{1,0:T(8,128)(2,1)S(1)} collective-permute-done((bf16[128,2048]{1,0:T(8,128)(2,1)S(1)}, bf16[128,2048]{1,0:T(8,128)(2,1)S(1)}, u32[]{:S(2)}, u32[]{:S(2)}) %collective-permute-start.6) | collective-permute-done | bytes 524320 | tf_op jit(solution)/shard_map/ppermute | solution.py:420
  77.3 0.4 shard_map.103
  78.2 0.9 shard_map.104
  79.1 1.5 copy-done
  80.6 7.1 %all-to-all-start = ((bf16[16,24,3072]{2,1,0:T(8,128)(2,1)}), bf16[16,24,3072]{2,1,0:T(8,128)(2,1)}, u32[]{:S(2)}, u32[]{:S(2)}) async-start(bf16[16,24,3072]{2,1,0:T(8,128)(2,1)} %bitcast.53), calls=%async_computation | async-start | bytes 4718592 | tf_op jit(solution)/shard_map/all_to_all | solution.py:376
  87.8 1.4 shard_map.105
  89.2 51.5 %all-to-all-done = bf16[16,24,3072]{2,1,0:T(8,128)(2,1)} async-done(((bf16[16,24,3072]{2,1,0:T(8,128)(2,1)}), bf16[16,24,3072]{2,1,0:T(8,128)(2,1)}, u32[]{:S(2)}, u32[]{:S(2)}) %all-to-all-start) | async-done | bytes 2359328 | tf_op jit(solution)/shard_map/all_to_all | solution.py:376
  140.7 5.9 %all-to-all-start.1 = ((bf16[16,24,1024]{2,1,0:T(8,128)(2,1)}), bf16[16,24,1024]{2,1,0:T(8,128)(2,1)S(1)}, u32[]{:S(2)}, u32[]{:S(2)}) async-start(bf16[16,24,1024]{2,1,0:T(8,128)(2,1)} %bitcast.16), calls=%async_computation.1 | async-start | bytes 1572864 | tf_op jit(solution)/shard_map/all_to_all | solution.py:376
  146.6 16.4 %shard_map.106 = (f32[384,1024]{1,0:T(8,128)}, f32[384,1024]{1,0:T(8,128)}, f32[384,1024]{1,0:T(8,128)}, f32[384,1024]{1,0:T(8,128)}) custom-call(bf16[384,3072]{1,0:T(8,128)(2,1)} %bitcast.15.rows_ref, bf16[4096,1024]{1,0:T(8,128)(2,1)} %bitcast.18.refs_0_, bf16[4096,1024]{1,0:T(8,128)(2,1)} %collective-permute-done.7.refs_1_, ...), custom_call_target="tpu_custom_call" | custom-call | flops 1024 | bytes 1024 | tf_op jit(solution)/shard_map/pallas_call | solution.py:193
  163.0 4.2 %all-to-all-done.1 = bf16[16,24,1024]{2,1,0:T(8,128)(2,1)S(1)} async-done(((bf16[16,24,1024]{2,1,0:T(8,128)(2,1)}), bf16[16,24,1024]{2,1,0:T(8,128)(2,1)S(1)}, u32[]{:S(2)}, u32[]{:S(2)}) %all-to-all-start.1) | async-done | bytes 786464 | tf_op jit(solution)/shard_map/all_to_all | solution.py:376
  167.2 0.9 copy-done.4
  168.1 10.9 %shard_map.107 = (bf16[384,1024]{1,0:T(8,128)(2,1)}, bf16[384,1024]{1,0:T(8,128)(2,1)}, bf16[384,1024]{1,0:T(8,128)(2,1)}) custom-call(bf16[384,1024]{1,0:T(8,128)(2,1)} %bitcast.61, bf16[4096,1024]{1,0:T(8,128)(2,1)} %bitcast.18.refs_0_, bf16[4096,1024]{1,0:T(8,128)(2,1)} %collective-permute-done.7.refs_1_, bf16[4096,1024]{1,0:T(8,128)(2,1)} %bitcast.19.refs_2_, ...), custom_call_target="tpu_custom_call" | custom-call | flops 1024 | bytes 1024 | tf_op jit(solution)/shard_map/pallas_call | solution.py:244
  179.0 3.6 %all-to-all-start.2 = ((bf16[16,24,1024]{2,1,0:T(8,128)(2,1)}), bf16[16,24,1024]{2,1,0:T(8,128)(2,1)S(1)}, u32[]{:S(2)}, u32[]{:S(2)}) async-start(bf16[16,24,1024]{2,1,0:T(8,128)(2,1)} %bitcast.62), calls=%async_computation.2 | async-start | bytes 1572864 | tf_op jit(solution)/shard_map/all_to_all | solution.py:376
  182.6 10.3 %shard_map.108 = bf16[384,3072]{1,0:T(8,128)(2,1)} custom-call(bf16[384,1024]{1,0:T(8,128)(2,1)} %get-tuple-element.49.mine_ref, bf16[384,1024]{1,0:T(8,128)(2,1)} %get-tuple-element.50.theirs_ref, bf16[1024,4096]{1,0:T(8,128)(2,1)} %bitcast.20.refs_8_.mine_w, bf16[1024,4096]{1,0:T(8,128)(2,1)} %collective-permute-done.9.refs_9_.theirs_w), custom_call_target="tpu_custom_call" | custom-call | flops 1024 | bytes 1024 | tf_op jit(solution)/shard_map/pallas_call | solution.py:271
  193.0 9.9 %all-to-all-done.2 = bf16[16,24,1024]{2,1,0:T(8,128)(2,1)S(1)} async-done(((bf16[16,24,1024]{2,1,0:T(8,128)(2,1)}), bf16[16,24,1024]{2,1,0:T(8,128)(2,1)S(1)}, u32[]{:S(2)}, u32[]{:S(2)}) %all-to-all-start.2) | async-done | bytes 786464 | tf_op jit(solution)/shard_map/all_to_all | solution.py:376
  202.9 4.5 %all-to-all-start.3 = ((bf16[16,24,3072]{2,1,0:T(8,128)(2,1)}), bf16[16,24,3072]{2,1,0:T(8,128)(2,1)}, u32[]{:S(2)}, u32[]{:S(2)}) async-start(bf16[16,24,3072]{2,1,0:T(8,128)(2,1)} %bitcast.60), calls=%async_computation.3 | async-start | bytes 4718592 | tf_op jit(solution)/shard_map/all_to_all | solution.py:376
  207.5 0.7 shard_map.109.refs_0_
  208.1 50.7 %all-to-all-done.3 = bf16[16,24,3072]{2,1,0:T(8,128)(2,1)} async-done(((bf16[16,24,3072]{2,1,0:T(8,128)(2,1)}), bf16[16,24,3072]{2,1,0:T(8,128)(2,1)}, u32[]{:S(2)}, u32[]{:S(2)}) %all-to-all-start.3) | async-done | bytes 2359328 | tf_op jit(solution)/shard_map/all_to_all | solution.py:376
  258.8 3.4 %shard_map.110 = bf16[128,4096]{1,0:T(8,128)(2,1)} custom-call(f32[128,2048]{1,0:T(8,128)S(1)} %get-tuple-element.34.refs_0_.early_ref, f32[128,2048]{1,0:T(8,128)S(1)} %get-tuple-element.38.refs_1_.late_ref, f32[4,4096]{1,0:T(4,128)S(1)} %copy-done.3, s32[128,2]{1,0:T(8,128)S(1)} %fusion.3.cells_ref, f32[128,2]{1,0:T(8,128)S(1)} %bitcast.59, ...), custom_call_target="tpu_custom_call" | custom-call | flops 1024 | bytes 1024 | tf_op jit(solution)/shard_map/pallas_call | solution.py:333
  (29 shorter events, 0.8 us)
Async XLA Ops:
  0.0 45.4 %copy-start.1 = (bf16[1024,4096]{1,0:T(8,128)(2,1)S(1)}, bf16[1024,4096]{1,0:T(8,128)(2,1)}, u32[]{:S(2)}) copy-start(bf16[1024,4096]{1,0:T(8,128)(2,1)} %mine_w.1) | copy-start | bytes 25165828
  2.3 43.0 %collective-permute-start.4 = (bf16[1024,4096]{1,0:T(8,128)(2,1)}, bf16[1024,4096]{1,0:T(8,128)(2,1)S(1)}, u32[]{:S(2)}, u32[]{:S(2)}) collective-permute-start(bf16[1024,4096]{1,0:T(8,128)(2,1)} %mine_w.1), channel_id=1, source_target_pairs={{0,8},{8,0},{1,9},{9,1},{2,10},{10,2},{3,11},{11,3},{4,12},{12,4},... | collective-permute-start | bytes 25165832 | tf_op jit(solution)/shard_map/ppermute | solution.py:371
  2.9 20.5 %collective-permute-start.2 = (bf16[3,128,1024]{2,1,0:T(8,128)(2,1)S(1)}, bf16[3,128,1024]{2,1,0:T(8,128)(2,1)S(1)}, u32[]{:S(2)}, u32[]{:S(2)}) collective-permute-start(bf16[3,128,1024]{2,1,0:T(8,128)(2,1)S(1)} %get-tuple-element.53), channel_id=1, source_target_pairs={{0,24},{8,16},{16,8},{24,0},{1,25},{9,17},{17,9},{25,1},{2,26},{10... | collective-permute-start | bytes 2359304 | tf_op jit(solution)/shard_map/ppermute | solution.py:391
  5.5 34.9 %collective-permute-start.1 = (bf16[3,128,1024]{2,1,0:T(8,128)(2,1)S(1)}, bf16[3,128,1024]{2,1,0:T(8,128)(2,1)S(1)}, u32[]{:S(2)}, u32[]{:S(2)}) collective-permute-start(bf16[3,128,1024]{2,1,0:T(8,128)(2,1)S(1)} %get-tuple-element.56), channel_id=1, source_target_pairs={{0,16},{8,24},{16,0},{24,8},{1,17},{9,25},{17,1},{25,9},{2,18},{10... | collective-permute-start | bytes 2359304 | tf_op jit(solution)/shard_map/ppermute | solution.py:391
  5.5 34.9 %collective-permute-start = (bf16[3,128,1024]{2,1,0:T(8,128)(2,1)S(1)}, bf16[3,128,1024]{2,1,0:T(8,128)(2,1)S(1)}, u32[]{:S(2)}, u32[]{:S(2)}) collective-permute-start(bf16[3,128,1024]{2,1,0:T(8,128)(2,1)S(1)} %get-tuple-element.54), channel_id=1, source_target_pairs={{0,8},{8,0},{16,24},{24,16},{1,9},{9,1},{17,25},{25,17},{2,10},{10... | collective-permute-start | bytes 2359304 | tf_op jit(solution)/shard_map/ppermute | solution.py:391
  43.4 2.0 collective-permute-start.3
  45.4 21.5 %copy-start.2 = (bf16[1,128,4096]{2,1,0:T(8,128)(2,1)S(1)}, bf16[1,128,4096]{2,1,0:T(8,128)(2,1)}, u32[]{:S(2)}) copy-start(bf16[1,128,4096]{2,1,0:T(8,128)(2,1)} %param.10) | copy-start | bytes 3145732
  45.4 21.5 %copy-start.3 = (f32[4,4096]{1,0:T(4,128)S(1)}, f32[4,4096]{1,0:T(4,128)}, u32[]{:S(2)}) copy-start(f32[4,4096]{1,0:T(4,128)} %mod_ref.11) | copy-start | bytes 196612
  52.1 25.8 %copy-start.5 = (s32[1,128,2]{1,2,0:T(2,128)S(1)}, s32[1,128,2]{1,2,0:T(2,128)}, u32[]{:S(2)}) copy-start(s32[1,128,2]{1,2,0:T(2,128)} %param.14) | copy-start | bytes 3076
  52.1 25.9 %copy-start.6 = (s32[1,128,2]{1,2,0:T(2,128)S(1)}, s32[1,128,2]{1,2,0:T(2,128)}, u32[]{:S(2)}) copy-start(s32[1,128,2]{1,2,0:T(2,128)} %param.15) | copy-start | bytes 3076
  52.1 14.8 %collective-permute-start.5 = (bf16[128,2048]{1,0:T(8,128)(2,1)S(1)}, bf16[128,2048]{1,0:T(8,128)(2,1)S(1)}, u32[]{:S(2)}, u32[]{:S(2)}) collective-permute-start(bf16[128,2048]{1,0:T(8,128)(2,1)S(1)} %get-tuple-element.33), channel_id=1, source_target_pairs={{0,16},{16,0},{1,17},{17,1},{2,18},{18,2},{3,19},{19,3},{4,20},{20... | collective-permute-start | bytes 1572872 | tf_op jit(solution)/shard_map/ppermute | solution.py:420
  53.9 23.5 %collective-permute-start.6 = (bf16[128,2048]{1,0:T(8,128)(2,1)S(1)}, bf16[128,2048]{1,0:T(8,128)(2,1)S(1)}, u32[]{:S(2)}, u32[]{:S(2)}) collective-permute-start(bf16[128,2048]{1,0:T(8,128)(2,1)S(1)} %get-tuple-element.36), channel_id=1, source_target_pairs={{0,16},{16,0},{1,17},{17,1},{2,18},{18,2},{3,19},{19,3},{4,20},{20... | collective-permute-start | bytes 1572872 | tf_op jit(solution)/shard_map/ppermute | solution.py:420
  54.2 92.4 %collective-permute-start.7 = (bf16[4096,1024]{1,0:T(8,128)(2,1)}, bf16[4096,1024]{1,0:T(8,128)(2,1)}, u32[]{:S(2)}, u32[]{:S(2)}) collective-permute-start(bf16[4096,1024]{1,0:T(8,128)(2,1)} %bitcast.18.refs_0_), channel_id=1, source_target_pairs={{0,8},{8,0},{1,9},{9,1},{2,10},{10,2},{3,11},{11,3},{4,12},{12,4},... | collective-permute-start | bytes 25165832 | tf_op jit(solution)/shard_map/ppermute | solution.py:371
  54.2 92.5 %collective-permute-start.8 = (bf16[4096,1024]{1,0:T(8,128)(2,1)}, bf16[4096,1024]{1,0:T(8,128)(2,1)}, u32[]{:S(2)}, u32[]{:S(2)}) collective-permute-start(bf16[4096,1024]{1,0:T(8,128)(2,1)} %bitcast.19.refs_2_), channel_id=1, source_target_pairs={{0,8},{8,0},{1,9},{9,1},{2,10},{10,2},{3,11},{11,3},{4,12},{12,4},... | collective-permute-start | bytes 25165832 | tf_op jit(solution)/shard_map/ppermute | solution.py:371
  77.8 89.4 %collective-permute-start.9 = (bf16[1024,4096]{1,0:T(8,128)(2,1)}, bf16[1024,4096]{1,0:T(8,128)(2,1)}, u32[]{:S(2)}, u32[]{:S(2)}) collective-permute-start(bf16[1024,4096]{1,0:T(8,128)(2,1)} %bitcast.20.refs_8_.mine_w), channel_id=1, source_target_pairs={{0,8},{8,0},{1,9},{9,1},{2,10},{10,2},{3,11},{11,3},{4,12},{12,4},... | collective-permute-start | bytes 25165832 | tf_op jit(solution)/shard_map/ppermute | solution.py:371
  79.1 1.5 copy-start
  80.6 60.0 %all-to-all-start = ((bf16[16,24,3072]{2,1,0:T(8,128)(2,1)}), bf16[16,24,3072]{2,1,0:T(8,128)(2,1)}, u32[]{:S(2)}, u32[]{:S(2)}) async-start(bf16[16,24,3072]{2,1,0:T(8,128)(2,1)} %bitcast.53), calls=%async_computation | async-start | bytes 4718592 | tf_op jit(solution)/shard_map/all_to_all | solution.py:376
  140.7 26.5 %all-to-all-start.1 = ((bf16[16,24,1024]{2,1,0:T(8,128)(2,1)}), bf16[16,24,1024]{2,1,0:T(8,128)(2,1)S(1)}, u32[]{:S(2)}, u32[]{:S(2)}) async-start(bf16[16,24,1024]{2,1,0:T(8,128)(2,1)} %bitcast.16), calls=%async_computation.1 | async-start | bytes 1572864 | tf_op jit(solution)/shard_map/all_to_all | solution.py:376
  167.2 0.9 copy-start.4
  179.0 23.9 %all-to-all-start.2 = ((bf16[16,24,1024]{2,1,0:T(8,128)(2,1)}), bf16[16,24,1024]{2,1,0:T(8,128)(2,1)S(1)}, u32[]{:S(2)}, u32[]{:S(2)}) async-start(bf16[16,24,1024]{2,1,0:T(8,128)(2,1)} %bitcast.62), calls=%async_computation.2 | async-start | bytes 1572864 | tf_op jit(solution)/shard_map/all_to_all | solution.py:376
  193.0 14.4 %copy-start.7 = (f32[1,128,2]{1,2,0:T(2,128)S(1)}, f32[1,128,2]{1,2,0:T(2,128)}, u32[]{:S(2)}) copy-start(f32[1,128,2]{1,2,0:T(2,128)} %param.16) | copy-start | bytes 3076
  202.9 55.9 %all-to-all-start.3 = ((bf16[16,24,3072]{2,1,0:T(8,128)(2,1)}), bf16[16,24,3072]{2,1,0:T(8,128)(2,1)}, u32[]{:S(2)}, u32[]{:S(2)}) async-start(bf16[16,24,3072]{2,1,0:T(8,128)(2,1)} %bitcast.60), calls=%async_computation.3 | async-start | bytes 4718592 | tf_op jit(solution)/shard_map/all_to_all | solution.py:376
